TPU v7x, 32 devices: a whole 2x2x4 slice. The times are simulated.
32 devices in a mesh: strip: 4 (over y, x), cuts: 8 (over z, core).
Axes of the slice: x: 2, y: 2, z: 4, core: 2. Of those that a mesh axis runs over, the one named last changes fastest.
Arguments:
- start_state: float32 [8, 6, 512, 512], P('cuts', None, 'strip'), may hold values from -6 to 6
- initial_state: float32 [6, 512, 512], P(None, 'strip'), may hold values from -6 to 6
- circ_stiff: float32 [512, 512], P('strip'), may hold values from 0.5 to 2
- axial_stiff: float32 [512, 512], P('strip'), may hold values from 0.5 to 2
- lumped_mass: float32 [512, 512], P('strip'), may hold values from 1 to 2
- hoop_stiff: float32 [512, 512], P('strip'), may hold values from 0.5 to 2
Outputs:
- new_start: float32 [8, 6, 512, 512], P('cuts', None, 'strip')
- fine_end: float32 [8, 6, 512, 512], P('cuts', None, 'strip')
All inputs are finite; a program needn't handle non-finite values.
Results may differ from a plain program's by a relative error of at most 0.00002.
Values sent between devices are 32-bit elements; how exact they have to be, the bound alone decides.
No kernel may reach another device: no remote copies, remote signals or barrier semaphores. Data moves between devices by JAX's collectives and lax.ppermute only.
A program may use at most 192 MiB of HBM per device.

v0:
```python
import jax
import jax.numpy as jnp
from jax import lax
from jax.sharding import PartitionSpec as P

step_length = 0.35
coupling_fine = 0.25


def shifted(value, axis, steps):
    count = lax.axis_size(axis)
    pairs = [(source, (source + steps) % count) for source in range(count)]
    return lax.ppermute(value, axis, pairs)


def padded_2(cells, sides, width):
    for axis, dim in sides:
        count = lax.axis_size(axis)
        head = lax.slice_in_dim(cells, 0, width, axis=dim)
        tail = lax.slice_in_dim(cells, cells.shape[dim] - width, cells.shape[dim], axis=dim)
        cells = jnp.concatenate(
            [
                lax.ppermute(tail, axis, [(i, (i + 1) % count) for i in range(count)]),
                cells,
                lax.ppermute(head, axis, [((i + 1) % count, i) for i in range(count)]),
            ],
            axis=dim,
        )
    return cells


def from_behind(value, axis, by):
    peers = lax.axis_size(axis)
    pairs = [(i, i + by) for i in range(peers) if 0 <= i + by < peers]
    return lax.ppermute(value, axis, pairs)


def combine_forces(
    displace, above_rows, below_rows, circ_stiff, circ_low, axial_stiff, hoop_stiff, coupling
):
    zero_col = jnp.zeros_like(displace[:, :, :1])
    forward = jnp.concatenate([displace[:, :, 1:], zero_col], axis=2)
    backward = jnp.concatenate([zero_col, displace[:, :, :-1]], axis=2)
    axial_low = jnp.concatenate([jnp.zeros_like(axial_stiff[:, :1]), axial_stiff[:, :-1]], axis=1)
    summed = circ_stiff * (above_rows - displace) + circ_low * (below_rows - displace)
    summed = summed + axial_stiff * (forward - displace) + axial_low * (backward - displace)
    gradient = 0.5 * (above_rows - below_rows)
    first_comp = summed[0] - coupling * gradient[2]
    third_comp = summed[2] + coupling * gradient[0] - hoop_stiff * displace[2]
    return jnp.stack([first_comp, summed[1], third_comp])


def verlet(current, force_fn, masses, increment, repeats):
    displace = current[:3]
    velocity = current[3:]
    acceleration = force_fn(displace) / masses
    for number in range(repeats):
        half_step = velocity + 0.5 * increment * acceleration
        displace = displace + increment * half_step
        acceleration = force_fn(displace) / masses
        velocity = half_step + 0.5 * increment * acceleration
    return jnp.concatenate([displace, velocity], axis=0)


def restrict(field):
    leading = field.shape[:-2]
    rows = field.shape[-2]
    cols = field.shape[-1]
    return field.reshape(leading + (rows // 2, 2, cols // 2, 2)).mean(axis=(-3, -1))


def prolong(field):
    return jnp.repeat(jnp.repeat(field, 2, axis=-2), 2, axis=-1)


def per_device(start_state, initial_state, circ_stiff, axial_stiff, lumped_mass, hoop_stiff):
    current = start_state[0]
    lower_rows = shifted(circ_stiff[-2:], "strip", 1)
    circ_low = jnp.concatenate([lower_rows[1:], circ_stiff[:-1]], axis=0)

    def fine_force(displace):
        padded = padded_2(displace, (("strip", 1),), 1)
        return combine_forces(
            displace,
            padded[:, 2:],
            padded[:, :-2],
            circ_stiff,
            circ_low,
            axial_stiff,
            hoop_stiff,
            coupling_fine,
        )

    fine_end = verlet(current, fine_force, lumped_mass, step_length, 2)
    received = from_behind(fine_end, "cuts", 1)
    position = lax.axis_index("cuts")
    mismatch = jnp.where(position == 0, initial_state - current, received - current)
    coarse_circ = restrict(circ_stiff)
    coarse_low = jnp.concatenate([restrict(lower_rows), coarse_circ[:-1]], axis=0)
    coarse_axial = restrict(axial_stiff)
    coarse_mass = 4.0 * restrict(lumped_mass)
    coarse_hoop = 4.0 * restrict(hoop_stiff)

    def coarse_force(displace):
        padded = padded_2(displace, (("strip", 1),), 1)
        return combine_forces(
            displace,
            padded[:, 2:],
            padded[:, :-2],
            coarse_circ,
            coarse_low,
            coarse_axial,
            coarse_hoop,
            2.0 * coupling_fine,
        )

    residue = restrict(mismatch)
    slices = lax.axis_size("cuts")
    carried = residue
    distance = 1
    while distance < slices:
        moved = from_behind(carried, "cuts", distance)
        for repeat_count in range(distance):
            moved = verlet(moved, coarse_force, coarse_mass, 2.0 * step_length, 1)
        carried = carried + jnp.where(position >= distance, moved, jnp.zeros_like(moved))
        distance = distance * 2
    new_start = current + mismatch + prolong(carried - residue)
    return (new_start[None], fine_end[None])


def solution(mesh):
    placed = (
        P("cuts", None, "strip", None),
        P(None, "strip", None),
        P("strip", None),
        P("strip", None),
        P("strip", None),
        P("strip", None),
    )
    return jax.shard_map(
        per_device,
        mesh=mesh,
        in_specs=placed,
        out_specs=(P("cuts", None, "strip", None), P("cuts", None, "strip", None)),
        check_vma=False,
    )
```

profile of v0, /device:TPU:24, one launch (start us, length us, event | category | flops | bytes accessed | tf_op | source)
XLA Modules:
  0.0 339.1 jit_solution(12252925526646124473)
XLA Ops:
  0.6 1.9 copy.150
  3.7 1.4 copy.155
  5.1 2.5 collective-permute-start
  7.9 2.0 collective-permute-start.1
  13.3 1.8 copy.164
  16.1 1.7 pad_maximum_fusion.7
  17.8 1.8 copy.157
  21.9 2.6 multiply_add_fusion.4
  25.7 1.4 fusion.167
  27.1 1.4 copy.165
  29.5 1.4 copy.167
  36.6 2.6 multiply_add_fusion.2
  41.6 1.4 fusion.165
  43.0 1.4 copy.170
  45.5 1.4 copy.172
  52.7 2.6 multiply_add_fusion
  56.6 1.9 fusion.163
  58.5 2.1 collective-permute-start.7
  60.7 18.1 %reshape.77 = f32[64,2,256,2]{3,2,1,0:T(8,128)} reshape(f32[128,512]{1,0:T(8,128)S(1)} %copy-done.7) | data formatting | bytes 524288 | tf_op jit(solution)/shard_map/reshape | solution.py:69
  78.8 18.1 %reshape.78 = f32[64,2,256,2]{3,2,1,0:T(8,128)} reshape(f32[128,512]{1,0:T(8,128)S(1)} %copy-done.9) | data formatting | bytes 524288 | tf_op jit(solution)/shard_map/reshape | solution.py:69
  96.9 18.1 %reshape.79 = f32[64,2,256,2]{3,2,1,0:T(8,128)} reshape(f32[128,512]{1,0:T(8,128)S(1)} %copy-done.17) | data formatting | bytes 524288 | tf_op jit(solution)/shard_map/reshape | solution.py:69
  115.0 18.1 %reshape.80 = f32[64,2,256,2]{3,2,1,0:T(8,128)} reshape(f32[128,512]{1,0:T(8,128)S(1)} %copy-done.18) | data formatting | bytes 524288 | tf_op jit(solution)/shard_map/reshape | solution.py:69
  133.0 1.6 copy.151
  134.6 8.0 %reduce_sum.64 = f32[64,256]{1,0:T(8,128)S(1)} reduce(f32[64,2,256,2]{3,2,1,0:T(8,128)} %reshape.77, f32[]{:T(128)} %constant.13.clone.1), dimensions={1,3}, to_apply=%region_1.2 | reduce | flops 49152 | bytes 327684 | tf_op jit(solution)/shard_map/reduce_sum | solution.py:69
  142.6 8.6 %reduce_sum.68 = f32[64,256]{1,0:T(8,128)} reduce(f32[64,2,256,2]{3,2,1,0:T(8,128)} %reshape.78, f32[]{:T(128)} %constant.13.clone.1), dimensions={1,3}, to_apply=%region_4.5 | reduce | flops 49152 | bytes 327684 | tf_op jit(solution)/shard_map/reduce_sum | solution.py:69
  151.3 8.0 %reduce_sum.69 = f32[64,256]{1,0:T(8,128)S(1)} reduce(f32[64,2,256,2]{3,2,1,0:T(8,128)} %reshape.79, f32[]{:T(128)} %constant.13.clone.1), dimensions={1,3}, to_apply=%region_5.6 | reduce | flops 49152 | bytes 327684 | tf_op jit(solution)/shard_map/reduce_sum | solution.py:69
  159.3 8.0 %reduce_sum.71 = f32[64,256]{1,0:T(8,128)S(1)} reduce(f32[64,2,256,2]{3,2,1,0:T(8,128)} %reshape.80, f32[]{:T(128)} %constant.13.clone.1), dimensions={1,3}, to_apply=%region_6.7 | reduce | flops 49152 | bytes 327684 | tf_op jit(solution)/shard_map/reduce_sum | solution.py:69
  167.6 2.1 fusion
  169.7 15.8 %copy.175 = f32[6,128,512]{0,2,1:T(8,128)} copy(f32[6,128,512]{1,2,0:T(8,128)S(1)} %fusion) | data formatting | bytes 3145728 | tf_op jit(solution)/shard_map/jit(_where)/select_n | solution.py:97
  185.6 32.3 %reduce_sum.63 = f32[6,64,256]{0,2,1:T(8,128)} reduce(f32[6,64,2,256,2]{0,4,3,2,1:T(2,128)} %bitcast.93, f32[]{:T(128)} %constant.13.clone.1), dimensions={2,4}, to_apply=%region_0.1 | reduce | flops 294912 | bytes 1966084 | tf_op jit(solution)/shard_map/reduce_sum | solution.py:69
  217.9 6.0 %copy.176 = f32[6,64,256]{2,1,0:T(8,128)} copy(f32[6,64,256]{0,2,1:T(8,128)} %reduce_sum.63) | data formatting | bytes 786432 | tf_op jit(solution)/shard_map/reduce_sum | solution.py:69
  224.9 1.9 collective-permute-start.8
  226.9 7.0 %collective-permute-done.8 = f32[6,64,256]{2,1,0:T(8,128)S(1)} collective-permute-done((f32[6,64,256]{2,1,0:T(8,128)S(1)}, f32[6,64,256]{2,1,0:T(8,128)S(1)}, u32[]{:S(2)}, u32[]{:S(2)}) %collective-permute-start.8) | collective-permute-done | bytes 393248 | tf_op jit(solution)/shard_map/ppermute | solution.py:35
  234.1 2.8 collective-permute-start.9
  237.0 1.4 collective-permute-done.10
  238.7 3.0 collective-permute-start.11
  243.0 3.2 collective-permute-done.12
  248.5 8.7 %collective-permute-done.13 = f32[6,64,256]{2,1,0:T(8,128)} collective-permute-done((f32[6,64,256]{2,1,0:T(8,128)}, f32[6,64,256]{2,1,0:T(8,128)}, u32[]{:S(2)}, u32[]{:S(2)}) %collective-permute-start.13) | collective-permute-done | bytes 393248 | tf_op jit(solution)/shard_map/ppermute | solution.py:35
  258.0 2.0 collective-permute-start.15
  264.6 1.4 collective-permute-start.16
  266.8 1.5 collective-permute-done.16
  268.3 2.2 collective-permute-done.17
  271.9 2.0 collective-permute-start.19
  274.0 1.5 collective-permute-done.18
  276.7 1.8 fusion.9
  279.8 3.0 copy.179
  282.8 10.7 %collective-permute-done.20 = f32[6,64,256]{2,1,0:T(8,128)} collective-permute-done((f32[6,64,256]{2,1,0:T(8,128)}, f32[6,64,256]{2,1,0:T(8,128)}, u32[]{:S(2)}, u32[]{:S(2)}) %collective-permute-start.20) | collective-permute-done | bytes 393248 | tf_op jit(solution)/shard_map/ppermute | solution.py:35
  294.2 1.7 collective-permute-start.21
  298.3 2.1 collective-permute-done.22
  303.1 1.5 collective-permute-start.24
  304.7 1.5 collective-permute-done.23
  306.2 1.4 collective-permute-done.24
  311.1 1.5 collective-permute-done.25
  312.6 1.7 collective-permute-done.26
  315.1 1.5 collective-permute-start.28
  316.7 1.5 collective-permute-done.27
  318.2 1.5 collective-permute-done.28
  322.1 1.5 collective-permute-done.29
  323.6 2.1 collective-permute-done.30
  328.2 2.6 reshape.81
  330.7 2.3 copy.177
  333.0 1.7 broadcast_in_dim.9
  334.7 1.4 fusion.2
  336.1 3.0 copy.178
  (165 shorter events, 57.5 us)
Async XLA Ops:
  3.7 4.2 %copy-start.6 = (f32[128,512]{1,0:T(8,128)S(1)}, f32[128,512]{1,0:T(8,128)}, u32[]{:S(2)}) copy-start(f32[128,512]{1,0:T(8,128)} %param.8) | copy-start | bytes 786436
  5.1 14.4 %collective-permute-start = (f32[3,1,512]{2,1,0:T(1,128)S(1)}, f32[3,1,512]{2,1,0:T(1,128)S(1)}, u32[]{:S(2)}, u32[]{:S(2)}) collective-permute-start(f32[3,1,512]{2,1,0:T(1,128)S(1)} %copy.155), channel_id=1, source_target_pairs={{8,0},{16,8},{24,16},{0,24},{9,1},{17,9},{25,17},{1,25},{10,2},{18... | collective-permute-start | bytes 18440 | tf_op jit(solution)/shard_map/ppermute | solution.py:25
  7.8 12.9 %collective-permute-start.2 = (f32[3,1,512]{2,1,0:T(1,128)S(1)}, f32[3,1,512]{2,1,0:T(1,128)S(1)}, u32[]{:S(2)}, u32[]{:S(2)}) collective-permute-start(f32[3,1,512]{2,1,0:T(1,128)S(1)} %copy.158), channel_id=1, source_target_pairs={{0,8},{8,16},{16,24},{24,0},{1,9},{9,17},{17,25},{25,1},{2,10},{10... | collective-permute-start | bytes 18440 | tf_op jit(solution)/shard_map/ppermute | solution.py:23
  7.9 3.4 copy-start.8
  7.9 8.2 %collective-permute-start.1 = (f32[2,512]{1,0:T(2,128)S(1)}, f32[2,512]{1,0:T(2,128)S(1)}, u32[]{:S(2)}, u32[]{:S(2)}) collective-permute-start(f32[2,512]{1,0:T(2,128)S(1)} %slice.628), channel_id=1, source_target_pairs={{0,8},{8,16},{16,24},{24,0},{1,9},{9,17},{17,25},{25,1},{2,10},{10... | collective-permute-start | bytes 12296 | tf_op jit(solution)/shard_map/ppermute | solution.py:13
  24.5 1.0 copy-start.2
  24.6 1.1 copy-start.10
  24.6 1.1 copy-start.12
  24.7 1.1 copy-start.14
  28.5 4.7 %collective-permute-start.3 = (f32[3,1,512]{2,1,0:T(1,128)S(1)}, f32[3,1,512]{2,1,0:T(1,128)S(1)}, u32[]{:S(2)}, u32[]{:S(2)}) collective-permute-start(f32[3,1,512]{2,1,0:T(1,128)S(1)} %copy.165), channel_id=1, source_target_pairs={{8,0},{16,8},{24,16},{0,24},{9,1},{17,9},{25,17},{1,25},{10,2},{18... | collective-permute-start | bytes 18440 | tf_op jit(solution)/shard_map/ppermute | solution.py:25
  30.9 4.6 %collective-permute-start.4 = (f32[3,1,512]{2,1,0:T(1,128)S(1)}, f32[3,1,512]{2,1,0:T(1,128)S(1)}, u32[]{:S(2)}, u32[]{:S(2)}) collective-permute-start(f32[3,1,512]{2,1,0:T(1,128)S(1)} %copy.167), channel_id=1, source_target_pairs={{0,8},{8,16},{16,24},{24,0},{1,9},{9,17},{17,25},{25,1},{2,10},{10... | collective-permute-start | bytes 18440 | tf_op jit(solution)/shard_map/ppermute | solution.py:23
  39.2 1.0 copy-start.3
  39.2 1.0 copy-start.11
  39.3 1.1 copy-start.13
  39.3 1.2 copy-start.15
  44.4 4.7 %collective-permute-start.5 = (f32[3,1,512]{2,1,0:T(1,128)S(1)}, f32[3,1,512]{2,1,0:T(1,128)S(1)}, u32[]{:S(2)}, u32[]{:S(2)}) collective-permute-start(f32[3,1,512]{2,1,0:T(1,128)S(1)} %copy.170), channel_id=1, source_target_pairs={{8,0},{16,8},{24,16},{0,24},{9,1},{17,9},{25,17},{1,25},{10,2},{18... | collective-permute-start | bytes 18440 | tf_op jit(solution)/shard_map/ppermute | solution.py:25
  46.9 4.6 %collective-permute-start.6 = (f32[3,1,512]{2,1,0:T(1,128)S(1)}, f32[3,1,512]{2,1,0:T(1,128)S(1)}, u32[]{:S(2)}, u32[]{:S(2)}) collective-permute-start(f32[3,1,512]{2,1,0:T(1,128)S(1)} %copy.172), channel_id=1, source_target_pairs={{0,8},{8,16},{16,24},{24,0},{1,9},{9,17},{17,25},{25,1},{2,10},{10... | collective-permute-start | bytes 18440 | tf_op jit(solution)/shard_map/ppermute | solution.py:23
  55.2 1.0 copy-start.4
  55.2 1.2 copy-start.5
  56.6 4.1 %copy-start.7 = (f32[128,512]{1,0:T(8,128)S(1)}, f32[128,512]{1,0:T(8,128)}, u32[]{:S(2)}) copy-start(f32[128,512]{1,0:T(8,128)} %param.8) | copy-start | bytes 786436
  58.5 109.1 %collective-permute-start.7 = (f32[6,128,512]{1,2,0:T(8,128)}, f32[6,128,512]{1,2,0:T(8,128)}, u32[]{:S(2)}, u32[]{:S(2)}) collective-permute-start(f32[6,128,512]{1,2,0:T(8,128)} %get-tuple-element.29), channel_id=1, source_target_pairs={{0,1},{1,2},{2,3},{3,4},{4,5},{5,6},{6,7},{8,9},{9,10},{10,11},{11... | collective-permute-start | bytes 4718600 | tf_op jit(solution)/shard_map/ppermute | solution.py:35
  60.6 18.1 %copy-start.9 = (f32[128,512]{1,0:T(8,128)S(1)}, f32[128,512]{1,0:T(8,128)}, u32[]{:S(2)}) copy-start(f32[128,512]{1,0:T(8,128)} %param.9) | copy-start | bytes 786436
  78.8 18.1 %copy-start.17 = (f32[128,512]{1,0:T(8,128)S(1)}, f32[128,512]{1,0:T(8,128)}, u32[]{:S(2)}) copy-start(f32[128,512]{1,0:T(8,128)} %param.11) | copy-start | bytes 786436
  96.9 18.1 %copy-start.18 = (f32[128,512]{1,0:T(8,128)S(1)}, f32[128,512]{1,0:T(8,128)}, u32[]{:S(2)}) copy-start(f32[128,512]{1,0:T(8,128)} %param.10) | copy-start | bytes 786436
  114.9 18.1 %copy-start.16 = (f32[6,128,512]{2,1,0:T(8,128)S(1)}, f32[6,128,512]{2,1,0:T(8,128)}, u32[]{:S(2)}) copy-start(f32[6,128,512]{2,1,0:T(8,128)} %param.7) | copy-start | bytes 4718596
  217.9 9.0 %copy-start.19 = (f32[64,256]{1,0:T(8,128)S(1)}, f32[64,256]{1,0:T(8,128)}, u32[]{:S(2)}) copy-start(f32[64,256]{1,0:T(8,128)} %reduce_sum.68) | copy-start | bytes 196612
  224.9 9.1 %collective-permute-start.8 = (f32[6,64,256]{2,1,0:T(8,128)S(1)}, f32[6,64,256]{2,1,0:T(8,128)S(1)}, u32[]{:S(2)}, u32[]{:S(2)}) collective-permute-start(f32[6,64,256]{2,1,0:T(8,128)S(1)} %broadcast_multiply_fusion), channel_id=1, source_target_pairs={{0,1},{1,2},{2,3},{3,4},{4,5},{5,6},{6,7},{8,9},{9,10},{10,11},{11... | collective-permute-start | bytes 1179656 | tf_op jit(solution)/shard_map/ppermute | solution.py:35
  234.0 4.5 %collective-permute-start.10 = (f32[3,1,256]{2,1,0:T(1,128)S(1)}, f32[3,1,256]{2,1,0:T(1,128)S(1)}, u32[]{:S(2)}, u32[]{:S(2)}) collective-permute-start(f32[3,1,256]{2,1,0:T(1,128)S(1)} %get-tuple-element.79), channel_id=1, source_target_pairs={{0,8},{8,16},{16,24},{24,0},{1,9},{9,17},{17,25},{25,1},{2,10},{10... | collective-permute-start | bytes 9224 | tf_op jit(solution)/shard_map/ppermute | solution.py:23
  234.1 4.3 %collective-permute-start.9 = (f32[3,1,256]{2,1,0:T(1,128)S(1)}, f32[3,1,256]{2,1,0:T(1,128)S(1)}, u32[]{:S(2)}, u32[]{:S(2)}) collective-permute-start(f32[3,1,256]{2,1,0:T(1,128)S(1)} %get-tuple-element.78), channel_id=1, source_target_pairs={{8,0},{16,8},{24,16},{0,24},{9,1},{17,9},{25,17},{1,25},{10,2},{18... | collective-permute-start | bytes 9224 | tf_op jit(solution)/shard_map/ppermute | solution.py:25
  238.7 4.3 %collective-permute-start.11 = (f32[3,1,256]{2,1,0:T(1,128)S(1)}, f32[3,1,256]{2,1,0:T(1,128)S(1)}, u32[]{:S(2)}, u32[]{:S(2)}) collective-permute-start(f32[3,1,256]{2,1,0:T(1,128)S(1)} %get-tuple-element.135), channel_id=1, source_target_pairs={{8,0},{16,8},{24,16},{0,24},{9,1},{17,9},{25,17},{1,25},{10,2},{18... | collective-permute-start | bytes 9224 | tf_op jit(solution)/shard_map/ppermute | solution.py:25
  241.7 4.5 %collective-permute-start.12 = (f32[3,1,256]{2,1,0:T(1,128)S(1)}, f32[3,1,256]{2,1,0:T(1,128)S(1)}, u32[]{:S(2)}, u32[]{:S(2)}) collective-permute-start(f32[3,1,256]{2,1,0:T(1,128)S(1)} %get-tuple-element.136), channel_id=1, source_target_pairs={{0,8},{8,16},{16,24},{24,0},{1,9},{9,17},{17,25},{25,1},{2,10},{10... | collective-permute-start | bytes 9224 | tf_op jit(solution)/shard_map/ppermute | solution.py:23
  241.8 4.6 %copy-start = (f32[6,64,256]{2,1,0:T(8,128)S(1)}, f32[6,64,256]{2,1,0:T(8,128)}, u32[]{:S(2)}) copy-start(f32[6,64,256]{2,1,0:T(8,128)} %copy.176) | copy-start | bytes 1179652
  247.3 10.0 %collective-permute-start.13 = (f32[6,64,256]{2,1,0:T(8,128)}, f32[6,64,256]{2,1,0:T(8,128)}, u32[]{:S(2)}, u32[]{:S(2)}) collective-permute-start(f32[6,64,256]{2,1,0:T(8,128)} %fusion.8), channel_id=1, source_target_pairs={{0,2},{1,3},{2,4},{3,5},{4,6},{5,7},{8,10},{9,11},{10,12},{11,13},... | collective-permute-start | bytes 1179656 | tf_op jit(solution)/shard_map/ppermute | solution.py:35
  258.0 4.1 %collective-permute-start.14 = (f32[3,1,256]{2,1,0:T(1,128)S(1)}, f32[3,1,256]{2,1,0:T(1,128)S(1)}, u32[]{:S(2)}, u32[]{:S(2)}) collective-permute-start(f32[3,1,256]{2,1,0:T(1,128)S(1)} %get-tuple-element.70), channel_id=1, source_target_pairs={{8,0},{16,8},{24,16},{0,24},{9,1},{17,9},{25,17},{1,25},{10,2},{18... | collective-permute-start | bytes 9224 | tf_op jit(solution)/shard_map/ppermute | solution.py:25
  258.0 4.5 %collective-permute-start.15 = (f32[3,1,256]{2,1,0:T(1,128)S(1)}, f32[3,1,256]{2,1,0:T(1,128)S(1)}, u32[]{:S(2)}, u32[]{:S(2)}) collective-permute-start(f32[3,1,256]{2,1,0:T(1,128)S(1)} %get-tuple-element.71), channel_id=1, source_target_pairs={{0,8},{8,16},{16,24},{24,0},{1,9},{9,17},{17,25},{25,1},{2,10},{10... | collective-permute-start | bytes 9224 | tf_op jit(solution)/shard_map/ppermute | solution.py:23
  264.6 3.6 %collective-permute-start.16 = (f32[3,1,256]{2,1,0:T(1,128)S(1)}, f32[3,1,256]{2,1,0:T(1,128)S(1)}, u32[]{:S(2)}, u32[]{:S(2)}) collective-permute-start(f32[3,1,256]{2,1,0:T(1,128)S(1)} %get-tuple-element.129), channel_id=1, source_target_pairs={{8,0},{16,8},{24,16},{0,24},{9,1},{17,9},{25,17},{1,25},{10,2},{18... | collective-permute-start | bytes 9224 | tf_op jit(solution)/shard_map/ppermute | solution.py:25
  266.0 4.5 %collective-permute-start.17 = (f32[3,1,256]{2,1,0:T(1,128)S(1)}, f32[3,1,256]{2,1,0:T(1,128)S(1)}, u32[]{:S(2)}, u32[]{:S(2)}) collective-permute-start(f32[3,1,256]{2,1,0:T(1,128)S(1)} %get-tuple-element.130), channel_id=1, source_target_pairs={{0,8},{8,16},{16,24},{24,0},{1,9},{9,17},{17,25},{25,1},{2,10},{10... | collective-permute-start | bytes 9224 | tf_op jit(solution)/shard_map/ppermute | solution.py:23
  271.8 3.6 %collective-permute-start.18 = (f32[3,1,256]{2,1,0:T(1,128)S(1)}, f32[3,1,256]{2,1,0:T(1,128)S(1)}, u32[]{:S(2)}, u32[]{:S(2)}) collective-permute-start(f32[3,1,256]{2,1,0:T(1,128)S(1)} %get-tuple-element.124), channel_id=1, source_target_pairs={{8,0},{16,8},{24,16},{0,24},{9,1},{17,9},{25,17},{1,25},{10,2},{18... | collective-permute-start | bytes 9224 | tf_op jit(solution)/shard_map/ppermute | solution.py:25
  271.9 4.5 %collective-permute-start.19 = (f32[3,1,256]{2,1,0:T(1,128)S(1)}, f32[3,1,256]{2,1,0:T(1,128)S(1)}, u32[]{:S(2)}, u32[]{:S(2)}) collective-permute-start(f32[3,1,256]{2,1,0:T(1,128)S(1)} %get-tuple-element.125), channel_id=1, source_target_pairs={{0,8},{8,16},{16,24},{24,0},{1,9},{9,17},{17,25},{25,1},{2,10},{10... | collective-permute-start | bytes 9224 | tf_op jit(solution)/shard_map/ppermute | solution.py:23
  278.5 15.0 %collective-permute-start.20 = (f32[6,64,256]{2,1,0:T(8,128)}, f32[6,64,256]{2,1,0:T(8,128)}, u32[]{:S(2)}, u32[]{:S(2)}) collective-permute-start(f32[6,64,256]{2,1,0:T(8,128)} %fusion.9), channel_id=1, source_target_pairs={{0,4},{1,5},{2,6},{3,7},{8,12},{9,13},{10,14},{11,15},{16,20},{17,... | collective-permute-start | bytes 1179656 | tf_op jit(solution)/shard_map/ppermute | solution.py:35
  294.2 4.1 %collective-permute-start.21 = (f32[3,1,256]{2,1,0:T(1,128)S(1)}, f32[3,1,256]{2,1,0:T(1,128)S(1)}, u32[]{:S(2)}, u32[]{:S(2)}) collective-permute-start(f32[3,1,256]{2,1,0:T(1,128)S(1)} %get-tuple-element.60), channel_id=1, source_target_pairs={{8,0},{16,8},{24,16},{0,24},{9,1},{17,9},{25,17},{1,25},{10,2},{18... | collective-permute-start | bytes 9224 | tf_op jit(solution)/shard_map/ppermute | solution.py:25
  295.9 4.5 %collective-permute-start.22 = (f32[3,1,256]{2,1,0:T(1,128)S(1)}, f32[3,1,256]{2,1,0:T(1,128)S(1)}, u32[]{:S(2)}, u32[]{:S(2)}) collective-permute-start(f32[3,1,256]{2,1,0:T(1,128)S(1)} %get-tuple-element.61), channel_id=1, source_target_pairs={{0,8},{8,16},{16,24},{24,0},{1,9},{9,17},{17,25},{25,1},{2,10},{10... | collective-permute-start | bytes 9224 | tf_op jit(solution)/shard_map/ppermute | solution.py:23
  302.5 3.6 %collective-permute-start.23 = (f32[3,1,256]{2,1,0:T(1,128)S(1)}, f32[3,1,256]{2,1,0:T(1,128)S(1)}, u32[]{:S(2)}, u32[]{:S(2)}) collective-permute-start(f32[3,1,256]{2,1,0:T(1,128)S(1)} %get-tuple-element.118), channel_id=1, source_target_pairs={{8,0},{16,8},{24,16},{0,24},{9,1},{17,9},{25,17},{1,25},{10,2},{18... | collective-permute-start | bytes 9224 | tf_op jit(solution)/shard_map/ppermute | solution.py:25
  303.1 4.5 %collective-permute-start.24 = (f32[3,1,256]{2,1,0:T(1,128)S(1)}, f32[3,1,256]{2,1,0:T(1,128)S(1)}, u32[]{:S(2)}, u32[]{:S(2)}) collective-permute-start(f32[3,1,256]{2,1,0:T(1,128)S(1)} %get-tuple-element.119), channel_id=1, source_target_pairs={{0,8},{8,16},{16,24},{24,0},{1,9},{9,17},{17,25},{25,1},{2,10},{10... | collective-permute-start | bytes 9224 | tf_op jit(solution)/shard_map/ppermute | solution.py:23
  308.9 3.6 %collective-permute-start.25 = (f32[3,1,256]{2,1,0:T(1,128)S(1)}, f32[3,1,256]{2,1,0:T(1,128)S(1)}, u32[]{:S(2)}, u32[]{:S(2)}) collective-permute-start(f32[3,1,256]{2,1,0:T(1,128)S(1)} %get-tuple-element.113), channel_id=1, source_target_pairs={{8,0},{16,8},{24,16},{0,24},{9,1},{17,9},{25,17},{1,25},{10,2},{18... | collective-permute-start | bytes 9224 | tf_op jit(solution)/shard_map/ppermute | solution.py:25
  309.8 4.5 %collective-permute-start.26 = (f32[3,1,256]{2,1,0:T(1,128)S(1)}, f32[3,1,256]{2,1,0:T(1,128)S(1)}, u32[]{:S(2)}, u32[]{:S(2)}) collective-permute-start(f32[3,1,256]{2,1,0:T(1,128)S(1)} %get-tuple-element.114), channel_id=1, source_target_pairs={{0,8},{8,16},{16,24},{24,0},{1,9},{9,17},{17,25},{25,1},{2,10},{10... | collective-permute-start | bytes 9224 | tf_op jit(solution)/shard_map/ppermute | solution.py:23
  314.5 3.6 %collective-permute-start.27 = (f32[3,1,256]{2,1,0:T(1,128)S(1)}, f32[3,1,256]{2,1,0:T(1,128)S(1)}, u32[]{:S(2)}, u32[]{:S(2)}) collective-permute-start(f32[3,1,256]{2,1,0:T(1,128)S(1)} %get-tuple-element.108), channel_id=1, source_target_pairs={{8,0},{16,8},{24,16},{0,24},{9,1},{17,9},{25,17},{1,25},{10,2},{18... | collective-permute-start | bytes 9224 | tf_op jit(solution)/shard_map/ppermute | solution.py:25
  315.1 4.5 %collective-permute-start.28 = (f32[3,1,256]{2,1,0:T(1,128)S(1)}, f32[3,1,256]{2,1,0:T(1,128)S(1)}, u32[]{:S(2)}, u32[]{:S(2)}) collective-permute-start(f32[3,1,256]{2,1,0:T(1,128)S(1)} %get-tuple-element.109), channel_id=1, source_target_pairs={{0,8},{8,16},{16,24},{24,0},{1,9},{9,17},{17,25},{25,1},{2,10},{10... | collective-permute-start | bytes 9224 | tf_op jit(solution)/shard_map/ppermute | solution.py:23
  319.9 3.6 %collective-permute-start.29 = (f32[3,1,256]{2,1,0:T(1,128)S(1)}, f32[3,1,256]{2,1,0:T(1,128)S(1)}, u32[]{:S(2)}, u32[]{:S(2)}) collective-permute-start(f32[3,1,256]{2,1,0:T(1,128)S(1)} %get-tuple-element.103), channel_id=1, source_target_pairs={{8,0},{16,8},{24,16},{0,24},{9,1},{17,9},{25,17},{1,25},{10,2},{18... | collective-permute-start | bytes 9224 | tf_op jit(solution)/shard_map/ppermute | solution.py:25
  321.2 4.7 %copy-start.1 = (f32[6,64,256]{2,1,0:T(8,128)S(1)}, f32[6,64,256]{2,1,0:T(8,128)}, u32[]{:S(2)}) copy-start(f32[6,64,256]{2,1,0:T(8,128)} %copy.176) | copy-start | bytes 1179652
  321.2 4.5 %collective-permute-start.30 = (f32[3,1,256]{2,1,0:T(1,128)S(1)}, f32[3,1,256]{2,1,0:T(1,128)S(1)}, u32[]{:S(2)}, u32[]{:S(2)}) collective-permute-start(f32[3,1,256]{2,1,0:T(1,128)S(1)} %get-tuple-element.104), channel_id=1, source_target_pairs={{0,8},{8,16},{16,24},{24,0},{1,9},{9,17},{17,25},{25,1},{2,10},{10... | collective-permute-start | bytes 9224 | tf_op jit(solution)/shard_map/ppermute | solution.py:23
where the time goes:
time: 341 us; the launch traced here: 339 us
  local copies, waits for them, and re-layouts  150 us (44%)
  other arithmetic  94.5 us (28%)
  waiting for transfers between devices  55.6 us (16%)
  starting transfers between devices  37.6 us (11%)
    reshape x4, local copies, waits for them, and re-layouts, restrict(): field.reshape(leading + (rows // 2, 2, cols // 2, 2)).mean(axis=(-3, -1))  72.4 us
    reduce_sum x7, other arithmetic, restrict(): field.reshape(leading + (rows // 2, 2, cols // 2, 2)).mean(axis=(-3, -1))  65.1 us
    ppermute x4, waiting for transfers between devices, from_behind(): return lax.ppermute(value, axis, pairs)  26.4 us
    ppermute x13, waiting for transfers between devices, padded_2(): lax.ppermute(tail, axis, [(i, (i + 1) % count) for i in range(count)])  19.3 us
    ppermute x13, starting transfers between devices, padded_2(): lax.ppermute(head, axis, [((i + 1) % count, i) for i in range(count)])  16.9 us
    unnamed x49, local copies, waits for them, and re-layouts  16.5 us
    select_n x1, local copies, waits for them, and re-layouts, per_device(): jnp.where(position == 0, initial_state - current, received - current)  15.8 us
    ppermute x13, starting transfers between devices, padded_2(): lax.ppermute(tail, axis, [(i, (i + 1) % count) for i in range(count)])  12.2 us
  transfers between devices with their start and end apart: 31, of which 22 were waited for; matrix products, arithmetic and copies ran while one was open for 39% of the time, Pallas kernels for 0%

commit v1 on v0

v1 whole, which is shorter than its diff:
```python
import jax
import jax.numpy as jnp
from jax import lax
from jax.experimental import pallas as pl
from jax.experimental.pallas import tpu as pltpu
from jax.sharding import PartitionSpec as P

FINE_STEP = 0.35
COARSE_STEP = 0.7
FINE_COUPLING = 0.25
COARSE_COUPLING = 0.5
SPEED = COARSE_STEP

FINE_ROWS = (3, 3, 3, 2, 2, 2, 3, 2, 2, 2)
COARSE_ROWS = (2, 2, 2, 1, 1, 1, 3, 2, 2, 2)
FINE_TOTAL = sum(FINE_ROWS)
PACK_ROWS = -(-(FINE_TOTAL + -(-sum(COARSE_ROWS) // 2)) // 8) * 8
CHUNK = 8
EDGE = 4

VMEM = pl.BlockSpec(memory_space=pltpu.VMEM)
ANY = pl.BlockSpec(memory_space=pl.ANY)
F32 = jnp.float32


def run(body, name, outs, args, scratch=(), specs=None, out_specs=None, aliases=None):
    return pl.pallas_call(
        body,
        name=name,
        out_shape=[jax.ShapeDtypeStruct(shape, F32) for shape in outs],
        in_specs=specs or [VMEM] * len(args),
        out_specs=out_specs or [VMEM] * len(outs),
        scratch_shapes=list(scratch),
        input_output_aliases=aliases or {},
        compiler_params=pltpu.CompilerParams(vmem_limit_bytes=20 << 20),
    )(*args)


def turn(value, steps, axis):
    return pltpu.roll(value, steps % value.shape[axis], axis)


def scaled_coefficients(kc, kc_low, ka, mass, hoop, step, coupling):
    lane = lax.broadcasted_iota(jnp.int32, ka.shape, 1)
    last = ka.shape[1] - 1
    ka_next = jnp.where(lane == last, 0.0, ka)
    ka_low = jnp.where(lane == 0, 0.0, turn(ka, 1, 1))
    unit = (step * step) / mass
    return (
        kc * unit,
        kc_low * unit,
        ka_next * unit,
        ka_low * unit,
        (kc + kc_low + ka + ka_low) * unit,
        hoop * unit,
        (0.5 * coupling) * unit,
    )


def accelerate(now, above, below, cf):
    up, down, fore, aft, centre, hoop, cross = cf
    out = []
    for i in range(3):
        w = now[i]
        out.append(
            up * above[i]
            + down * below[i]
            + fore * turn(w, -1, 1)
            + aft * turn(w, 1, 1)
            - centre * w
        )
    out[0] = out[0] - cross * (above[2] - below[2])
    out[2] = out[2] + cross * (above[0] - below[0]) - hoop * now[2]
    return out


def accelerate_block(now, cf):
    above = [turn(w, -1, 0) for w in now]
    below = [turn(w, 1, 0) for w in now]
    return accelerate(now, above, below, cf)


def steps_block(w, q, cf, repeats):
    acc = accelerate_block(w, cf)
    for _ in range(repeats):
        half = [a + 0.5 * b for a, b in zip(q, acc)]
        w = [a + b for a, b in zip(w, half)]
        acc = accelerate_block(w, cf)
        q = [a + 0.5 * b for a, b in zip(half, acc)]
    return w, q


def three_parts(value):
    high = value.astype(jnp.bfloat16)
    rest = value - high.astype(F32)
    middle = rest.astype(jnp.bfloat16)
    low = (rest - middle.astype(F32)).astype(jnp.bfloat16)
    return high, middle, low


def exact_dot(value, matrix):
    return sum(
        jnp.dot(part, matrix, preferred_element_type=F32) for part in three_parts(value)[::-1]
    )


def averaging(cols):
    row = lax.broadcasted_iota(jnp.int32, (cols, cols // 2), 0)
    col = lax.broadcasted_iota(jnp.int32, (cols, cols // 2), 1)
    return jnp.where(row // 2 == col, 0.25, 0.0).astype(jnp.bfloat16)


def spreading(cols):
    row = lax.broadcasted_iota(jnp.int32, (cols // 2, cols), 0)
    col = lax.broadcasted_iota(jnp.int32, (cols // 2, cols), 1)
    return jnp.where(col // 2 == row, 1.0, 0.0).astype(jnp.bfloat16)


LANES = 128


class Halver:
    def __init__(self, ref):
        self.ref = ref
        self.used = 0

    def __call__(self, source, lead, start, count):
        pieces = []
        for at in range(0, source.shape[-1], LANES):
            slot = self.ref.at[self.used]
            self.used += 1
            slot[0 : 2 * count, :] = source[
                lead + (pl.ds(start, 2 * count), pl.ds(at, LANES))
            ]
            pieces.append(
                slot[pl.ds(0, count, stride=2), :] + slot[pl.ds(1, count, stride=2), :]
            )
        return jnp.concatenate(pieces, axis=1)


def halver_scratch(fields, rows, cols):
    return pltpu.VMEM((fields * (cols // LANES), rows, LANES), F32)


def is_first():
    return (lax.axis_index("cuts") == 0).astype(F32)


def pack_body(u, init, kc, ka, mass, hoop, to_above, to_below, slots):
    pair_sum = Halver(slots)
    rows, cols = kc.shape
    first = is_first()
    fields = [(u, (i,)) for i in range(6)] + [(kc, ()), (ka, ()), (mass, ()), (hoop, ())]
    at = 0
    for (ref, lead), count in zip(fields, FINE_ROWS):
        to_above[at : at + count, :] = ref[lead + (slice(rows - count, rows), slice(None))]
        to_below[at : at + count, :] = ref[lead + (slice(0, count), slice(None))]
        at += count
    matrix = averaging(cols)
    sums = []
    for start in (rows - 8, 0):
        for number, (ref, lead) in enumerate(fields):
            value = pair_sum(ref, lead, start, 4)
            if number < 6:
                value = value - first * pair_sum(init, lead, start, 4)
            sums.append(value)
    means = exact_dot(jnp.concatenate(sums, axis=0), matrix)
    half = cols // 2
    at = 0
    for number, count in enumerate(COARSE_ROWS):
        for k in range(count):
            place = (slice(FINE_TOTAL + at // 2, FINE_TOTAL + at // 2 + 1), pl.ds((at % 2) * half, half))
            low = 4 * number + 4 - count + k
            high = 40 + 4 * number + k
            to_above[place] = means[low : low + 1]
            to_below[place] = means[high : high + 1]
            at += 1


def interior_body(u, init, kc, ka, mass, hoop, f, b, cc, raw, cf, w1, half, slots):
    pair_sum = Halver(slots)
    rows, cols = kc.shape
    starts = range(0, rows, CHUNK)

    def around(ref, lead, start):
        now = ref[lead + (pl.ds(start, CHUNK), slice(None))]
        if start + CHUNK < rows:
            above = ref[lead + (pl.ds(start + 1, CHUNK), slice(None))]
        else:
            above = turn(now, -1, 0)
        if start > 0:
            below = ref[lead + (pl.ds(start - 1, CHUNK), slice(None))]
        else:
            below = turn(now, 1, 0)
        return now, above, below

    for start in starts:
        at = pl.ds(start, CHUNK)
        stiff, _, stiff_low = around(kc, (), start)
        found = scaled_coefficients(
            stiff, stiff_low, ka[at, :], mass[at, :], hoop[at, :], FINE_STEP, FINE_COUPLING
        )
        for number in range(7):
            cf[number, at, :] = found[number]
        now, above, below = zip(*[around(u, (i,), start) for i in range(3)])
        acc = accelerate(now, above, below, found)
        for i in range(3):
            moved = FINE_STEP * u[3 + i, at, :] + 0.5 * acc[i]
            half[i, at, :] = moved
            w1[i, at, :] = now[i] + moved
    for start in starts:
        at = pl.ds(start, CHUNK)
        now, above, below = zip(*[around(w1, (i,), start) for i in range(3)])
        acc = accelerate(now, above, below, [cf[number, at, :] for number in range(7)])
        for i in range(3):
            moved = half[i, at, :] + acc[i]
            half[i, at, :] = moved
            f[i, at, :] = now[i] + moved
    for start in starts:
        at = pl.ds(start, CHUNK)
        now, above, below = zip(*[around(f, (i,), start) for i in range(3)])
        acc = accelerate(now, above, below, [cf[number, at, :] for number in range(7)])
        for i in range(3):
            f[3 + i, at, :] = (half[i, at, :] + 0.5 * acc[i]) * (1.0 / FINE_STEP)

    first = is_first()
    matrix = averaging(cols)
    few = rows // 2
    half_cols = cols // 2
    for number, ref in enumerate((kc, ka, mass, hoop)):
        raw[number] = exact_dot(pair_sum(ref, (), 0, few), matrix)
    ckc, cka, cm, ch = raw[0], raw[1], raw[2], raw[3]
    found = scaled_coefficients(
        ckc, turn(ckc, 1, 0), cka, 4.0 * cm, 4.0 * ch, COARSE_STEP, COARSE_COUPLING
    )
    for number in range(7):
        cc[number, 8 : 8 + few, :] = found[number]
    sums = [pair_sum(u, (i,), 0, few) - first * pair_sum(init, (i,), 0, few) for i in range(6)]
    means = exact_dot(jnp.concatenate(sums, axis=0), matrix)
    start_w = [means[i * few : (i + 1) * few] for i in range(3)]
    start_q = [SPEED * means[(3 + i) * few : (4 + i) * few] for i in range(3)]
    moved_w, moved_q = steps_block(start_w, start_q, found, 1)
    means = exact_dot(
        jnp.concatenate([pair_sum(f, (i,), 0, few) for i in range(6)], axis=0), matrix
    )
    for i in range(3):
        b[i] = means[i * few : (i + 1) * few] - moved_w[i]
        b[3 + i] = SPEED * means[(3 + i) * few : (4 + i) * few] - moved_q[i]


def edges_body(
    f_in, u, init, kc, ka, mass, hoop, b_in, cc_in, raw, from_below, from_above,
    f, b, cc, b_to_above, b_to_below, fine, coarse, done, means_at, slots, sems,
):
    pair_sum = Halver(slots)
    rows, cols = kc.shape
    few, half_cols = rows // 2, cols // 2
    first = is_first()
    matrix = averaging(cols)
    fields = [(u, (i,)) for i in range(6)] + [(kc, ()), (ka, ()), (mass, ()), (hoop, ())]
    at = 0
    for number, ((ref, lead), count) in enumerate(zip(fields, FINE_ROWS)):
        fine[number, 8 - count : 8, :] = from_below[at : at + count, :]
        fine[number, 8:24, :] = ref[lead + (slice(0, 16), slice(None))]
        fine[number, 24:40, :] = ref[lead + (slice(rows - 16, rows), slice(None))]
        fine[number, 40 : 40 + count, :] = from_above[at : at + count, :]
        at += count
    found = scaled_coefficients(
        fine[6], turn(fine[6], 1, 0), fine[7], fine[8], fine[9], FINE_STEP, FINE_COUPLING
    )
    w, q = steps_block(
        [fine[i] for i in range(3)], [FINE_STEP * fine[3 + i] for i in range(3)], found, 2
    )
    for i in range(3):
        done[i, 0:8, :] = w[i][8:16]
        done[i, 8:16, :] = w[i][32:40]
        done[3 + i, 0:8, :] = q[i][8:16] * (1.0 / FINE_STEP)
        done[3 + i, 8:16, :] = q[i][32:40] * (1.0 / FINE_STEP)
    low = pltpu.make_async_copy(done.at[:, 0:8], f.at[:, 0:8], sems.at[0])
    high = pltpu.make_async_copy(done.at[:, 8:16], f.at[:, rows - 8 : rows], sems.at[1])
    low.start()
    high.start()

    sums = []
    for start in (0, rows - 16):
        for i in range(6):
            sums.append(pair_sum(u, (i,), start, 8) - first * pair_sum(init, (i,), start, 8))
    for i in range(6):
        sums.append(pair_sum(done, (i,), 0, 8))
    means_at[...] = exact_dot(jnp.concatenate(sums, axis=0), matrix)
    for i in range(6):
        coarse[i, 8:16, :] = means_at[8 * i : 8 * i + 8, :]
        coarse[i, 16:24, :] = means_at[48 + 8 * i : 56 + 8 * i, :]
    for number in range(4):
        coarse[6 + number, 8:16, :] = raw[number, 0:8, :]
        coarse[6 + number, 16:24, :] = raw[number, few - 8 : few, :]
    at = 0
    for number, count in enumerate(COARSE_ROWS):
        for k in range(count):
            place = (
                slice(FINE_TOTAL + at // 2, FINE_TOTAL + at // 2 + 1),
                pl.ds((at % 2) * half_cols, half_cols),
            )
            coarse[number, 8 - count + k : 9 - count + k, :] = from_below[place]
            coarse[number, 24 + k : 25 + k, :] = from_above[place]
            at += 1
    found = scaled_coefficients(
        coarse[6], turn(coarse[6], 1, 0), coarse[7], 4.0 * coarse[8], 4.0 * coarse[9],
        COARSE_STEP, COARSE_COUPLING,
    )
    for number in range(7):
        cc[number, 0:16, :] = found[number][0:16]
        cc[number, 16 : few + 4, :] = cc_in[number, 16 : few + 4, :]
        cc[number, few + 4 : few + 16, :] = found[number][20:32]
    w, q = steps_block(
        [coarse[i] for i in range(3)], [SPEED * coarse[3 + i] for i in range(3)], found, 1
    )
    moved = w + q
    b[...] = b_in[...]
    for i in range(6):
        scale = 1.0 if i < 3 else SPEED
        ends = scale * means_at[96 + 8 * i : 104 + 8 * i, :]
        b[i, 0:4, :] = ends[0:4] - moved[i][8:12]
        b[i, few - 4 : few, :] = ends[4:8] - moved[i][20:24]
    write_edges(b, b_to_above, b_to_below)
    low.wait()
    high.wait()


def write_edges(ref, to_above, to_below):
    few = ref.shape[1]
    for i in range(6):
        to_above[EDGE * i : EDGE * (i + 1), :] = ref[i, few - EDGE : few, :]
        to_below[EDGE * i : EDGE * (i + 1), :] = ref[i, 0:EDGE, :]


def fill_ext(ext, main, below, above):
    few = main.shape[1]
    for i in range(6):
        ext[i, 8 - EDGE : 8, :] = below[EDGE * i : EDGE * (i + 1), :]
        ext[i, 8 : 8 + few, :] = main[i]
        ext[i, 8 + few : 8 + few + EDGE, :] = above[EDGE * i : EDGE * (i + 1), :]


def advance(ext, cc, repeats):
    few = ext.shape[1] - 16
    w, q = steps_block(
        [ext[i] for i in range(3)],
        [ext[3 + i] for i in range(3)],
        [cc[number] for number in range(7)],
        repeats,
    )
    return [value[8 : 8 + few] for value in w + q]


def advance_body(repeats, main, below, above, add, cc, out, to_above, to_below, ext):
    fill_ext(ext, main, below, above)
    for i, value in enumerate(advance(ext, cc, repeats)):
        out[i] = value + add[i]
    write_edges(out, to_above, to_below)


def closing_body(rounds, *refs):
    mains, belows, aboves = refs[:rounds], refs[rounds : 2 * rounds], refs[2 * rounds : 3 * rounds]
    b_even, cc, total, even_end, ext, below, above = refs[3 * rounds :]
    total[...] = sum(ref[...] for ref in mains)
    below[...] = sum(ref[...] for ref in belows)
    above[...] = sum(ref[...] for ref in aboves)
    fill_ext(ext, total, below, above)
    for i, value in enumerate(advance(ext, cc, 1)):
        even_end[i] = value + b_even[i]


def spread_add(values, base, out, cols, slots):
    wide = exact_dot(values, spreading(cols))
    few = wide.shape[0] // 6
    for i in range(6):
        for tile in range(cols // LANES):
            part = wide[i * few : (i + 1) * few, tile * LANES : (tile + 1) * LANES]
            slot = slots.at[i * (cols // LANES) + tile]
            slot[pl.ds(0, few, stride=2), :] = part
            slot[pl.ds(1, few, stride=2), :] = part
            at = (i, slice(None), pl.ds(tile * LANES, LANES))
            out[at] = base[at] + slot[...]


def remainder_body(previous, init, out, slots):
    pair_sum = Halver(slots)
    cols = previous.shape[2]
    few = previous.shape[1] // 2
    sums = [pair_sum(previous, (i,), 0, few) for i in range(6)]
    means = exact_dot(jnp.concatenate(sums, axis=0), averaging(cols))
    spread_add(-means, previous, out, cols, slots)

    @pl.when(lax.axis_index("cuts") == 0)
    def _():
        out[...] = init[...]


def correct_body(base, own, received, out, slots):
    cols = base.shape[2]
    odd = lax.axis_index("cuts") % 2
    values = []
    for i in range(6):
        value = jnp.where(odd == 1, own[i], received[i])
        values.append(value if i < 3 else value * (1.0 / SPEED))
    spread_add(jnp.concatenate(values, axis=0), base, out, cols, slots)


def per_device(start_state, initial_state, circ_stiff, axial_stiff, lumped_mass, hoop_stiff):
    u = start_state[0]
    strips, slices = lax.axis_size("strip"), lax.axis_size("cuts")
    chips = slices // 2
    _, rows, cols = u.shape
    few, half_cols = rows // 2, cols // 2
    state, coarse_state = (6, rows, cols), (6, few, half_cols)
    ext_state = (6, few + 16, half_cols)
    edge = (6 * EDGE, half_cols)
    fields = (circ_stiff, axial_stiff, lumped_mass, hoop_stiff)

    def around_loop(value, by):
        pairs = [(s, (s + by) % strips) for s in range(strips)]
        return lax.ppermute(value, "strip", pairs)

    def send(value, by, moves):
        pairs = [
            (s * slices + source, (s + by) % strips * slices + target)
            for s in range(strips)
            for source, target in moves
        ]
        return lax.ppermute(value, ("strip", "cuts"), pairs)

    def send_with_edges(main, to_above, to_below, moves):
        return (
            send(main, 0, moves),
            send(to_above, 1, moves),
            send(to_below, -1, moves),
        )

    pack = (PACK_ROWS, cols)
    to_above, to_below = run(
        pack_body, "pack", [pack, pack], [u, initial_state, *fields], [halver_scratch(32, 8, cols)]
    )
    from_below = around_loop(to_above, 1)
    from_above = around_loop(to_below, -1)
    f, b, cc, raw = run(
        interior_body,
        "interior",
        [state, coarse_state, (7, few + 16, half_cols), (4, few, half_cols)],
        [u, initial_state, *fields],
        [
            pltpu.VMEM((7, rows, cols), F32),
            pltpu.VMEM((3, rows, cols), F32),
            pltpu.VMEM((3, rows, cols), F32),
            halver_scratch(22, rows, cols),
        ],
    )
    f, b, cc, b_to_above, b_to_below = run(
        edges_body,
        "edges",
        [state, coarse_state, (7, few + 16, half_cols), edge, edge],
        [f, u, initial_state, *fields, b, cc, raw, from_below, from_above],
        [
            pltpu.VMEM((10, 48, cols), F32),
            pltpu.VMEM((10, 32, half_cols), F32),
            pltpu.VMEM((6, 16, cols), F32),
            pltpu.VMEM((144, half_cols), F32),
            halver_scratch(30, 16, cols),
            pltpu.SemaphoreType.DMA((2,)),
        ],
        specs=[ANY] + [VMEM] * 11,
        out_specs=[ANY] + [VMEM] * 4,
        aliases={0: 0},
    )
    inside = [(2 * z, 2 * z + 1) for z in range(chips)]
    b_even, b_below, b_above = send_with_edges(b, b_to_above, b_to_below, inside)
    ext = [pltpu.VMEM(ext_state, F32)]

    def advance_call(repeats, name, main, below, above, add):
        return run(
            lambda *refs: advance_body(repeats, *refs),
            name,
            [coarse_state, edge, edge],
            [main, below, above, add, cc],
            ext,
        )

    source = advance_call(1, "pair", b_even, b_below, b_above, b)
    at_end = source
    arrived = []
    for chip in range(chips - 1):
        moves = [(2 * chip + 1, 2 * chip + 3)]
        arrived.append(send_with_edges(*at_end, moves))
        if chip < chips - 2:
            at_end = advance_call(2, "chain", *arrived[-1], source[0])
    previous = lax.ppermute(f, "cuts", [(j, j + 1) for j in range(slices - 1)])
    mains, belows, aboves = zip(*arrived)
    total, even_end = run(
        lambda *refs: closing_body(chips - 1, *refs),
        "closing",
        [coarse_state, coarse_state],
        [*mains, *belows, *aboves, b_even, cc],
        ext + [pltpu.VMEM(edge, F32)] * 2,
    )
    received = send(total, 0, [(2 * z + 1, 2 * z) for z in range(chips)])
    full = [halver_scratch(6, rows, cols)]
    (base,) = run(remainder_body, "remainder", [state], [previous, initial_state], full)
    (new_start,) = run(correct_body, "correct", [state], [base, even_end, received], full)
    return new_start[None], f[None]


def solution(mesh):
    state = P("cuts", None, "strip", None)
    field = P("strip", None)
    return jax.shard_map(
        per_device,
        mesh=mesh,
        in_specs=(state, P(None, "strip", None), field, field, field, field),
        out_specs=(state, state),
        check_vma=False,
    )
```

time: 341 us -> 75.1 us (0.22)
  the two profiles are of different devices: /device:TPU:24 before, /device:TPU:25 now
where the time goes in v1:
time: 75.1 us; the launch traced here: 74.6 us
  waiting for transfers between devices  37.7 us (50%)
  starting transfers between devices  16.9 us (23%)
  Pallas kernels  12.5 us (17%)
  local copies, waits for them, and re-layouts  6.61 us (9%)
  between operations  0.88 us (1%)
    ppermute x13, waiting for transfers between devices, send(): return lax.ppermute(value, ('strip', 'cuts'), pairs)  37.7 us
    ppermute x13, starting transfers between devices, send(): return lax.ppermute(value, ('strip', 'cuts'), pairs)  13.2 us
    pallas_call x9, Pallas kernels, run(): pl.pallas_call(body, name=name, out_shape=[jax.ShapeDtypeStruct(shape, F3...  12.5 us
    unnamed x14, local copies, waits for them, and re-layouts  6.61 us
    ppermute x2, starting transfers between devices, around_loop(): return lax.ppermute(value, 'strip', pairs)  2.42 us
  transfers between devices with their start and end apart: 16, of which 3 were waited for; matrix products, arithmetic and copies ran while one was open for 0% of the time, Pallas kernels for 11%

profile of v1, /device:TPU:25, one launch (start us, length us, event | category | flops | bytes accessed | tf_op | source)
XLA Modules:
  0.0 74.6 jit_solution(13317674906758547293)
XLA Ops:
  0.6 0.0 copy-start
  0.6 1.4 %copy-done = f32[6,128,512]{2,1,0:T(8,128)S(1)} copy-done((f32[6,128,512]{2,1,0:T(8,128)S(1)}, f32[6,128,512]{2,1,0:T(8,128)}, u32[]{:S(2)}) %copy-start) | copy-done | bytes 1572888
  2.0 0.0 copy-start.2
  2.0 1.4 %copy-done.2 = f32[1,6,128,512]{3,2,1,0:T(8,128)S(1)} copy-done((f32[1,6,128,512]{3,2,1,0:T(8,128)S(1)}, f32[1,6,128,512]{3,2,1,0:T(8,128)}, u32[]{:S(2)}) %copy-start.2) | copy-done | bytes 1572888
  3.5 0.0 copy-start.3
  3.5 0.9 %copy-done.3 = f32[128,512]{1,0:T(8,128)S(1)} copy-done((f32[128,512]{1,0:T(8,128)S(1)}, f32[128,512]{1,0:T(8,128)}, u32[]{:S(2)}) %copy-start.3) | copy-done | bytes 262168
  4.4 0.0 copy-start.4
  4.4 0.9 %copy-done.4 = f32[128,512]{1,0:T(8,128)S(1)} copy-done((f32[128,512]{1,0:T(8,128)S(1)}, f32[128,512]{1,0:T(8,128)}, u32[]{:S(2)}) %copy-start.4) | copy-done | bytes 262168
  5.4 0.0 copy-start.5
  5.4 0.9 %copy-done.5 = f32[128,512]{1,0:T(8,128)S(1)} copy-done((f32[128,512]{1,0:T(8,128)S(1)}, f32[128,512]{1,0:T(8,128)}, u32[]{:S(2)}) %copy-start.5) | copy-done | bytes 262168
  6.3 0.0 copy-start.6
  6.3 0.9 %copy-done.6 = f32[128,512]{1,0:T(8,128)S(1)} copy-done((f32[128,512]{1,0:T(8,128)S(1)}, f32[128,512]{1,0:T(8,128)}, u32[]{:S(2)}) %copy-start.6) | copy-done | bytes 262168
  7.3 0.4 pack.1
  7.6 1.3 %collective-permute-start = (f32[40,512]{1,0:T(8,128)S(1)}, f32[40,512]{1,0:T(8,128)S(1)}, u32[]{:S(2)}, u32[]{:S(2)}) collective-permute-start(f32[40,512]{1,0:T(8,128)S(1)} %get-tuple-element.28), channel_id=1, source_target_pairs={{0,8},{8,16},{16,24},{24,0},{1,9},{9,17},{17,25},{25,1},{2,10},{10... | collective-permute-start | bytes 245768 | tf_op jit(solution)/shard_map/ppermute | solution.py:423
  8.9 1.2 %collective-permute-start.1 = (f32[40,512]{1,0:T(8,128)S(1)}, f32[40,512]{1,0:T(8,128)S(1)}, u32[]{:S(2)}, u32[]{:S(2)}) collective-permute-start(f32[40,512]{1,0:T(8,128)S(1)} %get-tuple-element.29), channel_id=1, source_target_pairs={{0,24},{8,0},{16,8},{24,16},{1,25},{9,1},{17,9},{25,17},{2,26},{10... | collective-permute-start | bytes 245768 | tf_op jit(solution)/shard_map/ppermute | solution.py:423
  10.0 4.8 %interior.1 = (f32[6,128,512]{2,1,0:T(8,128)}, f32[6,64,256]{2,1,0:T(8,128)S(1)}, f32[7,80,256]{2,1,0:T(8,128)S(1)}, f32[4,64,256]{2,1,0:T(8,128)S(1)}) custom-call(f32[6,128,512]{2,1,0:T(8,128)S(1)} %bitcast.4, f32[6,128,512]{2,1,0:T(8,128)S(1)} %copy-done, f32[128,512]{1,0:T(8,128)S(1)} %copy-done.3, f32[128,512]{1,0:T(8,128)S(1)} %copy-done.4, ...), custom_call_target="tpu_custom_call" | custom-call | tf_op jit(solution)/shard_map/interior/pallas_call | solution.py:27
  14.9 0.0 collective-permute-done.from_below
  14.9 0.0 collective-permute-done.1.from_above
  14.9 1.8 %edges.1 = (f32[6,128,512]{2,1,0:T(8,128)}, f32[6,64,256]{2,1,0:T(8,128)S(1)}, f32[7,80,256]{2,1,0:T(8,128)S(1)}, f32[24,256]{1,0:T(8,128)S(1)}, f32[24,256]{1,0:T(8,128)S(1)}) custom-call(f32[6,128,512]{2,1,0:T(8,128)} %get-tuple-element.24.f_in, f32[6,128,512]{2,1,0:T(8,128)S(1)} %bitcast.5, ...), custom_call_target="tpu_custom_call", output_to_operand_aliasing={{0}: (0, {})} | custom-call | tf_op jit(solution)/shard_map/edges/pallas_call | solution.py:27
  16.7 1.3 %collective-permute-start.3 = (f32[6,64,256]{2,1,0:T(8,128)S(1)}, f32[6,64,256]{2,1,0:T(8,128)S(1)}, u32[]{:S(2)}, u32[]{:S(2)}) collective-permute-start(f32[6,64,256]{2,1,0:T(8,128)S(1)} %get-tuple-element.31.refs_3_), channel_id=1, source_target_pairs={{0,1},{2,3},{4,5},{6,7},{8,9},{10,11},{12,13},{14,15},{16,17},{18,... | collective-permute-start | bytes 1179656 | tf_op jit(solution)/shard_map/ppermute | solution.py:431
  18.0 1.3 %collective-permute-start.4 = (f32[24,256]{1,0:T(8,128)S(1)}, f32[24,256]{1,0:T(8,128)S(1)}, u32[]{:S(2)}, u32[]{:S(2)}) collective-permute-start(f32[24,256]{1,0:T(8,128)S(1)} %get-tuple-element.32), channel_id=1, source_target_pairs={{0,9},{2,11},{4,13},{6,15},{8,17},{10,19},{12,21},{14,23},{16,25},... | collective-permute-start | bytes 73736 | tf_op jit(solution)/shard_map/ppermute | solution.py:431
  19.3 1.3 %collective-permute-start.5 = (f32[24,256]{1,0:T(8,128)S(1)}, f32[24,256]{1,0:T(8,128)S(1)}, u32[]{:S(2)}, u32[]{:S(2)}) collective-permute-start(f32[24,256]{1,0:T(8,128)S(1)} %get-tuple-element.33), channel_id=1, source_target_pairs={{0,25},{2,27},{4,29},{6,31},{8,1},{10,3},{12,5},{14,7},{16,9},{18,... | collective-permute-start | bytes 73736 | tf_op jit(solution)/shard_map/ppermute | solution.py:431
  20.6 3.4 %collective-permute-done.4.refs_1_ = f32[24,256]{1,0:T(8,128)S(1)} collective-permute-done((f32[24,256]{1,0:T(8,128)S(1)}, f32[24,256]{1,0:T(8,128)S(1)}, u32[]{:S(2)}, u32[]{:S(2)}) %collective-permute-start.4) | collective-permute-done | bytes 24608 | tf_op jit(solution)/shard_map/ppermute | solution.py:431
  24.1 1.4 %collective-permute-done.5.refs_2_ = f32[24,256]{1,0:T(8,128)S(1)} collective-permute-done((f32[24,256]{1,0:T(8,128)S(1)}, f32[24,256]{1,0:T(8,128)S(1)}, u32[]{:S(2)}, u32[]{:S(2)}) %collective-permute-start.5) | collective-permute-done | bytes 24608 | tf_op jit(solution)/shard_map/ppermute | solution.py:431
  25.4 0.0 collective-permute-done.3.refs_0_.refs_9_
  25.4 0.4 pair.1
  25.9 0.7 collective-permute-start.6
  26.6 1.3 %collective-permute-start.2 = (f32[6,128,512]{2,1,0:T(8,128)}, f32[6,128,512]{2,1,0:T(8,128)S(1)}, u32[]{:S(2)}, u32[]{:S(2)}) collective-permute-start(f32[6,128,512]{2,1,0:T(8,128)} %get-tuple-element.30), channel_id=1, source_target_pairs={{0,1},{1,2},{2,3},{3,4},{4,5},{5,6},{6,7},{8,9},{9,10},{10,11},{11... | collective-permute-start | bytes 4718600 | tf_op jit(solution)/shard_map/ppermute | solution.py:496
  27.9 0.7 collective-permute-start.7
  28.5 0.7 collective-permute-start.8
  29.2 0.0 collective-permute-done.7.refs_1_.refs_3_
  29.2 0.0 collective-permute-done.8.refs_2_.refs_6_
  29.2 0.0 collective-permute-done.6.refs_0_
  29.2 0.6 chain.2
  29.9 0.7 collective-permute-start.9
  30.6 0.7 collective-permute-start.10
  31.2 0.0 copy-start.1
  31.2 0.8 %collective-permute-start.11 = (f32[24,256]{1,0:T(8,128)S(1)}, f32[24,256]{1,0:T(8,128)S(1)}, u32[]{:S(2)}, u32[]{:S(2)}) collective-permute-start(f32[24,256]{1,0:T(8,128)S(1)} %get-tuple-element.40), channel_id=1, source_target_pairs={{3,29},{11,5},{19,13},{27,21}} | collective-permute-start | bytes 73736 | tf_op jit(solution)/shard_map/ppermute | solution.py:431
  32.0 0.0 collective-permute-done.10.refs_1_.refs_4_
  32.0 0.0 collective-permute-done.11.refs_2_.refs_7_
  32.1 0.0 collective-permute-done.9.refs_0_.refs_1_
  32.1 0.6 chain.3
  32.7 1.3 %collective-permute-start.12 = (f32[6,64,256]{2,1,0:T(8,128)S(1)}, f32[6,64,256]{2,1,0:T(8,128)S(1)}, u32[]{:S(2)}, u32[]{:S(2)}) collective-permute-start(f32[6,64,256]{2,1,0:T(8,128)S(1)} %get-tuple-element.41), channel_id=1, source_target_pairs={{5,7},{13,15},{21,23},{29,31}} | collective-permute-start | bytes 1179656 | tf_op jit(solution)/shard_map/ppermute | solution.py:431
  34.0 1.3 %collective-permute-start.13 = (f32[24,256]{1,0:T(8,128)S(1)}, f32[24,256]{1,0:T(8,128)S(1)}, u32[]{:S(2)}, u32[]{:S(2)}) collective-permute-start(f32[24,256]{1,0:T(8,128)S(1)} %get-tuple-element.42), channel_id=1, source_target_pairs={{5,15},{13,23},{21,31},{29,7}} | collective-permute-start | bytes 73736 | tf_op jit(solution)/shard_map/ppermute | solution.py:431
  35.3 1.3 %collective-permute-start.14 = (f32[24,256]{1,0:T(8,128)S(1)}, f32[24,256]{1,0:T(8,128)S(1)}, u32[]{:S(2)}, u32[]{:S(2)}) collective-permute-start(f32[24,256]{1,0:T(8,128)S(1)} %get-tuple-element.43), channel_id=1, source_target_pairs={{5,31},{13,7},{21,15},{29,23}} | collective-permute-start | bytes 73736 | tf_op jit(solution)/shard_map/ppermute | solution.py:431
  36.6 32.9 %collective-permute-done.13.refs_5_ = f32[24,256]{1,0:T(8,128)S(1)} collective-permute-done((f32[24,256]{1,0:T(8,128)S(1)}, f32[24,256]{1,0:T(8,128)S(1)}, u32[]{:S(2)}, u32[]{:S(2)}) %collective-permute-start.13) | collective-permute-done | bytes 24608 | tf_op jit(solution)/shard_map/ppermute | solution.py:431
  69.5 0.0 collective-permute-done.14.refs_8_
  69.5 0.0 collective-permute-done.12.refs_2_
  69.5 0.4 closing.1
  70.0 1.3 %collective-permute-start.15 = (f32[6,64,256]{2,1,0:T(8,128)S(1)}, f32[6,64,256]{2,1,0:T(8,128)S(1)}, u32[]{:S(2)}, u32[]{:S(2)}) collective-permute-start(f32[6,64,256]{2,1,0:T(8,128)S(1)} %get-tuple-element.45), channel_id=1, source_target_pairs={{1,0},{3,2},{5,4},{7,6},{9,8},{11,10},{13,12},{15,14},{17,16},{19,... | collective-permute-start | bytes 1179656 | tf_op jit(solution)/shard_map/ppermute | solution.py:431
  71.3 0.0 collective-permute-done.2.previous
  71.3 0.0 copy-done.1
  71.3 1.5 %remainder.1.base = f32[6,128,512]{2,1,0:T(8,128)S(1)} custom-call(f32[6,128,512]{2,1,0:T(8,128)S(1)} %collective-permute-done.2.previous, f32[6,128,512]{2,1,0:T(8,128)S(1)} %copy-done.1), custom_call_target="tpu_custom_call" | custom-call | tf_op jit(solution)/shard_map/remainder/pallas_call | solution.py:27
  72.8 0.0 collective-permute-done.15.received
  72.8 1.8 %correct.1 = f32[6,128,512]{2,1,0:T(8,128)} custom-call(f32[6,128,512]{2,1,0:T(8,128)S(1)} %remainder.1.base, f32[6,64,256]{2,1,0:T(8,128)S(1)} %get-tuple-element.44.own, f32[6,64,256]{2,1,0:T(8,128)S(1)} %collective-permute-done.15.received), custom_call_target="tpu_custom_call" | custom-call | tf_op jit(solution)/shard_map/correct/pallas_call | solution.py:27
Async XLA Ops:
  0.6 1.4 %copy-start = (f32[6,128,512]{2,1,0:T(8,128)S(1)}, f32[6,128,512]{2,1,0:T(8,128)}, u32[]{:S(2)}) copy-start(f32[6,128,512]{2,1,0:T(8,128)} %init.7) | copy-start | bytes 4718596
  2.0 1.4 %copy-start.2 = (f32[1,6,128,512]{3,2,1,0:T(8,128)S(1)}, f32[1,6,128,512]{3,2,1,0:T(8,128)}, u32[]{:S(2)}) copy-start(f32[1,6,128,512]{3,2,1,0:T(8,128)} %param.6) | copy-start | bytes 4718596
  3.5 0.9 %copy-start.3 = (f32[128,512]{1,0:T(8,128)S(1)}, f32[128,512]{1,0:T(8,128)}, u32[]{:S(2)}) copy-start(f32[128,512]{1,0:T(8,128)} %kc.5) | copy-start | bytes 786436
  4.4 0.9 %copy-start.4 = (f32[128,512]{1,0:T(8,128)S(1)}, f32[128,512]{1,0:T(8,128)}, u32[]{:S(2)}) copy-start(f32[128,512]{1,0:T(8,128)} %ka.5) | copy-start | bytes 786436
  5.4 0.9 %copy-start.5 = (f32[128,512]{1,0:T(8,128)S(1)}, f32[128,512]{1,0:T(8,128)}, u32[]{:S(2)}) copy-start(f32[128,512]{1,0:T(8,128)} %mass.5) | copy-start | bytes 786436
  6.3 0.9 %copy-start.6 = (f32[128,512]{1,0:T(8,128)S(1)}, f32[128,512]{1,0:T(8,128)}, u32[]{:S(2)}) copy-start(f32[128,512]{1,0:T(8,128)} %hoop.5) | copy-start | bytes 786436
  7.6 7.2 %collective-permute-start = (f32[40,512]{1,0:T(8,128)S(1)}, f32[40,512]{1,0:T(8,128)S(1)}, u32[]{:S(2)}, u32[]{:S(2)}) collective-permute-start(f32[40,512]{1,0:T(8,128)S(1)} %get-tuple-element.28), channel_id=1, source_target_pairs={{0,8},{8,16},{16,24},{24,0},{1,9},{9,17},{17,25},{25,1},{2,10},{10... | collective-permute-start | bytes 245768 | tf_op jit(solution)/shard_map/ppermute | solution.py:423
  8.9 6.0 %collective-permute-start.1 = (f32[40,512]{1,0:T(8,128)S(1)}, f32[40,512]{1,0:T(8,128)S(1)}, u32[]{:S(2)}, u32[]{:S(2)}) collective-permute-start(f32[40,512]{1,0:T(8,128)S(1)} %get-tuple-element.29), channel_id=1, source_target_pairs={{0,24},{8,0},{16,8},{24,16},{1,25},{9,1},{17,9},{25,17},{2,26},{10... | collective-permute-start | bytes 245768 | tf_op jit(solution)/shard_map/ppermute | solution.py:423
  16.7 8.7 %collective-permute-start.3 = (f32[6,64,256]{2,1,0:T(8,128)S(1)}, f32[6,64,256]{2,1,0:T(8,128)S(1)}, u32[]{:S(2)}, u32[]{:S(2)}) collective-permute-start(f32[6,64,256]{2,1,0:T(8,128)S(1)} %get-tuple-element.31.refs_3_), channel_id=1, source_target_pairs={{0,1},{2,3},{4,5},{6,7},{8,9},{10,11},{12,13},{14,15},{16,17},{18,... | collective-permute-start | bytes 1179656 | tf_op jit(solution)/shard_map/ppermute | solution.py:431
  18.0 6.0 %collective-permute-start.4 = (f32[24,256]{1,0:T(8,128)S(1)}, f32[24,256]{1,0:T(8,128)S(1)}, u32[]{:S(2)}, u32[]{:S(2)}) collective-permute-start(f32[24,256]{1,0:T(8,128)S(1)} %get-tuple-element.32), channel_id=1, source_target_pairs={{0,9},{2,11},{4,13},{6,15},{8,17},{10,19},{12,21},{14,23},{16,25},... | collective-permute-start | bytes 73736 | tf_op jit(solution)/shard_map/ppermute | solution.py:431
  19.3 6.1 %collective-permute-start.5 = (f32[24,256]{1,0:T(8,128)S(1)}, f32[24,256]{1,0:T(8,128)S(1)}, u32[]{:S(2)}, u32[]{:S(2)}) collective-permute-start(f32[24,256]{1,0:T(8,128)S(1)} %get-tuple-element.33), channel_id=1, source_target_pairs={{0,25},{2,27},{4,29},{6,31},{8,1},{10,3},{12,5},{14,7},{16,9},{18,... | collective-permute-start | bytes 73736 | tf_op jit(solution)/shard_map/ppermute | solution.py:431
  25.9 3.4 %collective-permute-start.6 = (f32[6,64,256]{2,1,0:T(8,128)S(1)}, f32[6,64,256]{2,1,0:T(8,128)S(1)}, u32[]{:S(2)}, u32[]{:S(2)}) collective-permute-start(f32[6,64,256]{2,1,0:T(8,128)S(1)} %get-tuple-element.35.refs_3_), channel_id=1, source_target_pairs={{1,3},{9,11},{17,19},{25,27}} | collective-permute-start | bytes 1179656 | tf_op jit(solution)/shard_map/ppermute | solution.py:431
  26.6 44.7 %collective-permute-start.2 = (f32[6,128,512]{2,1,0:T(8,128)}, f32[6,128,512]{2,1,0:T(8,128)S(1)}, u32[]{:S(2)}, u32[]{:S(2)}) collective-permute-start(f32[6,128,512]{2,1,0:T(8,128)} %get-tuple-element.30), channel_id=1, source_target_pairs={{0,1},{1,2},{2,3},{3,4},{4,5},{5,6},{6,7},{8,9},{9,10},{10,11},{11... | collective-permute-start | bytes 4718600 | tf_op jit(solution)/shard_map/ppermute | solution.py:496
  27.9 1.3 %collective-permute-start.7 = (f32[24,256]{1,0:T(8,128)S(1)}, f32[24,256]{1,0:T(8,128)S(1)}, u32[]{:S(2)}, u32[]{:S(2)}) collective-permute-start(f32[24,256]{1,0:T(8,128)S(1)} %get-tuple-element.36), channel_id=1, source_target_pairs={{1,11},{9,19},{17,27},{25,3}} | collective-permute-start | bytes 73736 | tf_op jit(solution)/shard_map/ppermute | solution.py:431
  28.5 0.7 collective-permute-start.8
  29.9 2.2 %collective-permute-start.9 = (f32[6,64,256]{2,1,0:T(8,128)S(1)}, f32[6,64,256]{2,1,0:T(8,128)S(1)}, u32[]{:S(2)}, u32[]{:S(2)}) collective-permute-start(f32[6,64,256]{2,1,0:T(8,128)S(1)} %get-tuple-element.38), channel_id=1, source_target_pairs={{3,5},{11,13},{19,21},{27,29}} | collective-permute-start | bytes 1179656 | tf_op jit(solution)/shard_map/ppermute | solution.py:431
  30.6 1.5 %collective-permute-start.10 = (f32[24,256]{1,0:T(8,128)S(1)}, f32[24,256]{1,0:T(8,128)S(1)}, u32[]{:S(2)}, u32[]{:S(2)}) collective-permute-start(f32[24,256]{1,0:T(8,128)S(1)} %get-tuple-element.39), channel_id=1, source_target_pairs={{3,13},{11,21},{19,29},{27,5}} | collective-permute-start | bytes 73736 | tf_op jit(solution)/shard_map/ppermute | solution.py:431
  31.2 40.1 %copy-start.1 = (f32[6,128,512]{2,1,0:T(8,128)S(1)}, f32[6,128,512]{2,1,0:T(8,128)}, u32[]{:S(2)}) copy-start(f32[6,128,512]{2,1,0:T(8,128)} %init.7) | copy-start | bytes 4718596
  31.2 0.8 %collective-permute-start.11 = (f32[24,256]{1,0:T(8,128)S(1)}, f32[24,256]{1,0:T(8,128)S(1)}, u32[]{:S(2)}, u32[]{:S(2)}) collective-permute-start(f32[24,256]{1,0:T(8,128)S(1)} %get-tuple-element.40), channel_id=1, source_target_pairs={{3,29},{11,5},{19,13},{27,21}} | collective-permute-start | bytes 73736 | tf_op jit(solution)/shard_map/ppermute | solution.py:431
  32.7 36.8 %collective-permute-start.12 = (f32[6,64,256]{2,1,0:T(8,128)S(1)}, f32[6,64,256]{2,1,0:T(8,128)S(1)}, u32[]{:S(2)}, u32[]{:S(2)}) collective-permute-start(f32[6,64,256]{2,1,0:T(8,128)S(1)} %get-tuple-element.41), channel_id=1, source_target_pairs={{5,7},{13,15},{21,23},{29,31}} | collective-permute-start | bytes 1179656 | tf_op jit(solution)/shard_map/ppermute | solution.py:431
  34.0 35.5 %collective-permute-start.13 = (f32[24,256]{1,0:T(8,128)S(1)}, f32[24,256]{1,0:T(8,128)S(1)}, u32[]{:S(2)}, u32[]{:S(2)}) collective-permute-start(f32[24,256]{1,0:T(8,128)S(1)} %get-tuple-element.42), channel_id=1, source_target_pairs={{5,15},{13,23},{21,31},{29,7}} | collective-permute-start | bytes 73736 | tf_op jit(solution)/shard_map/ppermute | solution.py:431
  35.3 34.2 %collective-permute-start.14 = (f32[24,256]{1,0:T(8,128)S(1)}, f32[24,256]{1,0:T(8,128)S(1)}, u32[]{:S(2)}, u32[]{:S(2)}) collective-permute-start(f32[24,256]{1,0:T(8,128)S(1)} %get-tuple-element.43), channel_id=1, source_target_pairs={{5,31},{13,7},{21,15},{29,23}} | collective-permute-start | bytes 73736 | tf_op jit(solution)/shard_map/ppermute | solution.py:431
  70.0 2.9 %collective-permute-start.15 = (f32[6,64,256]{2,1,0:T(8,128)S(1)}, f32[6,64,256]{2,1,0:T(8,128)S(1)}, u32[]{:S(2)}, u32[]{:S(2)}) collective-permute-start(f32[6,64,256]{2,1,0:T(8,128)S(1)} %get-tuple-element.45), channel_id=1, source_target_pairs={{1,0},{3,2},{5,4},{7,6},{9,8},{11,10},{13,12},{15,14},{17,16},{19,... | collective-permute-start | bytes 1179656 | tf_op jit(solution)/shard_map/ppermute | solution.py:431

commit v2 on v1

v2 whole, which is shorter than its diff:
```python
import jax
import jax.numpy as jnp
from jax import lax
from jax.experimental import pallas as pl
from jax.experimental.pallas import tpu as pltpu
from jax.sharding import PartitionSpec as P

FINE_STEP = 0.35
COARSE_STEP = 0.7
FINE_COUPLING = 0.25
COARSE_COUPLING = 0.5
SPEED = COARSE_STEP

FINE_ROWS = (3, 3, 3, 2, 2, 2, 3, 2, 2, 2)
COARSE_ROWS = (2, 2, 2, 1, 1, 1, 3, 2, 2, 2)
FINE_TOTAL = sum(FINE_ROWS)
PACK_ROWS = -(-(FINE_TOTAL + -(-sum(COARSE_ROWS) // 2)) // 8) * 8
CHUNK = 8
EDGE = 4
FRONT = 3

VMEM = pl.BlockSpec(memory_space=pltpu.VMEM)
ANY = pl.BlockSpec(memory_space=pl.ANY)
HBM = pl.BlockSpec(memory_space=pltpu.HBM)
F32 = jnp.float32


def run(body, name, outs, args, scratch=(), specs=None, out_specs=None, aliases=None, cost=None):
    if specs:
        args = [
            pltpu.with_memory_space_constraint(arg, pltpu.HBM) if spec is HBM else arg
            for arg, spec in zip(args, specs)
        ]
    return pl.pallas_call(
        body,
        name=name,
        out_shape=[jax.ShapeDtypeStruct(shape, F32) for shape in outs],
        in_specs=specs or [VMEM] * len(args),
        out_specs=out_specs or [VMEM] * len(outs),
        scratch_shapes=list(scratch),
        input_output_aliases=aliases or {},
        compiler_params=pltpu.CompilerParams(vmem_limit_bytes=20 << 20),
        cost_estimate=cost
        and pl.CostEstimate(flops=cost[0], bytes_accessed=cost[1], transcendentals=0),
    )(*args)


def turn(value, steps, axis):
    return pltpu.roll(value, steps % value.shape[axis], axis)


def scaled_coefficients(kc, kc_low, ka, mass, hoop, step, coupling):
    lane = lax.broadcasted_iota(jnp.int32, ka.shape, 1)
    last = ka.shape[1] - 1
    ka_next = jnp.where(lane == last, 0.0, ka)
    ka_low = jnp.where(lane == 0, 0.0, turn(ka, 1, 1))
    unit = (step * step) / mass
    return (
        kc * unit,
        kc_low * unit,
        ka_next * unit,
        ka_low * unit,
        (kc + kc_low + ka + ka_low) * unit,
        hoop * unit,
        (0.5 * coupling) * unit,
    )


def accelerate(now, above, below, cf):
    up, down, fore, aft, centre, hoop, cross = cf
    out = []
    for i in range(3):
        w = now[i]
        out.append(
            up * above[i]
            + down * below[i]
            + fore * turn(w, -1, 1)
            + aft * turn(w, 1, 1)
            - centre * w
        )
    out[0] = out[0] - cross * (above[2] - below[2])
    out[2] = out[2] + cross * (above[0] - below[0]) - hoop * now[2]
    return out


def accelerate_block(now, cf):
    above = [turn(w, -1, 0) for w in now]
    below = [turn(w, 1, 0) for w in now]
    return accelerate(now, above, below, cf)


def steps_block(w, q, cf, repeats):
    acc = accelerate_block(w, cf)
    for _ in range(repeats):
        half = [a + 0.5 * b for a, b in zip(q, acc)]
        w = [a + b for a, b in zip(w, half)]
        acc = accelerate_block(w, cf)
        q = [a + 0.5 * b for a, b in zip(half, acc)]
    return w, q


def three_parts(value):
    high = value.astype(jnp.bfloat16)
    rest = value - high.astype(F32)
    middle = rest.astype(jnp.bfloat16)
    low = (rest - middle.astype(F32)).astype(jnp.bfloat16)
    return high, middle, low


def exact_dot(value, matrix):
    return sum(
        jnp.dot(part, matrix, preferred_element_type=F32) for part in three_parts(value)[::-1]
    )


def averaging(cols):
    row = lax.broadcasted_iota(jnp.int32, (cols, cols // 2), 0)
    col = lax.broadcasted_iota(jnp.int32, (cols, cols // 2), 1)
    return jnp.where(row // 2 == col, 0.25, 0.0).astype(jnp.bfloat16)


def spreading(cols):
    row = lax.broadcasted_iota(jnp.int32, (cols // 2, cols), 0)
    col = lax.broadcasted_iota(jnp.int32, (cols // 2, cols), 1)
    return jnp.where(col // 2 == row, 1.0, 0.0).astype(jnp.bfloat16)


LANES = 128


class Halver:
    def __init__(self, ref):
        self.ref = ref
        self.used = 0

    def __call__(self, source, lead, start, count):
        pieces = []
        for at in range(0, source.shape[-1], LANES):
            slot = self.ref.at[self.used]
            self.used += 1
            slot[0 : 2 * count, :] = source[
                lead + (pl.ds(start, 2 * count), pl.ds(at, LANES))
            ]
            pieces.append(
                slot[pl.ds(0, count, stride=2), :] + slot[pl.ds(1, count, stride=2), :]
            )
        return jnp.concatenate(pieces, axis=1)


def halver_scratch(fields, rows, cols):
    return pltpu.VMEM((fields * (cols // LANES), rows, LANES), F32)


def field_of(front, back, i):
    return (front, i) if i < FRONT else (back, i - FRONT)


def is_first():
    return (lax.axis_index("cuts") == 0).astype(F32)


def pack_body(
    u_far, init, kc_far, ka_far, mass_far, hoop_far,
    to_above, to_below, own, own_coarse, u, kc, ka, mass, hoop, early, slots, sems,
):
    rows, cols = kc.shape
    pair_sum = Halver(slots)
    first = is_first()
    copies = [(init.at[:, start : start + 8], early.at[:, pl.ds(8 * end, 8)])
              for end, start in enumerate((0, rows - 8))]
    copies += [(u_far, u), (kc_far, kc), (ka_far, ka), (mass_far, mass), (hoop_far, hoop)]
    copies = [
        pltpu.make_async_copy(source, target, sems.at[n])
        for n, (source, target) in enumerate(copies)
    ]
    for copy in copies:
        copy.start()
    matrix = averaging(cols)
    for copy in copies:
        copy.wait()
    for end, start in enumerate((0, rows - 8)):
        at = pl.ds(8 * end, 8)
        for i in range(6):
            own[i, at, :] = u[i, start : start + 8, :]
        for number, ref in enumerate((kc, ka, mass, hoop)):
            own[6 + number, at, :] = ref[start : start + 8, :]
    at = 0
    for number, count in enumerate(FINE_ROWS):
        to_above[at : at + count, :] = own[number, 16 - count : 16, :]
        to_below[at : at + count, :] = own[number, 0:count, :]
        at += count
    sums = []
    for number in range(10):
        value = pair_sum(own, (number,), 0, 8)
        if number < 6:
            value = value - first * pair_sum(early, (number,), 0, 8)
        sums.append(value)
    means = exact_dot(jnp.concatenate(sums, axis=0), matrix)
    for number in range(10):
        own_coarse[number] = means[8 * number : 8 * number + 8]
    half = cols // 2
    at = 0
    for number, count in enumerate(COARSE_ROWS):
        for k in range(count):
            line = FINE_TOTAL + at // 2
            place = (slice(line, line + 1), pl.ds((at % 2) * half, half))
            low = 8 * number + 8 - count + k
            high = 8 * number + k
            to_above[place] = means[low : low + 1]
            to_below[place] = means[high : high + 1]
            at += 1


def interior_body(
    u, init, kc, ka, mass, hoop, front, back, b, cc, f_ends,
    cf, w1, half, sums, late, slots, sem,
):
    pair_sum = Halver(slots)
    rows, cols = kc.shape
    starts = range(0, rows, CHUNK)
    first = lax.axis_index("cuts") == 0
    prescribed = pltpu.make_async_copy(init, late, sem)

    @pl.when(first)
    def _():
        prescribed.start()

    def around(ref, lead, start):
        now = ref[lead + (pl.ds(start, CHUNK), slice(None))]
        if start + CHUNK < rows:
            above = ref[lead + (pl.ds(start + 1, CHUNK), slice(None))]
        else:
            above = turn(now, -1, 0)
        if start > 0:
            below = ref[lead + (pl.ds(start - 1, CHUNK), slice(None))]
        else:
            below = turn(now, 1, 0)
        return now, above, below

    for start in starts:
        at = pl.ds(start, CHUNK)
        stiff, _, stiff_low = around(kc, (), start)
        found = scaled_coefficients(
            stiff, stiff_low, ka[at, :], mass[at, :], hoop[at, :], FINE_STEP, FINE_COUPLING
        )
        for number in range(7):
            cf[number, at, :] = found[number]
        now, above, below = zip(*[around(u, (i,), start) for i in range(3)])
        acc = accelerate(now, above, below, found)
        for i in range(3):
            moved = FINE_STEP * u[3 + i, at, :] + 0.5 * acc[i]
            half[i, at, :] = moved
            w1[i, at, :] = now[i] + moved
    for start in starts:
        at = pl.ds(start, CHUNK)
        now, above, below = zip(*[around(w1, (i,), start) for i in range(3)])
        acc = accelerate(now, above, below, [cf[number, at, :] for number in range(7)])
        for i in range(3):
            moved = half[i, at, :] + acc[i]
            half[i, at, :] = moved
            front[i, at, :] = now[i] + moved
    for start in starts:
        at = pl.ds(start, CHUNK)
        now, above, below = zip(*[around(front, (i,), start) for i in range(3)])
        acc = accelerate(now, above, below, [cf[number, at, :] for number in range(7)])
        for i in range(3):
            ref, lead = field_of(front, back, 3 + i)
            ref[lead, at, :] = (half[i, at, :] + 0.5 * acc[i]) * (1.0 / FINE_STEP)

    for i in range(6):
        ref, lead = field_of(front, back, i)
        for end, start in enumerate((0, rows - 8)):
            f_ends[i, 8 * end : 8 * end + 8, :] = ref[lead, start : start + 8, :]

    matrix = averaging(cols)
    few = rows // 2
    for i in range(6):
        sums[i * few : (i + 1) * few, :] = pair_sum(u, (i,), 0, few)
    for number, ref in enumerate((kc, ka, mass, hoop)):
        sums[(6 + number) * few : (7 + number) * few, :] = pair_sum(ref, (), 0, few)

    @pl.when(first)
    def _():
        prescribed.wait()
        for i in range(6):
            sums[i * few : (i + 1) * few, :] -= pair_sum(late, (i,), 0, few)

    means = exact_dot(sums[...], matrix)
    parts = [means[i * few : (i + 1) * few] for i in range(10)]
    ckc, cka, cm, ch = parts[6:]
    found = scaled_coefficients(
        ckc, turn(ckc, 1, 0), cka, 4.0 * cm, 4.0 * ch, COARSE_STEP, COARSE_COUPLING
    )
    for number in range(7):
        cc[number, 8 : 8 + few, :] = found[number]
    moved = sum(steps_block(parts[:3], [SPEED * q for q in parts[3:6]], found, 1), [])
    means = exact_dot(
        jnp.concatenate(
            [
                pair_sum(ref, (lead,), 0, few)
                for ref, lead in (field_of(front, back, i) for i in range(6))
            ],
            axis=0,
        ),
        matrix,
    )
    for i in range(6):
        scale = 1.0 if i < 3 else SPEED
        b[i] = scale * means[i * few : (i + 1) * few] - moved[i]


def edges_body(
    front_in, back_in, f_ends, own, own_coarse, b_in, cc_in, from_below, from_above,
    front, back, b, cc, fine, coarse, done, slots, sems,
):
    rows, cols = front.shape[1:]
    few, half_cols = rows // 2, cols // 2
    pair_sum = Halver(slots)
    at = 0
    for number, count in enumerate(FINE_ROWS):
        fine[number, 8 - count : 8, :] = from_below[at : at + count, :]
        fine[number, 8:24, :] = own[number]
        fine[number, 24 : 24 + count, :] = from_above[at : at + count, :]
        at += count
    found = scaled_coefficients(
        fine[6], turn(fine[6], 1, 0), fine[7], fine[8], fine[9], FINE_STEP, FINE_COUPLING
    )
    w, q = steps_block(
        [fine[i] for i in range(3)], [FINE_STEP * fine[3 + i] for i in range(3)], found, 2
    )
    done[...] = f_ends[...]
    for i in range(3):
        done[i, 0:4, :] = w[i][8:12]
        done[i, 12:16, :] = w[i][20:24]
        done[3 + i, 0:4, :] = q[i][8:12] * (1.0 / FINE_STEP)
        done[3 + i, 12:16, :] = q[i][20:24] * (1.0 / FINE_STEP)
    copies = []
    for n, (ref, lead) in enumerate(((front, 0), (back, FRONT))):
        for end, start in enumerate((0, rows - 8)):
            copies.append(
                pltpu.make_async_copy(
                    done.at[lead : lead + ref.shape[0], 8 * end : 8 * end + 8],
                    ref.at[:, start : start + 8],
                    sems.at[2 * n + end],
                )
            )
    for copy in copies:
        copy.start()

    sums = [pair_sum(done, (i,), 0, 8) for i in range(6)]
    means = exact_dot(jnp.concatenate(sums, axis=0), averaging(cols))
    coarse[...] = jnp.ones_like(coarse)
    at = 0
    for number, count in enumerate(COARSE_ROWS):
        coarse[number, 8:16, :] = own_coarse[number]
        for k in range(count):
            line = FINE_TOTAL + at // 2
            place = (slice(line, line + 1), pl.ds((at % 2) * half_cols, half_cols))
            coarse[number, 8 - count + k : 9 - count + k, :] = from_below[place]
            coarse[number, 16 + k : 17 + k, :] = from_above[place]
            at += 1
    found = scaled_coefficients(
        coarse[6], turn(coarse[6], 1, 0), coarse[7], 4.0 * coarse[8], 4.0 * coarse[9],
        COARSE_STEP, COARSE_COUPLING,
    )
    for number in range(7):
        cc[number, 0:12, :] = found[number][0:12]
        cc[number, 12 : few + 8, :] = cc_in[number, 12 : few + 8, :]
        cc[number, few + 8 : few + 16, :] = found[number][16:24]
    w, q = steps_block(
        [coarse[i] for i in range(3)], [SPEED * coarse[3 + i] for i in range(3)], found, 1
    )
    moved = w + q
    b[...] = b_in[...]
    for i in range(6):
        scale = 1.0 if i < 3 else SPEED
        ends = scale * means[8 * i : 8 * i + 8, :]
        b[i, 0:2, :] = ends[0:2] - moved[i][8:10]
        b[i, few - 2 : few, :] = ends[6:8] - moved[i][14:16]
    for copy in copies:
        copy.wait()


def advance(ext, cc, repeats):
    return sum(
        steps_block(
            [ext[i] for i in range(3)],
            [ext[3 + i] for i in range(3)],
            [cc[number] for number in range(7)],
            repeats,
        ),
        [],
    )


def write_edges(message, to_above, to_below):
    few = (message.shape[0] - 24) // 6
    for i in range(6):
        own, beyond, at = i * few, 6 * few + 4 * i, 4 * i
        if i < 3:
            to_above[at : at + 3, :] = message[own + few - 3 : own + few, :]
            to_above[at + 3 : at + 4, :] = message[beyond + 1 : beyond + 2, :]
            to_below[at : at + 1, :] = message[beyond : beyond + 1, :]
            to_below[at + 1 : at + 4, :] = message[own : own + 3, :]
        else:
            to_above[at : at + 2, :] = message[own + few - 2 : own + few, :]
            to_above[at + 2 : at + 4, :] = message[beyond + 2 : beyond + 4, :]
            to_below[at : at + 2, :] = message[beyond : beyond + 2, :]
            to_below[at + 2 : at + 4, :] = message[own : own + 2, :]


def read_message(ext, message, below, above):
    few = ext.shape[1] - 16
    top = 8 + few
    for i in range(6):
        own, beyond, at = i * few, 6 * few + 4 * i, 4 * i
        ext[i, 8:top, :] = message[own : own + few, :]
        if i < 3:
            ext[i, 5:8, :] = below[at : at + 3, :]
            ext[i, 7:8, :] += message[beyond : beyond + 1, :]
            ext[i, 8:9, :] += below[at + 3 : at + 4, :]
            ext[i, top - 1 : top, :] += above[at : at + 1, :]
            ext[i, top : top + 3, :] = above[at + 1 : at + 4, :]
            ext[i, top : top + 1, :] += message[beyond + 1 : beyond + 2, :]
        else:
            ext[i, 6:8, :] = below[at : at + 2, :] + message[beyond : beyond + 2, :]
            ext[i, 8:10, :] += below[at + 2 : at + 4, :]
            ext[i, top - 2 : top, :] += above[at : at + 2, :]
            ext[i, top : top + 2, :] = (
                above[at + 2 : at + 4, :] + message[beyond + 2 : beyond + 4, :]
            )


def pair_body(b_even, b_odd, cc, message, to_above, to_below, ext):
    few = ext.shape[1] - 16
    top = 8 + few
    for i in range(6):
        ext[i, 0:8, :] = jnp.zeros_like(ext[i, 0:8, :])
        ext[i, 8:top, :] = b_even[i]
        ext[i, top : top + 8, :] = jnp.zeros_like(ext[i, 0:8, :])
    for i, value in enumerate(advance(ext, cc, 1)):
        own, beyond = i * few, 6 * few + 4 * i
        message[own : own + few, :] = value[8:top] + b_odd[i]
        if i < 3:
            message[beyond : beyond + 1, :] = value[7:8]
            message[beyond + 1 : beyond + 2, :] = value[top : top + 1]
            message[beyond + 2 : beyond + 4, :] = jnp.zeros_like(value[0:2])
        else:
            message[beyond : beyond + 2, :] = value[6:8]
            message[beyond + 2 : beyond + 4, :] = value[top : top + 2]
    write_edges(message, to_above, to_below)


def chain_body(message, below, above, source, cc, *refs):
    out, to_above, to_below, ext = refs[-4:]
    few = ext.shape[1] - 16
    ext[...] = jnp.zeros_like(ext)
    read_message(ext, message, below, above)
    for i, value in enumerate(advance(ext, cc, 2)):
        own = i * few
        out[own : own + few, :] = value[8 : 8 + few] + source[own : own + few, :]
    out[6 * few :, :] = source[6 * few :, :]
    write_edges(out, to_above, to_below)


def collect_body(rounds, *refs):
    messages, belows, aboves = [refs[k * rounds : (k + 1) * rounds] for k in range(3)]
    total, ext, message, below, above = refs[3 * rounds + 2 :]
    message[...] = sum(ref[...] for ref in messages)
    below[...] = sum(ref[...] for ref in belows)
    above[...] = sum(ref[...] for ref in aboves)
    ext[...] = jnp.zeros_like(ext)
    read_message(ext, message, below, above)
    for i in range(6):
        total[i] = ext[i, 8 : ext.shape[1] - 8, :]


def even_body(ext, b_even, cc, even_end):
    few = ext.shape[1] - 16
    for i, value in enumerate(advance(ext, cc, 1)):
        even_end[i] = value[8 : 8 + few] + b_even[i]


def second_body(front, back, after, out):
    @pl.when(lax.axis_index("cuts") == 1)
    def _():
        out[...] = front[...]

    @pl.when(lax.axis_index("cuts") != 1)
    def _():
        out[...] = back[...]


def third_body(back, after, out):
    out[...] = back[...]


def join_body(front, back, out, sems):
    low = pltpu.make_async_copy(front, out.at[0:FRONT], sems.at[0])
    high = pltpu.make_async_copy(back, out.at[FRONT:6], sems.at[1])
    low.start()
    high.start()
    low.wait()
    high.wait()


def spread_add(values, bases, outs, slots):
    cols = 2 * values.shape[1]
    wide = exact_dot(values, spreading(cols))
    few = wide.shape[0] // len(outs)
    for i, (base, out) in enumerate(zip(bases, outs)):
        for tile in range(cols // LANES):
            part = wide[i * few : (i + 1) * few, tile * LANES : (tile + 1) * LANES]
            slot = slots.at[i * (cols // LANES) + tile]
            slot[pl.ds(0, few, stride=2), :] = part
            slot[pl.ds(1, few, stride=2), :] = part
            at = (slice(None), pl.ds(tile * LANES, LANES))
            out[at] = base[at] + slot[...]


def remainder(parts, out, slots):
    pair_sum = Halver(slots)
    cols = out.shape[2]
    few = out.shape[1] // 2
    sums = [pair_sum(part, (), 0, few) for _, part in parts]
    means = exact_dot(jnp.concatenate(sums, axis=0), averaging(cols))
    spread_add(-means, [part for _, part in parts], [out.at[i] for i, _ in parts], slots)


def early_body(front, back, init, out, slots, sem):
    fields = [field_of(front, back, i) for i in range(6)]
    remainder([(i, ref.at[lead]) for i, (ref, lead) in enumerate(fields)], out, slots)

    @pl.when(lax.axis_index("cuts") == 0)
    def _():
        copy = pltpu.make_async_copy(init, out, sem)
        copy.start()
        copy.wait()


def late_body(base_in, front, back, base, slots, made, sems):
    place = lax.axis_index("cuts")
    for n, (lead, ref, found) in enumerate(
        ((0, front, place == 2), (FRONT, back, (place == 2) | (place == 4)))
    ):
        count = ref.shape[0]

        @pl.when(found)
        def _():
            remainder([(lead + i, ref.at[i]) for i in range(count)], made, slots)
            part = pl.ds(lead, count)
            copy = pltpu.make_async_copy(made.at[part], base.at[part], sems.at[n])
            copy.start()
            copy.wait()


def correct_body(base, own, received, out, slots, made, sems):
    odd = lax.axis_index("cuts") % 2
    copies = []
    for lead in (0, 3):
        values = []
        for i in range(lead, lead + 3):
            value = jnp.where(odd == 1, received[i], own[i])
            values.append(value if i < 3 else value * (1.0 / SPEED))
        part = [lead, lead + 1, lead + 2]
        spread_add(
            jnp.concatenate(values, axis=0),
            [base.at[i] for i in part],
            [made.at[i] for i in part],
            slots,
        )
        copies.append(
            pltpu.make_async_copy(
                made.at[pl.ds(lead, 3)], out.at[pl.ds(lead, 3)], sems.at[lead // 3]
            )
        )
        copies[-1].start()
    for copy in copies:
        copy.wait()


def per_device(start_state, initial_state, circ_stiff, axial_stiff, lumped_mass, hoop_stiff):
    u = start_state[0]
    strips, slices = lax.axis_size("strip"), lax.axis_size("cuts")
    chips = slices // 2
    _, rows, cols = u.shape
    few, half_cols = rows // 2, cols // 2
    state, coarse_state = (6, rows, cols), (6, few, half_cols)
    ext_state = (6, few + 16, half_cols)
    edge = (6 * EDGE, half_cols)
    fields = (circ_stiff, axial_stiff, lumped_mass, hoop_stiff)

    def around_loop(value, by):
        pairs = [(s, (s + by) % strips) for s in range(strips)]
        return lax.ppermute(value, "strip", pairs)

    def send(value, by, moves):
        pairs = [
            (s * slices + source, (s + by) % strips * slices + target)
            for s in range(strips)
            for source, target in moves
        ]
        return lax.ppermute(value, ("strip", "cuts"), pairs)

    def send_with_edges(main, to_above, to_below, moves):
        return (
            send(main, 0, moves),
            send(to_above, 1, moves),
            send(to_below, -1, moves),
        )

    pack = (PACK_ROWS, cols)
    half_state = (3, rows, cols)
    front_state, back_state = (FRONT, rows, cols), (6 - FRONT, rows, cols)
    ends = (6, 16, cols)
    message = (6 * few + 24, half_cols)
    cc_shape = (7, few + 16, half_cols)
    to_above, to_below, own, own_coarse, u_near, *near = run(
        pack_body,
        "pack",
        [pack, pack, (10, 16, cols), (10, 8, half_cols), state] + [(rows, cols)] * 4,
        [u, initial_state, *fields],
        [
            pltpu.VMEM(ends, F32),
            halver_scratch(16, 16, cols),
            pltpu.SemaphoreType.DMA((7,)),
        ],
        specs=[HBM] * 6,
    )
    from_below = around_loop(to_above, 1)
    from_above = around_loop(to_below, -1)
    front, back, b, cc, f_ends = run(
        interior_body,
        "interior",
        [front_state, back_state, coarse_state, cc_shape, ends],
        [u_near, initial_state, *near],
        [
            pltpu.VMEM((7, rows, cols), F32),
            pltpu.VMEM(half_state, F32),
            pltpu.VMEM(half_state, F32),
            pltpu.VMEM((10 * few, cols), F32),
            pltpu.VMEM(state, F32),
            halver_scratch(22, rows, cols),
            pltpu.SemaphoreType.DMA,
        ],
        specs=[VMEM, HBM] + [VMEM] * 4,
    )
    front, back, b, cc = run(
        edges_body,
        "edges",
        [front_state, back_state, coarse_state, cc_shape],
        [front, back, f_ends, own, own_coarse, b, cc, from_below, from_above],
        [
            pltpu.VMEM((10, 32, cols), F32),
            pltpu.VMEM((10, 24, half_cols), F32),
            pltpu.VMEM(ends, F32),
            halver_scratch(6, 16, cols),
            pltpu.SemaphoreType.DMA((4,)),
        ],
        specs=[ANY] * 2 + [VMEM] * 7,
        out_specs=[ANY] * 2 + [VMEM] * 2,
        aliases={0: 0, 1: 1},
    )
    ext = [pltpu.VMEM(ext_state, F32)]
    inside = [(2 * z, 2 * z + 1) for z in range(chips)]
    swap = inside + [(odd, even) for even, odd in inside]
    b_other = send(b, 0, swap)
    source = run(pair_body, "pair", [message, edge, edge], [b, b_other, cc], ext)

    def hops(links):
        return [(2 * z + 1, 2 * z + 2) for z in links if 0 <= z < chips - 1]

    sent_first = send(front, 0, inside + hops(range(1, chips)))
    at_end = source
    arrived = []
    for chip in range(chips - 1):
        arrived.append(send_with_edges(*at_end, [(2 * chip, 2 * chip + 2)]))
        if chip < chips - 2:
            extra = [sent_first] * (chip == 1)
            at_end = run(
                chain_body,
                "chain",
                [message, edge, edge],
                [*arrived[-1], source[0], cc] + extra,
                ext,
                specs=[VMEM] * 5 + [ANY] * len(extra),
            )
        if chip == 0:
            (part,) = run(
                second_body, "second", [back_state], [front, back, at_end[1]],
                specs=[VMEM, VMEM, ANY],
            )
            sent_second = send(part, 0, inside + hops([0, *range(2, chips)]))
        if chip == 1:
            (part,) = run(
                third_body, "third", [back_state], [back, at_end[1]], specs=[VMEM, ANY]
            )
            sent_third = send(part, 0, hops([0, 1]))
    messages, belows, aboves = zip(*arrived)
    (fine_end,) = run(
        join_body,
        "join",
        [state],
        [front, back],
        [pltpu.SemaphoreType.DMA((2,))],
        specs=[ANY] * 2,
        out_specs=[ANY],
        cost=(0, 6 * rows * cols * 8),
    )
    rem_scratch = [
        halver_scratch(6, rows, cols),
        pltpu.VMEM(state, F32),
        pltpu.SemaphoreType.DMA((2,)),
    ]
    (base,) = run(
        early_body,
        "remainder",
        [state],
        [sent_first, sent_second, initial_state],
        [halver_scratch(6, rows, cols), pltpu.SemaphoreType.DMA],
        specs=[VMEM, VMEM, HBM],
        cost=(0, 6 * rows * cols * 8),
    )
    total, wide = run(
        lambda *refs: collect_body(chips - 1, *refs),
        "collect",
        [coarse_state, ext_state],
        [*messages, *belows, *aboves, base, fine_end],
        [pltpu.VMEM(message, F32), pltpu.VMEM(edge, F32), pltpu.VMEM(edge, F32)],
        specs=[VMEM] * (3 * len(messages)) + [ANY, HBM],
    )
    (even_end,) = run(even_body, "even", [coarse_state], [wide, b, cc])
    received = send(even_end, 0, swap)
    (base,) = run(
        late_body,
        "late",
        [state],
        [base, sent_second, sent_third],
        rem_scratch,
        specs=[ANY, VMEM, VMEM],
        out_specs=[ANY],
        aliases={0: 0},
    )
    (new_start,) = run(
        correct_body,
        "correct",
        [state],
        [base, total, received],
        rem_scratch,
        out_specs=[HBM],
    )
    return new_start[None], fine_end[None]


def solution(mesh):
    state = P("cuts", None, "strip", None)
    field = P("strip", None)
    return jax.shard_map(
        per_device,
        mesh=mesh,
        in_specs=(state, P(None, "strip", None), field, field, field, field),
        out_specs=(state, state),
        check_vma=False,
    )
```

time: 75.1 us -> 53 us (0.71)
  the two profiles are of different devices: /device:TPU:25 before, /device:TPU:16 now
where the time goes in v2:
time: 53 us; the launch traced here: 52.7 us
  starting transfers between devices  19.1 us (36%)
  waiting for transfers between devices  17.5 us (33%)
  Pallas kernels  15.1 us (28%)
  between operations  0.92 us (2%)
    ppermute x14, waiting for transfers between devices, send(): return lax.ppermute(value, ('strip', 'cuts'), pairs)  17.5 us
    ppermute x14, starting transfers between devices, send(): return lax.ppermute(value, ('strip', 'cuts'), pairs)  16.2 us
    pallas_call x14, Pallas kernels, run(): pl.pallas_call(body, name=name, out_shape=[jax.ShapeDtypeStruct(shape, F3...  15.1 us
    ppermute x2, starting transfers between devices, around_loop(): return lax.ppermute(value, 'strip', pairs)  2.98 us
  transfers between devices with their start and end apart: 16, of which 5 were waited for; matrix products, arithmetic and copies ran while one was open for 0% of the time, Pallas kernels for 19%

profile of v2, /device:TPU:16, one launch (start us, length us, event | category | flops | bytes accessed | tf_op | source)
XLA Modules:
  0.0 52.7 jit_solution(5015622094933179337)
XLA Ops:
  0.6 2.1 %pack.1 = (f32[40,512]{1,0:T(8,128)S(1)}, f32[40,512]{1,0:T(8,128)S(1)}, f32[10,16,512]{2,1,0:T(8,128)S(1)}, f32[10,8,256]{2,1,0:T(8,128)S(1)}, f32[6,128,512]{2...) custom-call(f32[6,128,512]{2,1,0:T(8,128)} %bitcast.4, ...), custom_call_target="tpu_custom_call" | custom-call | tf_op jit(solution)/shard_map/pack/pallas_call | solution.py:34
  2.8 1.5 %collective-permute-start = (f32[40,512]{1,0:T(8,128)S(1)}, f32[40,512]{1,0:T(8,128)S(1)}, u32[]{:S(2)}, u32[]{:S(2)}) collective-permute-start(f32[40,512]{1,0:T(8,128)S(1)} %get-tuple-element.43), channel_id=1, source_target_pairs={{0,8},{8,16},{16,24},{24,0},{1,9},{9,17},{17,25},{25,1},{2,10},{10... | collective-permute-start | bytes 245768 | tf_op jit(solution)/shard_map/ppermute | solution.py:595
  4.3 1.4 %collective-permute-start.1 = (f32[40,512]{1,0:T(8,128)S(1)}, f32[40,512]{1,0:T(8,128)S(1)}, u32[]{:S(2)}, u32[]{:S(2)}) collective-permute-start(f32[40,512]{1,0:T(8,128)S(1)} %get-tuple-element.44), channel_id=1, source_target_pairs={{0,24},{8,0},{16,8},{24,16},{1,25},{9,1},{17,9},{25,17},{2,26},{10... | collective-permute-start | bytes 245768 | tf_op jit(solution)/shard_map/ppermute | solution.py:595
  5.8 4.2 %interior.1 = (f32[3,128,512]{2,1,0:T(8,128)S(1)}, f32[3,128,512]{2,1,0:T(8,128)S(1)}, f32[6,64,256]{2,1,0:T(8,128)S(1)}, f32[7,80,256]{2,1,0:T(8,128)S(1)}, f32[6,16,512]{2,1,0:T(8,128)S(1)}) custom-call(f32[6,128,512]{2,1,0:T(8,128)S(1)} %get-tuple-element.31.u, f32[6,128,512]{2,1,0:T(8,128)} %init.5, f32[128,512]{1,0:T(8,128)S(1)} %get-tuple-element.32.kc, ...), custom_call_target="tpu_custom_call" | custom-call | tf_op jit(solution)/shard_map/interior/pallas_call | solution.py:34
  10.0 0.0 collective-permute-done.from_below
  10.0 0.0 collective-permute-done.1.from_above
  10.0 0.9 %edges.1 = (f32[3,128,512]{2,1,0:T(8,128)S(1)}, f32[3,128,512]{2,1,0:T(8,128)S(1)}, f32[6,64,256]{2,1,0:T(8,128)S(1)}, f32[7,80,256]{2,1,0:T(8,128)S(1)}) custom-call(f32[3,128,512]{2,1,0:T(8,128)S(1)} %get-tuple-element.36.front_in, f32[3,128,512]{2,1,0:T(8,128)S(1)} %get-tuple-element.37.back_in, ...), custom_call_target="tpu_custom_call", output_to_operand_aliasing={{0}: (0, {}), {1}: (1, {})} | custom-call | tf_op jit(solution)/shard_map/edges/pallas_call | solution.py:34
  11.0 0.1 collective-permute-start.3
  11.0 1.7 %collective-permute-done.3.b_odd = f32[6,64,256]{2,1,0:T(8,128)S(1)} collective-permute-done((f32[6,64,256]{2,1,0:T(8,128)S(1)}, f32[6,64,256]{2,1,0:T(8,128)S(1)}, u32[]{:S(2)}, u32[]{:S(2)}) %collective-permute-start.3) | collective-permute-done | bytes 393248 | tf_op jit(solution)/shard_map/ppermute | solution.py:603
  12.8 0.5 pair.1
  13.3 0.7 %collective-permute-start.4 = (f32[408,256]{1,0:T(8,128)S(1)}, f32[408,256]{1,0:T(8,128)S(1)}, u32[]{:S(2)}, u32[]{:S(2)}) collective-permute-start(f32[408,256]{1,0:T(8,128)S(1)} %get-tuple-element.49.source), channel_id=1, source_target_pairs={{0,2},{8,10},{16,18},{24,26}} | collective-permute-start | bytes 1253384 | tf_op jit(solution)/shard_map/ppermute | solution.py:603
  14.0 2.0 %collective-permute-start.2 = (f32[3,128,512]{2,1,0:T(8,128)S(1)}, f32[3,128,512]{2,1,0:T(8,128)S(1)}, u32[]{:S(2)}, u32[]{:S(2)}) collective-permute-start(f32[3,128,512]{2,1,0:T(8,128)S(1)} %get-tuple-element.45.front), channel_id=1, source_target_pairs={{0,1},{2,3},{4,5},{6,7},{3,4},{5,6},{8,9},{10,11},{12,13},{14,15},... | collective-permute-start | bytes 2359304 | tf_op jit(solution)/shard_map/ppermute | solution.py:603
  16.0 0.7 %collective-permute-start.5 = (f32[24,256]{1,0:T(8,128)S(1)}, f32[24,256]{1,0:T(8,128)S(1)}, u32[]{:S(2)}, u32[]{:S(2)}) collective-permute-start(f32[24,256]{1,0:T(8,128)S(1)} %get-tuple-element.50), channel_id=1, source_target_pairs={{0,10},{8,18},{16,26},{24,2}} | collective-permute-start | bytes 73736 | tf_op jit(solution)/shard_map/ppermute | solution.py:603
  16.7 0.7 %collective-permute-start.6 = (f32[24,256]{1,0:T(8,128)S(1)}, f32[24,256]{1,0:T(8,128)S(1)}, u32[]{:S(2)}, u32[]{:S(2)}) collective-permute-start(f32[24,256]{1,0:T(8,128)S(1)} %get-tuple-element.51), channel_id=1, source_target_pairs={{0,26},{8,2},{16,10},{24,18}} | collective-permute-start | bytes 73736 | tf_op jit(solution)/shard_map/ppermute | solution.py:603
  17.3 0.0 collective-permute-done.5.below.refs_3_
  17.4 0.0 collective-permute-done.6.above.refs_6_
  17.4 0.0 collective-permute-done.4.message.refs_0_
  17.4 0.7 %chain.2 = (f32[408,256]{1,0:T(8,128)S(1)}, f32[24,256]{1,0:T(8,128)S(1)}, f32[24,256]{1,0:T(8,128)S(1)}) custom-call(f32[408,256]{1,0:T(8,128)S(1)} %collective-permute-done.4.message.refs_0_, f32[24,256]{1,0:T(8,128)S(1)} %collective-permute-done.5.below.refs_3_, f32[24,256]{1,0:T(8,128)S(1)} %collective-permute-done.6.above.refs_6_, ...), custom_call_target="tpu_custom_call" | custom-call | tf_op jit(solution)/shard_map/chain/pallas_call | solution.py:34
  18.1 1.3 %collective-permute-start.8 = (f32[408,256]{1,0:T(8,128)S(1)}, f32[408,256]{1,0:T(8,128)S(1)}, u32[]{:S(2)}, u32[]{:S(2)}) collective-permute-start(f32[408,256]{1,0:T(8,128)S(1)} %get-tuple-element.53), channel_id=1, source_target_pairs={{2,4},{10,12},{18,20},{26,28}} | collective-permute-start | bytes 1253384 | tf_op jit(solution)/shard_map/ppermute | solution.py:603
  19.4 0.1 second.1
  19.4 2.9 %collective-permute-start.7 = (f32[3,128,512]{2,1,0:T(8,128)S(1)}, f32[3,128,512]{2,1,0:T(8,128)S(1)}, u32[]{:S(2)}, u32[]{:S(2)}) collective-permute-start(f32[3,128,512]{2,1,0:T(8,128)S(1)} %second.1), channel_id=1, source_target_pairs={{0,1},{2,3},{4,5},{6,7},{1,2},{5,6},{8,9},{10,11},{12,13},{14,15},... | collective-permute-start | bytes 2359304 | tf_op jit(solution)/shard_map/ppermute | solution.py:603
  22.4 1.3 %collective-permute-start.9 = (f32[24,256]{1,0:T(8,128)S(1)}, f32[24,256]{1,0:T(8,128)S(1)}, u32[]{:S(2)}, u32[]{:S(2)}) collective-permute-start(f32[24,256]{1,0:T(8,128)S(1)} %get-tuple-element.52.after), channel_id=1, source_target_pairs={{2,12},{10,20},{18,28},{26,4}} | collective-permute-start | bytes 73736 | tf_op jit(solution)/shard_map/ppermute | solution.py:603
  23.7 1.3 %collective-permute-start.10 = (f32[24,256]{1,0:T(8,128)S(1)}, f32[24,256]{1,0:T(8,128)S(1)}, u32[]{:S(2)}, u32[]{:S(2)}) collective-permute-start(f32[24,256]{1,0:T(8,128)S(1)} %get-tuple-element.54), channel_id=1, source_target_pairs={{2,28},{10,4},{18,12},{26,20}} | collective-permute-start | bytes 73736 | tf_op jit(solution)/shard_map/ppermute | solution.py:603
  25.0 2.3 %collective-permute-done.2.front.refs_0_ = f32[3,128,512]{2,1,0:T(8,128)S(1)} collective-permute-done((f32[3,128,512]{2,1,0:T(8,128)S(1)}, f32[3,128,512]{2,1,0:T(8,128)S(1)}, u32[]{:S(2)}, u32[]{:S(2)}) %collective-permute-start.2) | collective-permute-done | bytes 786464 | tf_op jit(solution)/shard_map/ppermute | solution.py:603
  27.3 7.3 %collective-permute-done.9.below.refs_4_ = f32[24,256]{1,0:T(8,128)S(1)} collective-permute-done((f32[24,256]{1,0:T(8,128)S(1)}, f32[24,256]{1,0:T(8,128)S(1)}, u32[]{:S(2)}, u32[]{:S(2)}) %collective-permute-start.9) | collective-permute-done | bytes 24608 | tf_op jit(solution)/shard_map/ppermute | solution.py:603
  34.5 0.2 collective-permute-done.10.above.refs_7_
  34.7 0.0 collective-permute-done.8.message.refs_1_
  34.7 0.7 %chain.3 = (f32[408,256]{1,0:T(8,128)S(1)}, f32[24,256]{1,0:T(8,128)S(1)}, f32[24,256]{1,0:T(8,128)S(1)}) custom-call(f32[408,256]{1,0:T(8,128)S(1)} %collective-permute-done.8.message.refs_1_, f32[24,256]{1,0:T(8,128)S(1)} %collective-permute-done.9.below.refs_4_, f32[24,256]{1,0:T(8,128)S(1)} %collective-permute-done.10.above.refs_7_, ...), custom_call_target="tpu_custom_call" | custom-call | tf_op jit(solution)/shard_map/chain/pallas_call | solution.py:34
  35.4 1.3 %collective-permute-start.12 = (f32[408,256]{1,0:T(8,128)S(1)}, f32[408,256]{1,0:T(8,128)S(1)}, u32[]{:S(2)}, u32[]{:S(2)}) collective-permute-start(f32[408,256]{1,0:T(8,128)S(1)} %get-tuple-element.56), channel_id=1, source_target_pairs={{4,6},{12,14},{20,22},{28,30}} | collective-permute-start | bytes 1253384 | tf_op jit(solution)/shard_map/ppermute | solution.py:603
  36.7 0.1 third.1
  36.8 1.3 %collective-permute-start.11 = (f32[3,128,512]{2,1,0:T(8,128)S(1)}, f32[3,128,512]{2,1,0:T(8,128)S(1)}, u32[]{:S(2)}, u32[]{:S(2)}) collective-permute-start(f32[3,128,512]{2,1,0:T(8,128)S(1)} %third.1), channel_id=1, source_target_pairs={{1,2},{3,4},{9,10},{11,12},{17,18},{19,20},{25,26},{27,28}} | collective-permute-start | bytes 2359304 | tf_op jit(solution)/shard_map/ppermute | solution.py:603
  38.1 1.3 %collective-permute-start.13 = (f32[24,256]{1,0:T(8,128)S(1)}, f32[24,256]{1,0:T(8,128)S(1)}, u32[]{:S(2)}, u32[]{:S(2)}) collective-permute-start(f32[24,256]{1,0:T(8,128)S(1)} %get-tuple-element.55.after), channel_id=1, source_target_pairs={{4,14},{12,22},{20,30},{28,6}} | collective-permute-start | bytes 73736 | tf_op jit(solution)/shard_map/ppermute | solution.py:603
  39.4 1.3 %collective-permute-start.14 = (f32[24,256]{1,0:T(8,128)S(1)}, f32[24,256]{1,0:T(8,128)S(1)}, u32[]{:S(2)}, u32[]{:S(2)}) collective-permute-start(f32[24,256]{1,0:T(8,128)S(1)} %get-tuple-element.57), channel_id=1, source_target_pairs={{4,30},{12,6},{20,14},{28,22}} | collective-permute-start | bytes 73736 | tf_op jit(solution)/shard_map/ppermute | solution.py:603
  40.7 1.2 %join.1.refs_10_ = f32[6,128,512]{2,1,0:T(8,128)} custom-call(f32[3,128,512]{2,1,0:T(8,128)S(1)} %get-tuple-element.45.front, f32[3,128,512]{2,1,0:T(8,128)S(1)} %get-tuple-element.46.back), custom_call_target="tpu_custom_call" | custom-call | bytes 3145728 | tf_op jit(solution)/shard_map/join/pallas_call | solution.py:34
  41.9 0.0 collective-permute-done.7.back.front
  41.9 1.6 %remainder.1.base_in.refs_9_ = f32[6,128,512]{2,1,0:T(8,128)S(1)} custom-call(f32[3,128,512]{2,1,0:T(8,128)S(1)} %collective-permute-done.2.front.refs_0_, f32[3,128,512]{2,1,0:T(8,128)S(1)} %collective-permute-done.7.back.front, f32[6,128,512]{2,1,0:T(8,128)} %init.5), custom_call_target="tpu_custom_call" | custom-call | bytes 3145728 | tf_op jit(solution)/shard_map/remainder/pallas_call | solution.py:34
  43.4 0.0 collective-permute-done.13.refs_5_
  43.5 0.0 collective-permute-done.14.refs_8_
  43.5 0.0 collective-permute-done.12.refs_2_
  43.5 0.1 collect.1
  43.6 0.4 even.1
  44.1 0.1 collective-permute-start.15
  44.1 6.0 %collective-permute-done.11.back = f32[3,128,512]{2,1,0:T(8,128)S(1)} collective-permute-done((f32[3,128,512]{2,1,0:T(8,128)S(1)}, f32[3,128,512]{2,1,0:T(8,128)S(1)}, u32[]{:S(2)}, u32[]{:S(2)}) %collective-permute-start.11) | collective-permute-done | bytes 786464 | tf_op jit(solution)/shard_map/ppermute | solution.py:603
  50.1 1.0 %late.1.base = f32[6,128,512]{2,1,0:T(8,128)S(1)} custom-call(f32[6,128,512]{2,1,0:T(8,128)S(1)} %remainder.1.base_in.refs_9_, f32[3,128,512]{2,1,0:T(8,128)S(1)} %collective-permute-done.7.back.front, f32[3,128,512]{2,1,0:T(8,128)S(1)} %collective-permute-done.11.back), custom_call_target="tpu_custom_call", output_to_operand_aliasing={{}: (0, {})} | custom-call | tf_op jit(solution)/shard_map/late/pallas_call | solution.py:34
  51.1 0.0 collective-permute-done.15.received
  51.1 1.6 %correct.1 = f32[6,128,512]{2,1,0:T(8,128)} custom-call(f32[6,128,512]{2,1,0:T(8,128)S(1)} %late.1.base, f32[6,64,256]{2,1,0:T(8,128)S(1)} %get-tuple-element.58.own, f32[6,64,256]{2,1,0:T(8,128)S(1)} %collective-permute-done.15.received), custom_call_target="tpu_custom_call" | custom-call | tf_op jit(solution)/shard_map/correct/pallas_call | solution.py:34
Async XLA Ops:
  2.8 7.2 %collective-permute-start = (f32[40,512]{1,0:T(8,128)S(1)}, f32[40,512]{1,0:T(8,128)S(1)}, u32[]{:S(2)}, u32[]{:S(2)}) collective-permute-start(f32[40,512]{1,0:T(8,128)S(1)} %get-tuple-element.43), channel_id=1, source_target_pairs={{0,8},{8,16},{16,24},{24,0},{1,9},{9,17},{17,25},{25,1},{2,10},{10... | collective-permute-start | bytes 245768 | tf_op jit(solution)/shard_map/ppermute | solution.py:595
  4.3 5.7 %collective-permute-start.1 = (f32[40,512]{1,0:T(8,128)S(1)}, f32[40,512]{1,0:T(8,128)S(1)}, u32[]{:S(2)}, u32[]{:S(2)}) collective-permute-start(f32[40,512]{1,0:T(8,128)S(1)} %get-tuple-element.44), channel_id=1, source_target_pairs={{0,24},{8,0},{16,8},{24,16},{1,25},{9,1},{17,9},{25,17},{2,26},{10... | collective-permute-start | bytes 245768 | tf_op jit(solution)/shard_map/ppermute | solution.py:595
  11.0 1.8 %collective-permute-start.3 = (f32[6,64,256]{2,1,0:T(8,128)S(1)}, f32[6,64,256]{2,1,0:T(8,128)S(1)}, u32[]{:S(2)}, u32[]{:S(2)}) collective-permute-start(f32[6,64,256]{2,1,0:T(8,128)S(1)} %get-tuple-element.47.b_even), channel_id=1, source_target_pairs={{0,1},{2,3},{4,5},{6,7},{1,0},{3,2},{5,4},{7,6},{8,9},{10,11},{12,... | collective-permute-start | bytes 1179656 | tf_op jit(solution)/shard_map/ppermute | solution.py:603
  13.3 4.1 %collective-permute-start.4 = (f32[408,256]{1,0:T(8,128)S(1)}, f32[408,256]{1,0:T(8,128)S(1)}, u32[]{:S(2)}, u32[]{:S(2)}) collective-permute-start(f32[408,256]{1,0:T(8,128)S(1)} %get-tuple-element.49.source), channel_id=1, source_target_pairs={{0,2},{8,10},{16,18},{24,26}} | collective-permute-start | bytes 1253384 | tf_op jit(solution)/shard_map/ppermute | solution.py:603
  14.0 13.3 %collective-permute-start.2 = (f32[3,128,512]{2,1,0:T(8,128)S(1)}, f32[3,128,512]{2,1,0:T(8,128)S(1)}, u32[]{:S(2)}, u32[]{:S(2)}) collective-permute-start(f32[3,128,512]{2,1,0:T(8,128)S(1)} %get-tuple-element.45.front), channel_id=1, source_target_pairs={{0,1},{2,3},{4,5},{6,7},{3,4},{5,6},{8,9},{10,11},{12,13},{14,15},... | collective-permute-start | bytes 2359304 | tf_op jit(solution)/shard_map/ppermute | solution.py:603
  16.0 1.3 %collective-permute-start.5 = (f32[24,256]{1,0:T(8,128)S(1)}, f32[24,256]{1,0:T(8,128)S(1)}, u32[]{:S(2)}, u32[]{:S(2)}) collective-permute-start(f32[24,256]{1,0:T(8,128)S(1)} %get-tuple-element.50), channel_id=1, source_target_pairs={{0,10},{8,18},{16,26},{24,2}} | collective-permute-start | bytes 73736 | tf_op jit(solution)/shard_map/ppermute | solution.py:603
  16.7 0.7 %collective-permute-start.6 = (f32[24,256]{1,0:T(8,128)S(1)}, f32[24,256]{1,0:T(8,128)S(1)}, u32[]{:S(2)}, u32[]{:S(2)}) collective-permute-start(f32[24,256]{1,0:T(8,128)S(1)} %get-tuple-element.51), channel_id=1, source_target_pairs={{0,26},{8,2},{16,10},{24,18}} | collective-permute-start | bytes 73736 | tf_op jit(solution)/shard_map/ppermute | solution.py:603
  18.1 16.7 %collective-permute-start.8 = (f32[408,256]{1,0:T(8,128)S(1)}, f32[408,256]{1,0:T(8,128)S(1)}, u32[]{:S(2)}, u32[]{:S(2)}) collective-permute-start(f32[408,256]{1,0:T(8,128)S(1)} %get-tuple-element.53), channel_id=1, source_target_pairs={{2,4},{10,12},{18,20},{26,28}} | collective-permute-start | bytes 1253384 | tf_op jit(solution)/shard_map/ppermute | solution.py:603
  19.4 22.4 %collective-permute-start.7 = (f32[3,128,512]{2,1,0:T(8,128)S(1)}, f32[3,128,512]{2,1,0:T(8,128)S(1)}, u32[]{:S(2)}, u32[]{:S(2)}) collective-permute-start(f32[3,128,512]{2,1,0:T(8,128)S(1)} %second.1), channel_id=1, source_target_pairs={{0,1},{2,3},{4,5},{6,7},{1,2},{5,6},{8,9},{10,11},{12,13},{14,15},... | collective-permute-start | bytes 2359304 | tf_op jit(solution)/shard_map/ppermute | solution.py:603
  22.4 12.2 %collective-permute-start.9 = (f32[24,256]{1,0:T(8,128)S(1)}, f32[24,256]{1,0:T(8,128)S(1)}, u32[]{:S(2)}, u32[]{:S(2)}) collective-permute-start(f32[24,256]{1,0:T(8,128)S(1)} %get-tuple-element.52.after), channel_id=1, source_target_pairs={{2,12},{10,20},{18,28},{26,4}} | collective-permute-start | bytes 73736 | tf_op jit(solution)/shard_map/ppermute | solution.py:603
  23.7 11.1 %collective-permute-start.10 = (f32[24,256]{1,0:T(8,128)S(1)}, f32[24,256]{1,0:T(8,128)S(1)}, u32[]{:S(2)}, u32[]{:S(2)}) collective-permute-start(f32[24,256]{1,0:T(8,128)S(1)} %get-tuple-element.54), channel_id=1, source_target_pairs={{2,28},{10,4},{18,12},{26,20}} | collective-permute-start | bytes 73736 | tf_op jit(solution)/shard_map/ppermute | solution.py:603
  35.4 8.0 %collective-permute-start.12 = (f32[408,256]{1,0:T(8,128)S(1)}, f32[408,256]{1,0:T(8,128)S(1)}, u32[]{:S(2)}, u32[]{:S(2)}) collective-permute-start(f32[408,256]{1,0:T(8,128)S(1)} %get-tuple-element.56), channel_id=1, source_target_pairs={{4,6},{12,14},{20,22},{28,30}} | collective-permute-start | bytes 1253384 | tf_op jit(solution)/shard_map/ppermute | solution.py:603
  36.8 13.3 %collective-permute-start.11 = (f32[3,128,512]{2,1,0:T(8,128)S(1)}, f32[3,128,512]{2,1,0:T(8,128)S(1)}, u32[]{:S(2)}, u32[]{:S(2)}) collective-permute-start(f32[3,128,512]{2,1,0:T(8,128)S(1)} %third.1), channel_id=1, source_target_pairs={{1,2},{3,4},{9,10},{11,12},{17,18},{19,20},{25,26},{27,28}} | collective-permute-start | bytes 2359304 | tf_op jit(solution)/shard_map/ppermute | solution.py:603
  38.1 5.3 %collective-permute-start.13 = (f32[24,256]{1,0:T(8,128)S(1)}, f32[24,256]{1,0:T(8,128)S(1)}, u32[]{:S(2)}, u32[]{:S(2)}) collective-permute-start(f32[24,256]{1,0:T(8,128)S(1)} %get-tuple-element.55.after), channel_id=1, source_target_pairs={{4,14},{12,22},{20,30},{28,6}} | collective-permute-start | bytes 73736 | tf_op jit(solution)/shard_map/ppermute | solution.py:603
  39.4 4.0 %collective-permute-start.14 = (f32[24,256]{1,0:T(8,128)S(1)}, f32[24,256]{1,0:T(8,128)S(1)}, u32[]{:S(2)}, u32[]{:S(2)}) collective-permute-start(f32[24,256]{1,0:T(8,128)S(1)} %get-tuple-element.57), channel_id=1, source_target_pairs={{4,30},{12,6},{20,14},{28,22}} | collective-permute-start | bytes 73736 | tf_op jit(solution)/shard_map/ppermute | solution.py:603
  44.1 7.1 %collective-permute-start.15 = (f32[6,64,256]{2,1,0:T(8,128)S(1)}, f32[6,64,256]{2,1,0:T(8,128)S(1)}, u32[]{:S(2)}, u32[]{:S(2)}) collective-permute-start(f32[6,64,256]{2,1,0:T(8,128)S(1)} %even.1), channel_id=1, source_target_pairs={{0,1},{2,3},{4,5},{6,7},{1,0},{3,2},{5,4},{7,6},{8,9},{10,11},{12,... | collective-permute-start | bytes 1179656 | tf_op jit(solution)/shard_map/ppermute | solution.py:603

commit v3 on v2

--- a/solution.py
+++ b/solution.py
@@ -15,9 +15,9 @@
 COARSE_ROWS = (2, 2, 2, 1, 1, 1, 3, 2, 2, 2)
 FINE_TOTAL = sum(FINE_ROWS)
 PACK_ROWS = -(-(FINE_TOTAL + -(-sum(COARSE_ROWS) // 2)) // 8) * 8
-CHUNK = 8
+CHUNK = 16
+MARGIN = 8
 EDGE = 4
-FRONT = 3
 
 VMEM = pl.BlockSpec(memory_space=pltpu.VMEM)
 ANY = pl.BlockSpec(memory_space=pl.ANY)
@@ -136,6 +136,7 @@
     def __call__(self, source, lead, start, count):
         pieces = []
         for at in range(0, source.shape[-1], LANES):
+            assert self.used < self.ref.shape[0] and 2 * count <= self.ref.shape[1]
             slot = self.ref.at[self.used]
             self.used += 1
             slot[0 : 2 * count, :] = source[
@@ -151,17 +152,13 @@
     return pltpu.VMEM((fields * (cols // LANES), rows, LANES), F32)
 
 
-def field_of(front, back, i):
-    return (front, i) if i < FRONT else (back, i - FRONT)
-
-
 def is_first():
     return (lax.axis_index("cuts") == 0).astype(F32)
 
 
 def pack_body(
     u_far, init, kc_far, ka_far, mass_far, hoop_far,
-    to_above, to_below, own, own_coarse, u, kc, ka, mass, hoop, early, slots, sems,
+    to_above, to_below, own, own_coarse, u, kc, ka, mass, hoop, middle, early, slots, sems,
 ):
     rows, cols = kc.shape
     pair_sum = Halver(slots)
@@ -209,15 +206,59 @@
             to_above[place] = means[low : low + 1]
             to_below[place] = means[high : high + 1]
             at += 1
+    lead = rows // 4 - MARGIN
+    middle[...] = u[:, lead : rows - lead, :]
+
+
+def propagate(u, coefficients, w1, half, f):
+    rows = u.shape[1]
+    chunk = CHUNK if rows % CHUNK == 0 else 8
+    starts = range(0, rows, chunk)
+
+    def around(ref, start):
+        found = []
+        for i in range(3):
+            now = ref[i, start : start + chunk, :]
+            if start + chunk < rows:
+                above = ref[i, start + 1 : start + chunk + 1, :]
+            else:
+                above = turn(now, -1, 0)
+            if start > 0:
+                below = ref[i, start - 1 : start + chunk - 1, :]
+            else:
+                below = turn(now, 1, 0)
+            found.append((now, above, below))
+        return zip(*found)
+
+    for start in starts:
+        at = pl.ds(start, chunk)
+        now, above, below = around(u, start)
+        acc = accelerate(now, above, below, coefficients(start, chunk, True))
+        for i in range(3):
+            moved = FINE_STEP * u[3 + i, at, :] + 0.5 * acc[i]
+            half[i, at, :] = moved
+            w1[i, at, :] = now[i] + moved
+    for start in starts:
+        at = pl.ds(start, chunk)
+        now, above, below = around(w1, start)
+        acc = accelerate(now, above, below, coefficients(start, chunk, False))
+        for i in range(3):
+            moved = half[i, at, :] + acc[i]
+            half[i, at, :] = moved
+            f[i, at, :] = now[i] + moved
+    for start in starts:
+        at = pl.ds(start, chunk)
+        now, above, below = around(f, start)
+        acc = accelerate(now, above, below, coefficients(start, chunk, False))
+        for i in range(3):
+            f[3 + i, at, :] = (half[i, at, :] + 0.5 * acc[i]) * (1.0 / FINE_STEP)
 
 
 def interior_body(
-    u, init, kc, ka, mass, hoop, front, back, b, cc, f_ends,
-    cf, w1, half, sums, late, slots, sem,
+    u, init, kc, ka, mass, hoop, f, b, cc, cf, w1, half, sums, late, slots, sem
 ):
     pair_sum = Halver(slots)
     rows, cols = kc.shape
-    starts = range(0, rows, CHUNK)
     first = lax.axis_index("cuts") == 0
     prescribed = pltpu.make_async_copy(init, late, sem)
 
@@ -225,52 +266,20 @@
     def _():
         prescribed.start()
 
-    def around(ref, lead, start):
-        now = ref[lead + (pl.ds(start, CHUNK), slice(None))]
-        if start + CHUNK < rows:
-            above = ref[lead + (pl.ds(start + 1, CHUNK), slice(None))]
-        else:
-            above = turn(now, -1, 0)
-        if start > 0:
-            below = ref[lead + (pl.ds(start - 1, CHUNK), slice(None))]
-        else:
-            below = turn(now, 1, 0)
-        return now, above, below
-
-    for start in starts:
-        at = pl.ds(start, CHUNK)
-        stiff, _, stiff_low = around(kc, (), start)
+    def coefficients(start, count, fresh):
+        at = pl.ds(start, count)
+        if not fresh:
+            return [cf[number, at, :] for number in range(7)]
+        stiff = kc[at, :]
+        stiff_low = kc[start - 1 : start + count - 1, :] if start else turn(stiff, 1, 0)
         found = scaled_coefficients(
             stiff, stiff_low, ka[at, :], mass[at, :], hoop[at, :], FINE_STEP, FINE_COUPLING
         )
         for number in range(7):
             cf[number, at, :] = found[number]
-        now, above, below = zip(*[around(u, (i,), start) for i in range(3)])
-        acc = accelerate(now, above, below, found)
-        for i in range(3):
-            moved = FINE_STEP * u[3 + i, at, :] + 0.5 * acc[i]
-            half[i, at, :] = moved
-            w1[i, at, :] = now[i] + moved
-    for start in starts:
-        at = pl.ds(start, CHUNK)
-        now, above, below = zip(*[around(w1, (i,), start) for i in range(3)])
-        acc = accelerate(now, above, below, [cf[number, at, :] for number in range(7)])
-        for i in range(3):
-            moved = half[i, at, :] + acc[i]
-            half[i, at, :] = moved
-            front[i, at, :] = now[i] + moved
-    for start in starts:
-        at = pl.ds(start, CHUNK)
-        now, above, below = zip(*[around(front, (i,), start) for i in range(3)])
-        acc = accelerate(now, above, below, [cf[number, at, :] for number in range(7)])
-        for i in range(3):
-            ref, lead = field_of(front, back, 3 + i)
-            ref[lead, at, :] = (half[i, at, :] + 0.5 * acc[i]) * (1.0 / FINE_STEP)
-
-    for i in range(6):
-        ref, lead = field_of(front, back, i)
-        for end, start in enumerate((0, rows - 8)):
-            f_ends[i, 8 * end : 8 * end + 8, :] = ref[lead, start : start + 8, :]
+        return found
+
+    propagate(u, coefficients, w1, half, f)
 
     matrix = averaging(cols)
     few = rows // 2
@@ -295,14 +304,7 @@
         cc[number, 8 : 8 + few, :] = found[number]
     moved = sum(steps_block(parts[:3], [SPEED * q for q in parts[3:6]], found, 1), [])
     means = exact_dot(
-        jnp.concatenate(
-            [
-                pair_sum(ref, (lead,), 0, few)
-                for ref, lead in (field_of(front, back, i) for i in range(6))
-            ],
-            axis=0,
-        ),
-        matrix,
+        jnp.concatenate([pair_sum(f, (i,), 0, few) for i in range(6)], axis=0), matrix
     )
     for i in range(6):
         scale = 1.0 if i < 3 else SPEED
@@ -310,10 +312,10 @@
 
 
 def edges_body(
-    front_in, back_in, f_ends, own, own_coarse, b_in, cc_in, from_below, from_above,
-    front, back, b, cc, fine, coarse, done, slots, sems,
+    f, own, own_coarse, b_in, cc_in, from_below, from_above,
+    done, b, cc, fine, coarse, slots,
 ):
-    rows, cols = front.shape[1:]
+    rows, cols = f.shape[1:]
     few, half_cols = rows // 2, cols // 2
     pair_sum = Halver(slots)
     at = 0
@@ -328,24 +330,14 @@
     w, q = steps_block(
         [fine[i] for i in range(3)], [FINE_STEP * fine[3 + i] for i in range(3)], found, 2
     )
-    done[...] = f_ends[...]
+    for i in range(6):
+        done[i, 0:8, :] = f[i, 0:8, :]
+        done[i, 8:16, :] = f[i, rows - 8 : rows, :]
     for i in range(3):
         done[i, 0:4, :] = w[i][8:12]
         done[i, 12:16, :] = w[i][20:24]
         done[3 + i, 0:4, :] = q[i][8:12] * (1.0 / FINE_STEP)
         done[3 + i, 12:16, :] = q[i][20:24] * (1.0 / FINE_STEP)
-    copies = []
-    for n, (ref, lead) in enumerate(((front, 0), (back, FRONT))):
-        for end, start in enumerate((0, rows - 8)):
-            copies.append(
-                pltpu.make_async_copy(
-                    done.at[lead : lead + ref.shape[0], 8 * end : 8 * end + 8],
-                    ref.at[:, start : start + 8],
-                    sems.at[2 * n + end],
-                )
-            )
-    for copy in copies:
-        copy.start()
 
     sums = [pair_sum(done, (i,), 0, 8) for i in range(6)]
     means = exact_dot(jnp.concatenate(sums, axis=0), averaging(cols))
@@ -377,8 +369,6 @@
         ends = scale * means[8 * i : 8 * i + 8, :]
         b[i, 0:2, :] = ends[0:2] - moved[i][8:10]
         b[i, few - 2 : few, :] = ends[6:8] - moved[i][14:16]
-    for copy in copies:
-        copy.wait()
 
 
 def advance(ext, cc, repeats):
@@ -465,12 +455,15 @@
 
 def collect_body(rounds, *refs):
     messages, belows, aboves = [refs[k * rounds : (k + 1) * rounds] for k in range(3)]
-    total, ext, message, below, above = refs[3 * rounds + 2 :]
-    message[...] = sum(ref[...] for ref in messages)
-    below[...] = sum(ref[...] for ref in belows)
-    above[...] = sum(ref[...] for ref in aboves)
+    total, ext = refs[3 * rounds + 2 :]
+    chip = lax.axis_index("cuts") // 2
     ext[...] = jnp.zeros_like(ext)
-    read_message(ext, message, below, above)
+    for number in range(rounds):
+
+        @pl.when(chip == number + 1)
+        def _():
+            read_message(ext, messages[number], belows[number], aboves[number])
+
     for i in range(6):
         total[i] = ext[i, 8 : ext.shape[1] - 8, :]
 
@@ -481,27 +474,40 @@
         even_end[i] = value[8 : 8 + few] + b_even[i]
 
 
-def second_body(front, back, after, out):
-    @pl.when(lax.axis_index("cuts") == 1)
-    def _():
-        out[...] = front[...]
-
-    @pl.when(lax.axis_index("cuts") != 1)
-    def _():
-        out[...] = back[...]
-
-
-def third_body(back, after, out):
-    out[...] = back[...]
-
-
-def join_body(front, back, out, sems):
-    low = pltpu.make_async_copy(front, out.at[0:FRONT], sems.at[0])
-    high = pltpu.make_async_copy(back, out.at[FRONT:6], sems.at[1])
-    low.start()
-    high.start()
-    low.wait()
-    high.wait()
+def outer_body(f, ends, out):
+    rows = f.shape[1]
+    quarter = rows // 4
+    out[:, 0:8, :] = ends[:, 0:8, :]
+    out[:, 8:quarter, :] = f[:, 8:quarter, :]
+    out[:, quarter : 2 * quarter - 8, :] = f[:, rows - quarter : rows - 8, :]
+    out[:, 2 * quarter - 8 : 2 * quarter, :] = ends[:, 8:16, :]
+
+
+def copy_body(value, after, out):
+    out[...] = value[...]
+
+
+def again_body(u, cf, out, w1, half, made):
+    lead = cf.shape[1] // 4 - MARGIN
+
+    def coefficients(start, count, fresh):
+        return [cf[number, lead + start : lead + start + count, :] for number in range(7)]
+
+    propagate(u, coefficients, w1, half, made)
+    out[...] = made[:, MARGIN : made.shape[1] - MARGIN, :]
+
+
+def join_body(f, ends, out, sems):
+    rows = f.shape[1]
+    copies = [
+        pltpu.make_async_copy(f.at[:, 8 : rows - 8], out.at[:, 8 : rows - 8], sems.at[0]),
+        pltpu.make_async_copy(ends.at[:, 0:8], out.at[:, 0:8], sems.at[1]),
+        pltpu.make_async_copy(ends.at[:, 8:16], out.at[:, rows - 8 : rows], sems.at[2]),
+    ]
+    for copy in copies:
+        copy.start()
+    for copy in copies:
+        copy.wait()
 
 
 def spread_add(values, bases, outs, slots):
@@ -511,47 +517,55 @@
     for i, (base, out) in enumerate(zip(bases, outs)):
         for tile in range(cols // LANES):
             part = wide[i * few : (i + 1) * few, tile * LANES : (tile + 1) * LANES]
+            assert i * (cols // LANES) + tile < slots.shape[0] and 2 * few <= slots.shape[1]
             slot = slots.at[i * (cols // LANES) + tile]
             slot[pl.ds(0, few, stride=2), :] = part
             slot[pl.ds(1, few, stride=2), :] = part
             at = (slice(None), pl.ds(tile * LANES, LANES))
-            out[at] = base[at] + slot[...]
-
-
-def remainder(parts, out, slots):
+            out[at] = base[at] + slot[0 : 2 * few, :]
+
+
+def remainder(parts, outs, slots):
     pair_sum = Halver(slots)
-    cols = out.shape[2]
-    few = out.shape[1] // 2
-    sums = [pair_sum(part, (), 0, few) for _, part in parts]
+    cols = parts[0].shape[1]
+    few = parts[0].shape[0] // 2
+    sums = [pair_sum(part, (), 0, few) for part in parts]
     means = exact_dot(jnp.concatenate(sums, axis=0), averaging(cols))
-    spread_add(-means, [part for _, part in parts], [out.at[i] for i, _ in parts], slots)
-
-
-def early_body(front, back, init, out, slots, sem):
-    fields = [field_of(front, back, i) for i in range(6)]
-    remainder([(i, ref.at[lead]) for i, (ref, lead) in enumerate(fields)], out, slots)
-
-    @pl.when(lax.axis_index("cuts") == 0)
+    spread_add(-means, parts, outs, slots)
+
+
+def outer_parts(ref, quarter):
+    rows = ref.shape[1]
+    ends = (pl.ds(0, quarter), pl.ds(rows - quarter, quarter))
+    return [ref.at[i, end] for i in range(6) for end in ends]
+
+
+def early_body(inner, outer, after_hop, init, out, picked, slots, sem):
+    place = lax.axis_index("cuts")
+    rows = out.shape[1]
+    quarter = rows // 4
+    middle = pl.ds(quarter, rows // 2)
+
+    @pl.when(place == 2)
+    def _():
+        picked[...] = after_hop[...]
+
+    @pl.when(place != 2)
+    def _():
+        picked[...] = outer[...]
+
+    @pl.when(place != 0)
+    def _():
+        remainder(
+            [inner.at[i] for i in range(6)], [out.at[i, middle] for i in range(6)], slots
+        )
+        remainder(outer_parts(picked, quarter), outer_parts(out, quarter), slots)
+
+    @pl.when(place == 0)
     def _():
         copy = pltpu.make_async_copy(init, out, sem)
         copy.start()
         copy.wait()
-
-
-def late_body(base_in, front, back, base, slots, made, sems):
-    place = lax.axis_index("cuts")
-    for n, (lead, ref, found) in enumerate(
-        ((0, front, place == 2), (FRONT, back, (place == 2) | (place == 4)))
-    ):
-        count = ref.shape[0]
-
-        @pl.when(found)
-        def _():
-            remainder([(lead + i, ref.at[i]) for i in range(count)], made, slots)
-            part = pl.ds(lead, count)
-            copy = pltpu.make_async_copy(made.at[part], base.at[part], sems.at[n])
-            copy.start()
-            copy.wait()
 
 
 def correct_body(base, own, received, out, slots, made, sems):
@@ -594,34 +608,42 @@
         pairs = [(s, (s + by) % strips) for s in range(strips)]
         return lax.ppermute(value, "strip", pairs)
 
-    def send(value, by, moves):
-        pairs = [
-            (s * slices + source, (s + by) % strips * slices + target)
-            for s in range(strips)
-            for source, target in moves
-        ]
+
+    def along_cuts(value, moves):
+        rest = [j for j in range(slices) if j not in moves]
+        pairs = list(moves.items()) + [(j, j ^ 1) for j in rest]
+        assert sorted(target for _, target in pairs) == list(range(slices))
+        return lax.ppermute(value, "cuts", pairs)
+
+    def hop(value, by, chip):
+        a, b = 2 * chip, 2 * chip + 2
+        pairs = []
+        for s in range(strips):
+            here, there = s * slices, (s + by) % strips * slices
+            pairs += [(here + a, there + b), (there + b, there + b + 1)]
+            pairs += [(there + b + 1, here + a + 1), (here + a + 1, here + a)]
+            pairs += [(here + j, here + (j ^ 1)) for j in range(slices) if not a <= j < a + 4]
         return lax.ppermute(value, ("strip", "cuts"), pairs)
 
-    def send_with_edges(main, to_above, to_below, moves):
-        return (
-            send(main, 0, moves),
-            send(to_above, 1, moves),
-            send(to_below, -1, moves),
-        )
+    def hop_with_edges(main, to_above, to_below, chip):
+        return hop(main, 0, chip), hop(to_above, 1, chip), hop(to_below, -1, chip)
 
     pack = (PACK_ROWS, cols)
-    half_state = (3, rows, cols)
-    front_state, back_state = (FRONT, rows, cols), (6 - FRONT, rows, cols)
-    ends = (6, 16, cols)
+    third = (3, rows, cols)
+    ends_shape = (6, 16, cols)
     message = (6 * few + 24, half_cols)
-    cc_shape = (7, few + 16, half_cols)
-    to_above, to_below, own, own_coarse, u_near, *near = run(
+    cc_shape, cf_shape = (7, few + 16, half_cols), (7, rows, cols)
+    middle_shape = (6, few + 2 * MARGIN, cols)
+    outer_shape = (6, few, cols)
+    to_above, to_below, own, own_coarse, u_near, *near, middle = run(
         pack_body,
         "pack",
-        [pack, pack, (10, 16, cols), (10, 8, half_cols), state] + [(rows, cols)] * 4,
+        [pack, pack, (10, 16, cols), (10, 8, half_cols), state]
+        + [(rows, cols)] * 4
+        + [middle_shape],
         [u, initial_state, *fields],
         [
-            pltpu.VMEM(ends, F32),
+            pltpu.VMEM(ends_shape, F32),
             halver_scratch(16, 16, cols),
             pltpu.SemaphoreType.DMA((7,)),
         ],
@@ -629,15 +651,15 @@
     )
     from_below = around_loop(to_above, 1)
     from_above = around_loop(to_below, -1)
-    front, back, b, cc, f_ends = run(
+    raw = along_cuts(middle, {j: (j + 1) % slices for j in range(slices)})
+    f, b, cc, cf = run(
         interior_body,
         "interior",
-        [front_state, back_state, coarse_state, cc_shape, ends],
+        [state, coarse_state, cc_shape, cf_shape],
         [u_near, initial_state, *near],
         [
-            pltpu.VMEM((7, rows, cols), F32),
-            pltpu.VMEM(half_state, F32),
-            pltpu.VMEM(half_state, F32),
+            pltpu.VMEM(third, F32),
+            pltpu.VMEM(third, F32),
             pltpu.VMEM((10 * few, cols), F32),
             pltpu.VMEM(state, F32),
             halver_scratch(22, rows, cols),
@@ -645,38 +667,29 @@
         ],
         specs=[VMEM, HBM] + [VMEM] * 4,
     )
-    front, back, b, cc = run(
+    ends, b, cc = run(
         edges_body,
         "edges",
-        [front_state, back_state, coarse_state, cc_shape],
-        [front, back, f_ends, own, own_coarse, b, cc, from_below, from_above],
+        [ends_shape, coarse_state, cc_shape],
+        [f, own, own_coarse, b, cc, from_below, from_above],
         [
             pltpu.VMEM((10, 32, cols), F32),
             pltpu.VMEM((10, 24, half_cols), F32),
-            pltpu.VMEM(ends, F32),
             halver_scratch(6, 16, cols),
-            pltpu.SemaphoreType.DMA((4,)),
         ],
-        specs=[ANY] * 2 + [VMEM] * 7,
-        out_specs=[ANY] * 2 + [VMEM] * 2,
-        aliases={0: 0, 1: 1},
     )
     ext = [pltpu.VMEM(ext_state, F32)]
-    inside = [(2 * z, 2 * z + 1) for z in range(chips)]
-    swap = inside + [(odd, even) for even, odd in inside]
-    b_other = send(b, 0, swap)
+    b_other = along_cuts(b, {})
     source = run(pair_body, "pair", [message, edge, edge], [b, b_other, cc], ext)
-
-    def hops(links):
-        return [(2 * z + 1, 2 * z + 2) for z in links if 0 <= z < chips - 1]
-
-    sent_first = send(front, 0, inside + hops(range(1, chips)))
+    (outer,) = run(outer_body, "outer", [outer_shape], [f, ends])
+
+    previous = along_cuts(outer, {j: j + 1 for j in range(2, slices - 1)} | {slices - 1: 2})
     at_end = source
     arrived = []
     for chip in range(chips - 1):
-        arrived.append(send_with_edges(*at_end, [(2 * chip, 2 * chip + 2)]))
+        arrived.append(hop_with_edges(*at_end, chip))
         if chip < chips - 2:
-            extra = [sent_first] * (chip == 1)
+            extra = {0: [raw], 1: [previous]}.get(chip, [])
             at_end = run(
                 chain_body,
                 "chain",
@@ -687,28 +700,30 @@
             )
         if chip == 0:
             (part,) = run(
-                second_body, "second", [back_state], [front, back, at_end[1]],
-                specs=[VMEM, VMEM, ANY],
+                copy_body, "later", [outer_shape], [outer, at_end[1]], specs=[VMEM, ANY]
             )
-            sent_second = send(part, 0, inside + hops([0, *range(2, chips)]))
-        if chip == 1:
-            (part,) = run(
-                third_body, "third", [back_state], [back, at_end[1]], specs=[VMEM, ANY]
-            )
-            sent_third = send(part, 0, hops([0, 1]))
+            after_hop = lax.ppermute(part, "cuts", [(1, 2)])
     messages, belows, aboves = zip(*arrived)
     (fine_end,) = run(
         join_body,
         "join",
         [state],
-        [front, back],
-        [pltpu.SemaphoreType.DMA((2,))],
+        [f, ends],
+        [pltpu.SemaphoreType.DMA((3,))],
         specs=[ANY] * 2,
         out_specs=[ANY],
         cost=(0, 6 * rows * cols * 8),
     )
+    (inner,) = run(
+        again_body,
+        "again",
+        [outer_shape],
+        [raw, cf],
+        [pltpu.VMEM((3,) + middle_shape[1:], F32)] * 2 + [pltpu.VMEM(middle_shape, F32)],
+        cost=(0, 6 * rows * cols * 8),
+    )
     rem_scratch = [
-        halver_scratch(6, rows, cols),
+        halver_scratch(12, rows, cols),
         pltpu.VMEM(state, F32),
         pltpu.SemaphoreType.DMA((2,)),
     ]
@@ -716,9 +731,13 @@
         early_body,
         "remainder",
         [state],
-        [sent_first, sent_second, initial_state],
-        [halver_scratch(6, rows, cols), pltpu.SemaphoreType.DMA],
-        specs=[VMEM, VMEM, HBM],
+        [inner, previous, after_hop, initial_state],
+        [
+            pltpu.VMEM(outer_shape, F32),
+            halver_scratch(12, few, cols),
+            pltpu.SemaphoreType.DMA,
+        ],
+        specs=[VMEM] * 3 + [HBM],
         cost=(0, 6 * rows * cols * 8),
     )
     total, wide = run(
@@ -726,21 +745,10 @@
         "collect",
         [coarse_state, ext_state],
         [*messages, *belows, *aboves, base, fine_end],
-        [pltpu.VMEM(message, F32), pltpu.VMEM(edge, F32), pltpu.VMEM(edge, F32)],
         specs=[VMEM] * (3 * len(messages)) + [ANY, HBM],
     )
     (even_end,) = run(even_body, "even", [coarse_state], [wide, b, cc])
-    received = send(even_end, 0, swap)
-    (base,) = run(
-        late_body,
-        "late",
-        [state],
-        [base, sent_second, sent_third],
-        rem_scratch,
-        specs=[ANY, VMEM, VMEM],
-        out_specs=[ANY],
-        aliases={0: 0},
-    )
+    received = along_cuts(even_end, {})
     (new_start,) = run(
         correct_body,
         "correct",

time: 53 us -> 45.5 us (0.86)
  the two profiles are of different devices: /device:TPU:16 before, /device:TPU:27 now
where the time goes in v3:
time: 45.5 us; the launch traced here: 45.3 us
  starting transfers between devices  19.2 us (42%)
  Pallas kernels  15.8 us (35%)
  waiting for transfers between devices  9.5 us (21%)
  between operations  0.78 us (2%)
    pallas_call x14, Pallas kernels, run(): pl.pallas_call(body, name=name, out_shape=[jax.ShapeDtypeStruct(shape, F3...  15.8 us
    ppermute x9, starting transfers between devices, hop(): return lax.ppermute(value, ('strip', 'cuts'), pairs)  12.4 us
    ppermute x4, waiting for transfers between devices, along_cuts(): return lax.ppermute(value, 'cuts', pairs)  7.17 us
    ppermute x4, starting transfers between devices, along_cuts(): return lax.ppermute(value, 'cuts', pairs)  4.67 us
    ppermute x9, waiting for transfers between devices, hop(): return lax.ppermute(value, ('strip', 'cuts'), pairs)  1.48 us
    ppermute x2, starting transfers between devices, around_loop(): return lax.ppermute(value, 'strip', pairs)  1.47 us
  transfers between devices with their start and end apart: 16, of which 5 were waited for; matrix products, arithmetic and copies ran while one was open for 0% of the time, Pallas kernels for 25%

profile of v3, /device:TPU:27, one launch (start us, length us, event | category | flops | bytes accessed | tf_op | source)
XLA Modules:
  0.0 45.3 jit_solution(11655922348585139672)
XLA Ops:
  0.6 2.2 %pack.1 = (f32[40,512]{1,0:T(8,128)S(1)}, f32[40,512]{1,0:T(8,128)S(1)}, f32[10,16,512]{2,1,0:T(8,128)S(1)}, f32[10,8,256]{2,1,0:T(8,128)S(1)}, f32[6,128,512]{2...) custom-call(f32[6,128,512]{2,1,0:T(8,128)} %bitcast.4, ...), custom_call_target="tpu_custom_call" | custom-call | tf_op jit(solution)/shard_map/pack/pallas_call | solution.py:34
  2.8 0.6 %collective-permute-start = (f32[6,80,512]{2,1,0:T(8,128)S(1)}, f32[6,80,512]{2,1,0:T(8,128)S(1)}, u32[]{:S(2)}, u32[]{:S(2)}) collective-permute-start(f32[6,80,512]{2,1,0:T(8,128)S(1)} %get-tuple-element.30), channel_id=1, source_target_pairs={{0,1},{1,2},{2,3},{3,4},{4,5},{5,6},{6,7},{7,0},{8,9},{9,10},{10,1... | collective-permute-start | bytes 2949128 | tf_op jit(solution)/shard_map/ppermute | solution.py:616
  3.4 1.2 %collective-permute-start.1 = (f32[40,512]{1,0:T(8,128)S(1)}, f32[40,512]{1,0:T(8,128)S(1)}, u32[]{:S(2)}, u32[]{:S(2)}) collective-permute-start(f32[40,512]{1,0:T(8,128)S(1)} %get-tuple-element.42), channel_id=1, source_target_pairs={{0,8},{8,16},{16,24},{24,0},{1,9},{9,17},{17,25},{25,1},{2,10},{10... | collective-permute-start | bytes 245768 | tf_op jit(solution)/shard_map/ppermute | solution.py:609
  4.6 0.3 collective-permute-start.2
  4.9 4.2 %interior.1 = (f32[6,128,512]{2,1,0:T(8,128)S(1)}, f32[6,64,256]{2,1,0:T(8,128)S(1)}, f32[7,80,256]{2,1,0:T(8,128)S(1)}, f32[7,128,512]{2,1,0:T(8,128)S(1)}) custom-call(f32[6,128,512]{2,1,0:T(8,128)S(1)} %get-tuple-element.31.u, f32[6,128,512]{2,1,0:T(8,128)} %init.5, f32[128,512]{1,0:T(8,128)S(1)} %get-tuple-element.32.kc, ...), custom_call_target="tpu_custom_call" | custom-call | tf_op jit(solution)/shard_map/interior/pallas_call | solution.py:34
  9.1 0.0 collective-permute-done.1.from_below
  9.1 0.8 %collective-permute-done.2.from_above = f32[40,512]{1,0:T(8,128)S(1)} collective-permute-done((f32[40,512]{1,0:T(8,128)S(1)}, f32[40,512]{1,0:T(8,128)S(1)}, u32[]{:S(2)}, u32[]{:S(2)}) %collective-permute-start.2) | collective-permute-done | bytes 81952 | tf_op jit(solution)/shard_map/ppermute | solution.py:609
  10.0 0.8 %edges.1 = (f32[6,16,512]{2,1,0:T(8,128)S(1)}, f32[6,64,256]{2,1,0:T(8,128)S(1)}, f32[7,80,256]{2,1,0:T(8,128)S(1)}) custom-call(f32[6,128,512]{2,1,0:T(8,128)S(1)} %get-tuple-element.37.f, f32[10,16,512]{2,1,0:T(8,128)S(1)} %get-tuple-element.38.own, f32[10,8,256]{2,1,0:T(8,128)S(1)} %get-tuple-element.39.own_coarse, ...), custom_call_target="tpu_custom_call" | custom-call | tf_op jit(solution)/shard_map/edges/pallas_call | solution.py:34
  10.8 1.1 %collective-permute-start.4 = (f32[6,64,256]{2,1,0:T(8,128)S(1)}, f32[6,64,256]{2,1,0:T(8,128)S(1)}, u32[]{:S(2)}, u32[]{:S(2)}) collective-permute-start(f32[6,64,256]{2,1,0:T(8,128)S(1)} %get-tuple-element.45.b_even), channel_id=1, source_target_pairs={{0,1},{1,0},{2,3},{3,2},{4,5},{5,4},{6,7},{7,6},{8,9},{9,8},{10,11... | collective-permute-start | bytes 1179656 | tf_op jit(solution)/shard_map/ppermute | solution.py:616
  11.9 1.3 %collective-permute-done.4.b_odd = f32[6,64,256]{2,1,0:T(8,128)S(1)} collective-permute-done((f32[6,64,256]{2,1,0:T(8,128)S(1)}, f32[6,64,256]{2,1,0:T(8,128)S(1)}, u32[]{:S(2)}, u32[]{:S(2)}) %collective-permute-start.4) | collective-permute-done | bytes 393248 | tf_op jit(solution)/shard_map/ppermute | solution.py:616
  13.2 0.5 %pair.1 = (f32[408,256]{1,0:T(8,128)S(1)}, f32[24,256]{1,0:T(8,128)S(1)}, f32[24,256]{1,0:T(8,128)S(1)}) custom-call(f32[6,64,256]{2,1,0:T(8,128)S(1)} %get-tuple-element.45.b_even, f32[6,64,256]{2,1,0:T(8,128)S(1)} %collective-permute-done.4.b_odd, f32[7,80,256]{2,1,0:T(8,128)S(1)} %get-tuple-element.46.cc), custom_call_target="tpu_custom_call" | custom-call | tf_op jit(solution)/shard_map/pair/pallas_call | solution.py:34
  13.8 0.4 collective-permute-start.5
  14.2 0.1 outer.1.value
  14.2 0.6 %collective-permute-start.3 = (f32[6,64,512]{2,1,0:T(8,128)S(1)}, f32[6,64,512]{2,1,0:T(8,128)S(1)}, u32[]{:S(2)}, u32[]{:S(2)}) collective-permute-start(f32[6,64,512]{2,1,0:T(8,128)S(1)} %outer.1.value), channel_id=1, source_target_pairs={{2,3},{3,4},{4,5},{5,6},{6,7},{7,2},{0,1},{1,0},{10,11},{11,12},{1... | collective-permute-start | bytes 2359304 | tf_op jit(solution)/shard_map/ppermute | solution.py:616
  14.8 0.0 collective-permute-start.6
  14.8 0.5 %collective-permute-start.7 = (f32[24,256]{1,0:T(8,128)S(1)}, f32[24,256]{1,0:T(8,128)S(1)}, u32[]{:S(2)}, u32[]{:S(2)}) collective-permute-start(f32[24,256]{1,0:T(8,128)S(1)} %get-tuple-element.49), channel_id=1, source_target_pairs={{0,26},{26,27},{27,1},{1,0},{4,5},{5,4},{6,7},{7,6},{8,2},{2,3},{3... | collective-permute-start | bytes 73736 | tf_op jit(solution)/shard_map/ppermute | solution.py:626
  15.3 1.4 %collective-permute-done.6.below.refs_3_ = f32[24,256]{1,0:T(8,128)S(1)} collective-permute-done((f32[24,256]{1,0:T(8,128)S(1)}, f32[24,256]{1,0:T(8,128)S(1)}, u32[]{:S(2)}, u32[]{:S(2)}) %collective-permute-start.6) | collective-permute-done | bytes 24608 | tf_op jit(solution)/shard_map/ppermute | solution.py:626
  16.7 0.0 collective-permute-done.7.above.refs_6_
  16.8 0.0 collective-permute-done.5.message.refs_0_
  16.8 0.0 collective-permute-done.u.refs_0_
  16.8 0.8 %chain.2 = (f32[408,256]{1,0:T(8,128)S(1)}, f32[24,256]{1,0:T(8,128)S(1)}, f32[24,256]{1,0:T(8,128)S(1)}) custom-call(f32[408,256]{1,0:T(8,128)S(1)} %collective-permute-done.5.message.refs_0_, f32[24,256]{1,0:T(8,128)S(1)} %collective-permute-done.6.below.refs_3_, f32[24,256]{1,0:T(8,128)S(1)} %collective-permute-done.7.above.refs_6_, ...), custom_call_target="tpu_custom_call" | custom-call | tf_op jit(solution)/shard_map/chain/pallas_call | solution.py:34
  17.5 0.4 collective-permute-start.9
  17.9 0.1 later.1
  18.0 0.7 %collective-permute-start.8 = (f32[6,64,512]{2,1,0:T(8,128)S(1)}, f32[6,64,512]{2,1,0:T(8,128)S(1)}, u32[]{:S(2)}, u32[]{:S(2)}) collective-permute-start(f32[6,64,512]{2,1,0:T(8,128)S(1)} %later.1), channel_id=1, source_target_pairs={{1,2},{9,10},{17,18},{25,26}} | collective-permute-start | bytes 2359304 | tf_op jit(solution)/shard_map/ppermute | solution.py:705
  18.7 0.2 collective-permute-start.11
  18.9 0.3 collective-permute-start.10
  19.2 4.5 %collective-permute-done.3.outer.refs_0_ = f32[6,64,512]{2,1,0:T(8,128)S(1)} collective-permute-done((f32[6,64,512]{2,1,0:T(8,128)S(1)}, f32[6,64,512]{2,1,0:T(8,128)S(1)}, u32[]{:S(2)}, u32[]{:S(2)}) %collective-permute-start.3) | collective-permute-done | bytes 786464 | tf_op jit(solution)/shard_map/ppermute | solution.py:616
  23.7 0.0 collective-permute-done.11.above.refs_7_
  23.7 0.0 collective-permute-done.10.below.refs_4_
  23.7 0.0 collective-permute-done.9.message.refs_1_
  23.7 0.8 %chain.3 = (f32[408,256]{1,0:T(8,128)S(1)}, f32[24,256]{1,0:T(8,128)S(1)}, f32[24,256]{1,0:T(8,128)S(1)}) custom-call(f32[408,256]{1,0:T(8,128)S(1)} %collective-permute-done.9.message.refs_1_, f32[24,256]{1,0:T(8,128)S(1)} %collective-permute-done.10.below.refs_4_, f32[24,256]{1,0:T(8,128)S(1)} %collective-permute-done.11.above.refs_7_, ...), custom_call_target="tpu_custom_call" | custom-call | tf_op jit(solution)/shard_map/chain/pallas_call | solution.py:34
  24.5 6.3 %collective-permute-start.12 = (f32[408,256]{1,0:T(8,128)S(1)}, f32[408,256]{1,0:T(8,128)S(1)}, u32[]{:S(2)}, u32[]{:S(2)}) collective-permute-start(f32[408,256]{1,0:T(8,128)S(1)} %get-tuple-element.53), channel_id=1, source_target_pairs={{4,6},{6,7},{7,5},{5,4},{0,1},{1,0},{2,3},{3,2},{12,14},{14,15},{1... | collective-permute-start | bytes 1253384 | tf_op jit(solution)/shard_map/ppermute | solution.py:626
  30.7 3.2 %collective-permute-start.13 = (f32[24,256]{1,0:T(8,128)S(1)}, f32[24,256]{1,0:T(8,128)S(1)}, u32[]{:S(2)}, u32[]{:S(2)}) collective-permute-start(f32[24,256]{1,0:T(8,128)S(1)} %get-tuple-element.54), channel_id=1, source_target_pairs={{4,14},{14,15},{15,5},{5,4},{0,1},{1,0},{2,3},{3,2},{12,22},{22,23... | collective-permute-start | bytes 73736 | tf_op jit(solution)/shard_map/ppermute | solution.py:626
  34.0 1.1 %collective-permute-start.14 = (f32[24,256]{1,0:T(8,128)S(1)}, f32[24,256]{1,0:T(8,128)S(1)}, u32[]{:S(2)}, u32[]{:S(2)}) collective-permute-start(f32[24,256]{1,0:T(8,128)S(1)} %get-tuple-element.55), channel_id=1, source_target_pairs={{4,30},{30,31},{31,5},{5,4},{0,1},{1,0},{2,3},{3,2},{12,6},{6,7},{... | collective-permute-start | bytes 73736 | tf_op jit(solution)/shard_map/ppermute | solution.py:626
  35.0 1.1 %join.1.refs_10_ = f32[6,128,512]{2,1,0:T(8,128)} custom-call(f32[6,128,512]{2,1,0:T(8,128)S(1)} %get-tuple-element.37.f, f32[6,16,512]{2,1,0:T(8,128)S(1)} %get-tuple-element.44.ends), custom_call_target="tpu_custom_call" | custom-call | bytes 3145728 | tf_op jit(solution)/shard_map/join/pallas_call | solution.py:34
  36.2 1.2 %again.1.inner = f32[6,64,512]{2,1,0:T(8,128)S(1)} custom-call(f32[6,80,512]{2,1,0:T(8,128)S(1)} %collective-permute-done.u.refs_0_, f32[7,128,512]{2,1,0:T(8,128)S(1)} %get-tuple-element.36.cf), custom_call_target="tpu_custom_call" | custom-call | bytes 3145728 | tf_op jit(solution)/shard_map/again/pallas_call | solution.py:34
  37.4 0.0 collective-permute-done.8.after_hop
  37.4 1.8 %remainder.1.refs_9_.base = f32[6,128,512]{2,1,0:T(8,128)S(1)} custom-call(f32[6,64,512]{2,1,0:T(8,128)S(1)} %again.1.inner, f32[6,64,512]{2,1,0:T(8,128)S(1)} %collective-permute-done.3.outer.refs_0_, f32[6,64,512]{2,1,0:T(8,128)S(1)} %collective-permute-done.8.after_hop, f32[6,128,512]{2,1,0:T(8,128)} %init.5), custom_call_target="tpu_custom_call" | custom-call | bytes 3145728 | tf_op jit(solution)/shard_map/remainder/pallas_call | solution.py:34
  39.3 0.0 collective-permute-done.13.refs_5_
  39.3 0.0 collective-permute-done.14.refs_8_
  39.3 0.0 collective-permute-done.12.refs_2_
  39.3 0.1 collect.1
  39.4 0.5 %even.1 = f32[6,64,256]{2,1,0:T(8,128)S(1)} custom-call(f32[6,80,256]{2,1,0:T(8,128)S(1)} %get-tuple-element.57.ext, f32[6,64,256]{2,1,0:T(8,128)S(1)} %get-tuple-element.45.b_even, f32[7,80,256]{2,1,0:T(8,128)S(1)} %get-tuple-element.46.cc), custom_call_target="tpu_custom_call" | custom-call | tf_op jit(solution)/shard_map/even/pallas_call | solution.py:34
  39.9 2.5 %collective-permute-start.15 = (f32[6,64,256]{2,1,0:T(8,128)S(1)}, f32[6,64,256]{2,1,0:T(8,128)S(1)}, u32[]{:S(2)}, u32[]{:S(2)}) collective-permute-start(f32[6,64,256]{2,1,0:T(8,128)S(1)} %even.1), channel_id=1, source_target_pairs={{0,1},{1,0},{2,3},{3,2},{4,5},{5,4},{6,7},{7,6},{8,9},{9,8},{10,11... | collective-permute-start | bytes 1179656 | tf_op jit(solution)/shard_map/ppermute | solution.py:616
  42.4 1.3 %collective-permute-done.15.received = f32[6,64,256]{2,1,0:T(8,128)S(1)} collective-permute-done((f32[6,64,256]{2,1,0:T(8,128)S(1)}, f32[6,64,256]{2,1,0:T(8,128)S(1)}, u32[]{:S(2)}, u32[]{:S(2)}) %collective-permute-start.15) | collective-permute-done | bytes 393248 | tf_op jit(solution)/shard_map/ppermute | solution.py:616
  43.8 1.5 %correct.1 = f32[6,128,512]{2,1,0:T(8,128)} custom-call(f32[6,128,512]{2,1,0:T(8,128)S(1)} %remainder.1.refs_9_.base, f32[6,64,256]{2,1,0:T(8,128)S(1)} %get-tuple-element.56.own, f32[6,64,256]{2,1,0:T(8,128)S(1)} %collective-permute-done.15.received), custom_call_target="tpu_custom_call" | custom-call | tf_op jit(solution)/shard_map/correct/pallas_call | solution.py:34
Async XLA Ops:
  2.8 13.9 %collective-permute-start = (f32[6,80,512]{2,1,0:T(8,128)S(1)}, f32[6,80,512]{2,1,0:T(8,128)S(1)}, u32[]{:S(2)}, u32[]{:S(2)}) collective-permute-start(f32[6,80,512]{2,1,0:T(8,128)S(1)} %get-tuple-element.30), channel_id=1, source_target_pairs={{0,1},{1,2},{2,3},{3,4},{4,5},{5,6},{6,7},{7,0},{8,9},{9,10},{10,1... | collective-permute-start | bytes 2949128 | tf_op jit(solution)/shard_map/ppermute | solution.py:616
  3.4 5.7 %collective-permute-start.1 = (f32[40,512]{1,0:T(8,128)S(1)}, f32[40,512]{1,0:T(8,128)S(1)}, u32[]{:S(2)}, u32[]{:S(2)}) collective-permute-start(f32[40,512]{1,0:T(8,128)S(1)} %get-tuple-element.42), channel_id=1, source_target_pairs={{0,8},{8,16},{16,24},{24,0},{1,9},{9,17},{17,25},{25,1},{2,10},{10... | collective-permute-start | bytes 245768 | tf_op jit(solution)/shard_map/ppermute | solution.py:609
  4.6 5.4 %collective-permute-start.2 = (f32[40,512]{1,0:T(8,128)S(1)}, f32[40,512]{1,0:T(8,128)S(1)}, u32[]{:S(2)}, u32[]{:S(2)}) collective-permute-start(f32[40,512]{1,0:T(8,128)S(1)} %get-tuple-element.43), channel_id=1, source_target_pairs={{0,24},{8,0},{16,8},{24,16},{1,25},{9,1},{17,9},{25,17},{2,26},{10... | collective-permute-start | bytes 245768 | tf_op jit(solution)/shard_map/ppermute | solution.py:609
  10.8 2.4 %collective-permute-start.4 = (f32[6,64,256]{2,1,0:T(8,128)S(1)}, f32[6,64,256]{2,1,0:T(8,128)S(1)}, u32[]{:S(2)}, u32[]{:S(2)}) collective-permute-start(f32[6,64,256]{2,1,0:T(8,128)S(1)} %get-tuple-element.45.b_even), channel_id=1, source_target_pairs={{0,1},{1,0},{2,3},{3,2},{4,5},{5,4},{6,7},{7,6},{8,9},{9,8},{10,11... | collective-permute-start | bytes 1179656 | tf_op jit(solution)/shard_map/ppermute | solution.py:616
  13.8 3.0 %collective-permute-start.5 = (f32[408,256]{1,0:T(8,128)S(1)}, f32[408,256]{1,0:T(8,128)S(1)}, u32[]{:S(2)}, u32[]{:S(2)}) collective-permute-start(f32[408,256]{1,0:T(8,128)S(1)} %get-tuple-element.47.source), channel_id=1, source_target_pairs={{0,2},{2,3},{3,1},{1,0},{4,5},{5,4},{6,7},{7,6},{8,10},{10,11},{11... | collective-permute-start | bytes 1253384 | tf_op jit(solution)/shard_map/ppermute | solution.py:626
  14.2 9.5 %collective-permute-start.3 = (f32[6,64,512]{2,1,0:T(8,128)S(1)}, f32[6,64,512]{2,1,0:T(8,128)S(1)}, u32[]{:S(2)}, u32[]{:S(2)}) collective-permute-start(f32[6,64,512]{2,1,0:T(8,128)S(1)} %outer.1.value), channel_id=1, source_target_pairs={{2,3},{3,4},{4,5},{5,6},{6,7},{7,2},{0,1},{1,0},{10,11},{11,12},{1... | collective-permute-start | bytes 2359304 | tf_op jit(solution)/shard_map/ppermute | solution.py:616
  14.8 1.9 %collective-permute-start.6 = (f32[24,256]{1,0:T(8,128)S(1)}, f32[24,256]{1,0:T(8,128)S(1)}, u32[]{:S(2)}, u32[]{:S(2)}) collective-permute-start(f32[24,256]{1,0:T(8,128)S(1)} %get-tuple-element.48), channel_id=1, source_target_pairs={{0,10},{10,11},{11,1},{1,0},{4,5},{5,4},{6,7},{7,6},{8,18},{18,19}... | collective-permute-start | bytes 73736 | tf_op jit(solution)/shard_map/ppermute | solution.py:626
  14.8 2.0 %collective-permute-start.7 = (f32[24,256]{1,0:T(8,128)S(1)}, f32[24,256]{1,0:T(8,128)S(1)}, u32[]{:S(2)}, u32[]{:S(2)}) collective-permute-start(f32[24,256]{1,0:T(8,128)S(1)} %get-tuple-element.49), channel_id=1, source_target_pairs={{0,26},{26,27},{27,1},{1,0},{4,5},{5,4},{6,7},{7,6},{8,2},{2,3},{3... | collective-permute-start | bytes 73736 | tf_op jit(solution)/shard_map/ppermute | solution.py:626
  17.5 6.2 %collective-permute-start.9 = (f32[408,256]{1,0:T(8,128)S(1)}, f32[408,256]{1,0:T(8,128)S(1)}, u32[]{:S(2)}, u32[]{:S(2)}) collective-permute-start(f32[408,256]{1,0:T(8,128)S(1)} %get-tuple-element.51), channel_id=1, source_target_pairs={{2,4},{4,5},{5,3},{3,2},{0,1},{1,0},{6,7},{7,6},{10,12},{12,13},{1... | collective-permute-start | bytes 1253384 | tf_op jit(solution)/shard_map/ppermute | solution.py:626
  18.0 19.5 %collective-permute-start.8 = (f32[6,64,512]{2,1,0:T(8,128)S(1)}, f32[6,64,512]{2,1,0:T(8,128)S(1)}, u32[]{:S(2)}, u32[]{:S(2)}) collective-permute-start(f32[6,64,512]{2,1,0:T(8,128)S(1)} %later.1), channel_id=1, source_target_pairs={{1,2},{9,10},{17,18},{25,26}} | collective-permute-start | bytes 2359304 | tf_op jit(solution)/shard_map/ppermute | solution.py:705
  18.7 5.0 %collective-permute-start.11 = (f32[24,256]{1,0:T(8,128)S(1)}, f32[24,256]{1,0:T(8,128)S(1)}, u32[]{:S(2)}, u32[]{:S(2)}) collective-permute-start(f32[24,256]{1,0:T(8,128)S(1)} %get-tuple-element.52), channel_id=1, source_target_pairs={{2,28},{28,29},{29,3},{3,2},{0,1},{1,0},{6,7},{7,6},{10,4},{4,5},{... | collective-permute-start | bytes 73736 | tf_op jit(solution)/shard_map/ppermute | solution.py:626
  18.9 4.8 %collective-permute-start.10 = (f32[24,256]{1,0:T(8,128)S(1)}, f32[24,256]{1,0:T(8,128)S(1)}, u32[]{:S(2)}, u32[]{:S(2)}) collective-permute-start(f32[24,256]{1,0:T(8,128)S(1)} %get-tuple-element.50.after), channel_id=1, source_target_pairs={{2,12},{12,13},{13,3},{3,2},{0,1},{1,0},{6,7},{7,6},{10,20},{20,21... | collective-permute-start | bytes 73736 | tf_op jit(solution)/shard_map/ppermute | solution.py:626
  24.5 14.8 %collective-permute-start.12 = (f32[408,256]{1,0:T(8,128)S(1)}, f32[408,256]{1,0:T(8,128)S(1)}, u32[]{:S(2)}, u32[]{:S(2)}) collective-permute-start(f32[408,256]{1,0:T(8,128)S(1)} %get-tuple-element.53), channel_id=1, source_target_pairs={{4,6},{6,7},{7,5},{5,4},{0,1},{1,0},{2,3},{3,2},{12,14},{14,15},{1... | collective-permute-start | bytes 1253384 | tf_op jit(solution)/shard_map/ppermute | solution.py:626
  30.7 8.5 %collective-permute-start.13 = (f32[24,256]{1,0:T(8,128)S(1)}, f32[24,256]{1,0:T(8,128)S(1)}, u32[]{:S(2)}, u32[]{:S(2)}) collective-permute-start(f32[24,256]{1,0:T(8,128)S(1)} %get-tuple-element.54), channel_id=1, source_target_pairs={{4,14},{14,15},{15,5},{5,4},{0,1},{1,0},{2,3},{3,2},{12,22},{22,23... | collective-permute-start | bytes 73736 | tf_op jit(solution)/shard_map/ppermute | solution.py:626
  34.0 5.3 %collective-permute-start.14 = (f32[24,256]{1,0:T(8,128)S(1)}, f32[24,256]{1,0:T(8,128)S(1)}, u32[]{:S(2)}, u32[]{:S(2)}) collective-permute-start(f32[24,256]{1,0:T(8,128)S(1)} %get-tuple-element.55), channel_id=1, source_target_pairs={{4,30},{30,31},{31,5},{5,4},{0,1},{1,0},{2,3},{3,2},{12,6},{6,7},{... | collective-permute-start | bytes 73736 | tf_op jit(solution)/shard_map/ppermute | solution.py:626
  39.9 3.8 %collective-permute-start.15 = (f32[6,64,256]{2,1,0:T(8,128)S(1)}, f32[6,64,256]{2,1,0:T(8,128)S(1)}, u32[]{:S(2)}, u32[]{:S(2)}) collective-permute-start(f32[6,64,256]{2,1,0:T(8,128)S(1)} %even.1), channel_id=1, source_target_pairs={{0,1},{1,0},{2,3},{3,2},{4,5},{5,4},{6,7},{7,6},{8,9},{9,8},{10,11... | collective-permute-start | bytes 1179656 | tf_op jit(solution)/shard_map/ppermute | solution.py:616

commit v4 on v3

--- a/solution.py
+++ b/solution.py
@@ -12,12 +12,13 @@
 SPEED = COARSE_STEP
 
 FINE_ROWS = (3, 3, 3, 2, 2, 2, 3, 2, 2, 2)
-COARSE_ROWS = (2, 2, 2, 1, 1, 1, 3, 2, 2, 2)
+COARSE_ROWS = (2, 2, 2, 1, 1, 1, 6, 5, 5, 5)
 FINE_TOTAL = sum(FINE_ROWS)
 PACK_ROWS = -(-(FINE_TOTAL + -(-sum(COARSE_ROWS) // 2)) // 8) * 8
 CHUNK = 16
+HALO_COST = int(3.4e9)
+LAST_COST = int(1e9)
 MARGIN = 8
-EDGE = 4
 
 VMEM = pl.BlockSpec(memory_space=pltpu.VMEM)
 ANY = pl.BlockSpec(memory_space=pl.ANY)
@@ -149,7 +150,7 @@
 
 
 def halver_scratch(fields, rows, cols):
-    return pltpu.VMEM((fields * (cols // LANES), rows, LANES), F32)
+    return pltpu.VMEM((fields * (cols // LANES), rows + 8, LANES), F32)
 
 
 def is_first():
@@ -163,8 +164,10 @@
     rows, cols = kc.shape
     pair_sum = Halver(slots)
     first = is_first()
-    copies = [(init.at[:, start : start + 8], early.at[:, pl.ds(8 * end, 8)])
-              for end, start in enumerate((0, rows - 8))]
+    copies = [
+        (init.at[:, start : start + 16], early.at[:, pl.ds(16 * end, 16)])
+        for end, start in enumerate((0, rows - 16))
+    ]
     copies += [(u_far, u), (kc_far, kc), (ka_far, ka), (mass_far, mass), (hoop_far, hoop)]
     copies = [
         pltpu.make_async_copy(source, target, sems.at[n])
@@ -187,24 +190,24 @@
         to_below[at : at + count, :] = own[number, 0:count, :]
         at += count
     sums = []
-    for number in range(10):
-        value = pair_sum(own, (number,), 0, 8)
-        if number < 6:
-            value = value - first * pair_sum(early, (number,), 0, 8)
-        sums.append(value)
+    for start in (rows - 16, 0):
+        for number, ref in enumerate([u] * 6 + [kc, ka, mass, hoop]):
+            value = pair_sum(ref, (number,) if number < 6 else (), start, 8)
+            if number < 6:
+                value = value - first * pair_sum(early, (number,), 16 * (start > 0), 8)
+            sums.append(value)
     means = exact_dot(jnp.concatenate(sums, axis=0), matrix)
-    for number in range(10):
-        own_coarse[number] = means[8 * number : 8 * number + 8]
     half = cols // 2
     at = 0
     for number, count in enumerate(COARSE_ROWS):
+        high, low = means[8 * number : 8 * number + 8], means[80 + 8 * number : 88 + 8 * number]
+        own_coarse[number, 0:4, :] = low[0:4]
+        own_coarse[number, 4:8, :] = high[4:8]
         for k in range(count):
             line = FINE_TOTAL + at // 2
             place = (slice(line, line + 1), pl.ds((at % 2) * half, half))
-            low = 8 * number + 8 - count + k
-            high = 8 * number + k
-            to_above[place] = means[low : low + 1]
-            to_below[place] = means[high : high + 1]
+            to_above[place] = high[8 - count + k : 9 - count + k]
+            to_below[place] = low[k : k + 1]
             at += 1
     lead = rows // 4 - MARGIN
     middle[...] = u[:, lead : rows - lead, :]
@@ -385,40 +388,36 @@
 
 def write_edges(message, to_above, to_below):
     few = (message.shape[0] - 24) // 6
+    lines = to_above.shape[0] // 6
     for i in range(6):
-        own, beyond, at = i * few, 6 * few + 4 * i, 4 * i
-        if i < 3:
-            to_above[at : at + 3, :] = message[own + few - 3 : own + few, :]
-            to_above[at + 3 : at + 4, :] = message[beyond + 1 : beyond + 2, :]
-            to_below[at : at + 1, :] = message[beyond : beyond + 1, :]
-            to_below[at + 1 : at + 4, :] = message[own : own + 3, :]
-        else:
-            to_above[at : at + 2, :] = message[own + few - 2 : own + few, :]
-            to_above[at + 2 : at + 4, :] = message[beyond + 2 : beyond + 4, :]
-            to_below[at : at + 2, :] = message[beyond : beyond + 2, :]
-            to_below[at + 2 : at + 4, :] = message[own : own + 2, :]
+        own, beyond, at = i * few, 6 * few + 4 * i, lines * i
+        extra = 1 if i < 3 else 2
+        rows = lines - extra
+        to_above[at : at + rows, :] = message[own + few - rows : own + few, :]
+        to_above[at + rows : at + lines, :] = message[beyond + extra : beyond + 2 * extra, :]
+        to_below[at : at + extra, :] = message[beyond : beyond + extra, :]
+        to_below[at + extra : at + lines, :] = message[own : own + rows, :]
 
 
 def read_message(ext, message, below, above):
     few = ext.shape[1] - 16
     top = 8 + few
+    lines = below.shape[0] // 6
     for i in range(6):
-        own, beyond, at = i * few, 6 * few + 4 * i, 4 * i
+        own, beyond, at = i * few, 6 * few + 4 * i, lines * i
+        extra = 1 if i < 3 else 2
+        rows = lines - extra
         ext[i, 8:top, :] = message[own : own + few, :]
-        if i < 3:
-            ext[i, 5:8, :] = below[at : at + 3, :]
-            ext[i, 7:8, :] += message[beyond : beyond + 1, :]
-            ext[i, 8:9, :] += below[at + 3 : at + 4, :]
-            ext[i, top - 1 : top, :] += above[at : at + 1, :]
-            ext[i, top : top + 3, :] = above[at + 1 : at + 4, :]
-            ext[i, top : top + 1, :] += message[beyond + 1 : beyond + 2, :]
-        else:
-            ext[i, 6:8, :] = below[at : at + 2, :] + message[beyond : beyond + 2, :]
-            ext[i, 8:10, :] += below[at + 2 : at + 4, :]
-            ext[i, top - 2 : top, :] += above[at : at + 2, :]
-            ext[i, top : top + 2, :] = (
-                above[at + 2 : at + 4, :] + message[beyond + 2 : beyond + 4, :]
-            )
+        ext[i, 8 - rows : 8, :] = below[at : at + rows, :]
+        ext[i, top : top + rows, :] = above[at + extra : at + lines, :]
+        ext[i, 8 - extra : 8, :] += message[beyond : beyond + extra, :]
+        ext[i, top : top + extra, :] += message[beyond + extra : beyond + 2 * extra, :]
+        ext[i, 8 : 8 + extra, :] += below[at + rows : at + lines, :]
+        ext[i, top - extra : top, :] += above[at : at + extra, :]
+
+
+def halves(ref):
+    return ref.at[0], ref.at[1]
 
 
 def pair_body(b_even, b_odd, cc, message, to_above, to_below, ext):
@@ -441,8 +440,14 @@
     write_edges(message, to_above, to_below)
 
 
-def chain_body(message, below, above, source, cc, *refs):
+def halo_body(below, above, out):
+    out[0] = below[...]
+    out[1] = above[...]
+
+
+def chain_body(message, halo, source, cc, *refs):
     out, to_above, to_below, ext = refs[-4:]
+    below, above = halves(halo)
     few = ext.shape[1] - 16
     ext[...] = jnp.zeros_like(ext)
     read_message(ext, message, below, above)
@@ -454,18 +459,73 @@
 
 
 def collect_body(rounds, *refs):
-    messages, belows, aboves = [refs[k * rounds : (k + 1) * rounds] for k in range(3)]
-    total, ext = refs[3 * rounds + 2 :]
+    messages, halos = refs[:rounds], refs[rounds : 2 * rounds]
+    total, ext = refs[2 * rounds + 2 :]
     chip = lax.axis_index("cuts") // 2
     ext[...] = jnp.zeros_like(ext)
     for number in range(rounds):
 
         @pl.when(chip == number + 1)
         def _():
-            read_message(ext, messages[number], belows[number], aboves[number])
+            read_message(ext, messages[number], *halves(halos[number]))
 
     for i in range(6):
         total[i] = ext[i, 8 : ext.shape[1] - 8, :]
+
+
+def leap_body(message, halo, source, halo_source, cc, *refs):
+    out, ext, add = refs[-3:]
+    chip = lax.axis_index("cuts") // 2
+    rows = ext.shape[1]
+
+    @pl.when((chip == 1) | (chip == 2))
+    def _():
+        add[...] = jnp.zeros_like(add)
+        read_message(add, source, *halves(halo_source))
+
+    @pl.when(chip == 1)
+    def _():
+        ext[...] = jnp.zeros_like(ext)
+        read_message(ext, message, *halves(halo))
+        for i, value in enumerate(advance(ext, cc, 2)):
+            out[i] = (value + add[i])[4 : rows - 4]
+
+    @pl.when(chip == 2)
+    def _():
+        out[...] = add[:, 4 : rows - 4, :]
+
+
+def last_body(leaped, cc, out, ext):
+    rows = ext.shape[1]
+
+    @pl.when(lax.axis_index("cuts") // 2 == 3)
+    def _():
+        ext[...] = jnp.zeros_like(ext)
+        ext[:, 4 : rows - 4, :] = leaped[...]
+        for i, value in enumerate(advance(ext, cc, 2)):
+            out[i] = value
+
+
+def arrive_body(message, halo, last, step, *refs):
+    total, ext = refs[-2:]
+    chip = lax.axis_index("cuts") // 2
+    rows = ext.shape[1]
+    ext[...] = jnp.zeros_like(ext)
+
+    @pl.when(chip == 1)
+    def _():
+        read_message(ext, message, *halves(halo))
+
+    @pl.when(chip >= 2)
+    def _():
+        ext[:, 4 : rows - 4, :] = step[...]
+
+    @pl.when(chip == 3)
+    def _():
+        ext[...] += last[...]
+
+    for i in range(6):
+        total[i] = ext[i, 8 : rows - 8, :]
 
 
 def even_body(ext, b_even, cc, even_end):
@@ -540,26 +600,18 @@
     return [ref.at[i, end] for i in range(6) for end in ends]
 
 
-def early_body(inner, outer, after_hop, init, out, picked, slots, sem):
+def early_body(inner, outer, init, out, slots, sem):
     place = lax.axis_index("cuts")
     rows = out.shape[1]
     quarter = rows // 4
     middle = pl.ds(quarter, rows // 2)
 
-    @pl.when(place == 2)
-    def _():
-        picked[...] = after_hop[...]
-
-    @pl.when(place != 2)
-    def _():
-        picked[...] = outer[...]
-
     @pl.when(place != 0)
     def _():
         remainder(
             [inner.at[i] for i in range(6)], [out.at[i, middle] for i in range(6)], slots
         )
-        remainder(outer_parts(picked, quarter), outer_parts(out, quarter), slots)
+        remainder(outer_parts(outer, quarter), outer_parts(out, quarter), slots)
 
     @pl.when(place == 0)
     def _():
@@ -568,24 +620,46 @@
         copy.wait()
 
 
+def late_body(base_in, after_hop, base, slots, made, sems):
+    rows = base.shape[1]
+    quarter = rows // 4
+
+    @pl.when(lax.axis_index("cuts") == 2)
+    def _():
+        remainder(outer_parts(after_hop, quarter), outer_parts(made, quarter), slots)
+        copies = [
+            pltpu.make_async_copy(
+                made.at[:, pl.ds(n * quarter, quarter)],
+                base.at[:, pl.ds(start, quarter)],
+                sems.at[n],
+            )
+            for n, start in enumerate((0, rows - quarter))
+        ]
+        for copy in copies:
+            copy.start()
+        for copy in copies:
+            copy.wait()
+
+
 def correct_body(base, own, received, out, slots, made, sems):
     odd = lax.axis_index("cuts") % 2
+    cols = base.shape[2]
     copies = []
-    for lead in (0, 3):
+    for lead in range(0, 6, 2):
+        part = range(lead, lead + 2)
         values = []
-        for i in range(lead, lead + 3):
+        for i in part:
             value = jnp.where(odd == 1, received[i], own[i])
             values.append(value if i < 3 else value * (1.0 / SPEED))
-        part = [lead, lead + 1, lead + 2]
         spread_add(
             jnp.concatenate(values, axis=0),
             [base.at[i] for i in part],
             [made.at[i] for i in part],
-            slots,
+            slots.at[pl.ds(cols // LANES * lead, cols // LANES * 2)],
         )
         copies.append(
             pltpu.make_async_copy(
-                made.at[pl.ds(lead, 3)], out.at[pl.ds(lead, 3)], sems.at[lead // 3]
+                made.at[pl.ds(lead, 2)], out.at[pl.ds(lead, 2)], sems.at[lead // 2]
             )
         )
         copies[-1].start()
@@ -601,7 +675,9 @@
     few, half_cols = rows // 2, cols // 2
     state, coarse_state = (6, rows, cols), (6, few, half_cols)
     ext_state = (6, few + 16, half_cols)
-    edge = (6 * EDGE, half_cols)
+    leap = chips == 4
+    reach = 7 if leap else 3
+    edge = (6 * (reach + 1), half_cols)
     fields = (circ_stiff, axial_stiff, lumped_mass, hoop_stiff)
 
     def around_loop(value, by):
@@ -616,17 +692,43 @@
         return lax.ppermute(value, "cuts", pairs)
 
     def hop(value, by, chip):
-        a, b = 2 * chip, 2 * chip + 2
+        third = None
+        if chip > 0:
+            third = chip + 2 if chip + 2 < chips else chip - 1
+        used = {chip, chip + 1, third}
         pairs = []
         for s in range(strips):
             here, there = s * slices, (s + by) % strips * slices
-            pairs += [(here + a, there + b), (there + b, there + b + 1)]
-            pairs += [(there + b + 1, here + a + 1), (here + a + 1, here + a)]
-            pairs += [(here + j, here + (j ^ 1)) for j in range(slices) if not a <= j < a + 4]
+            a, b = here + 2 * chip, there + 2 * chip + 2
+            path = [a, b, b + 1]
+            if third is not None:
+                path += [there + 2 * third, there + 2 * third + 1]
+            path.append(a + 1)
+            pairs += list(zip(path, path[1:] + path[:1]))
+            pairs += [(here + j, here + (j ^ 1)) for j in range(slices) if j // 2 not in used]
+        assert sorted(target for _, target in pairs) == list(range(strips * slices))
         return lax.ppermute(value, ("strip", "cuts"), pairs)
 
-    def hop_with_edges(main, to_above, to_below, chip):
-        return hop(main, 0, chip), hop(to_above, 1, chip), hop(to_below, -1, chip)
+    def hop_with_edges(main, to_above, to_below, move):
+        edges = [move(to_above, 1), move(to_below, -1)]
+        (halo,) = run(
+            halo_body, "halo", [(2,) + edge], edges, cost=(HALO_COST, HALO_COST)
+        )
+        return move(main, 0), halo
+
+    def to_chip_1(value, by):
+        pairs = []
+        for s in range(strips):
+            here, there, beyond = (slices * ((s + k * by) % strips) for k in range(3))
+            path = [here, there + 2, beyond + 3, here + 1]
+            pairs += list(zip(path, path[1:] + path[:1]))
+            for j in range(4, slices, 2):
+                pairs += [(here + j, there + j + 1), (here + j + 1, here + j)]
+        assert sorted(target for _, target in pairs) == list(range(strips * slices))
+        return lax.ppermute(value, ("strip", "cuts"), pairs)
+
+    def around_cuts(value, *path):
+        return along_cuts(value, dict(zip(path, path[1:] + path[:1])))
 
     pack = (PACK_ROWS, cols)
     third = (3, rows, cols)
@@ -643,8 +745,8 @@
         + [middle_shape],
         [u, initial_state, *fields],
         [
-            pltpu.VMEM(ends_shape, F32),
-            halver_scratch(16, 16, cols),
+            pltpu.VMEM((6, 32, cols), F32),
+            halver_scratch(32, 16, cols),
             pltpu.SemaphoreType.DMA((7,)),
         ],
         specs=[HBM] * 6,
@@ -684,26 +786,45 @@
     (outer,) = run(outer_body, "outer", [outer_shape], [f, ends])
 
     previous = along_cuts(outer, {j: j + 1 for j in range(2, slices - 1)} | {slices - 1: 2})
-    at_end = source
-    arrived = []
-    for chip in range(chips - 1):
-        arrived.append(hop_with_edges(*at_end, chip))
-        if chip < chips - 2:
-            extra = {0: [raw], 1: [previous]}.get(chip, [])
-            at_end = run(
-                chain_body,
-                "chain",
-                [message, edge, edge],
-                [*arrived[-1], source[0], cc] + extra,
-                ext,
-                specs=[VMEM] * 5 + [ANY] * len(extra),
-            )
-        if chip == 0:
-            (part,) = run(
-                copy_body, "later", [outer_shape], [outer, at_end[1]], specs=[VMEM, ANY]
-            )
-            after_hop = lax.ppermute(part, "cuts", [(1, 2)])
-    messages, belows, aboves = zip(*arrived)
+    if leap:
+        main, halo = hop_with_edges(*source, to_chip_1)
+        halo_source = along_cuts(halo, {})
+        (leaped,) = run(
+            leap_body,
+            "leap",
+            [(6, few + 8, half_cols)],
+            [main, halo, source[0], halo_source, cc, raw],
+            ext * 2,
+            specs=[VMEM] * 5 + [ANY],
+        )
+        after_leap = leaped
+        to_chip_3 = around_cuts(leaped, 2, 6, 7, 3)
+        to_next = around_cuts(leaped, 2, 4, 6, 7, 5, 3)
+        (last,) = run(
+            last_body, "last", [ext_state], [to_chip_3, cc], ext, cost=(LAST_COST, LAST_COST)
+        )
+        close, received_by_chain = arrive_body, [main, halo, last, to_next]
+    else:
+        at_end = source
+        arrived = []
+        for chip in range(chips - 1):
+            arrived.append(hop_with_edges(*at_end, lambda value, by: hop(value, by, chip)))
+            if chip < chips - 2:
+                extra = {0: [raw], 1: [previous]}.get(chip, [])
+                at_end = run(
+                    chain_body,
+                    "chain",
+                    [message, edge, edge],
+                    [*arrived[-1], source[0], cc] + extra,
+                    ext,
+                    specs=[VMEM] * 4 + [ANY] * len(extra),
+                )
+            if chip == 0:
+                after_leap = at_end[1]
+        messages, halos = zip(*arrived)
+        close, received_by_chain = lambda *refs: collect_body(chips - 1, *refs), [*messages, *halos]
+    (part,) = run(copy_body, "later", [outer_shape], [outer, after_leap], specs=[VMEM, ANY])
+    after_hop = lax.ppermute(part, "cuts", [(1, 2)])
     (fine_end,) = run(
         join_body,
         "join",
@@ -723,32 +844,45 @@
         cost=(0, 6 * rows * cols * 8),
     )
     rem_scratch = [
-        halver_scratch(12, rows, cols),
+        halver_scratch(6, rows, cols),
         pltpu.VMEM(state, F32),
-        pltpu.SemaphoreType.DMA((2,)),
+        pltpu.SemaphoreType.DMA((3,)),
     ]
     (base,) = run(
         early_body,
         "remainder",
         [state],
-        [inner, previous, after_hop, initial_state],
+        [inner, previous, initial_state],
         [
-            pltpu.VMEM(outer_shape, F32),
             halver_scratch(12, few, cols),
             pltpu.SemaphoreType.DMA,
         ],
-        specs=[VMEM] * 3 + [HBM],
+        specs=[VMEM] * 2 + [HBM],
         cost=(0, 6 * rows * cols * 8),
     )
-    total, wide = run(
-        lambda *refs: collect_body(chips - 1, *refs),
+    total, ended = run(
+        close,
         "collect",
         [coarse_state, ext_state],
-        [*messages, *belows, *aboves, base, fine_end],
-        specs=[VMEM] * (3 * len(messages)) + [ANY, HBM],
-    )
-    (even_end,) = run(even_body, "even", [coarse_state], [wide, b, cc])
+        [*received_by_chain, base, fine_end],
+        specs=[VMEM] * len(received_by_chain) + [ANY, HBM],
+    )
+    (even_end,) = run(even_body, "even", [coarse_state], [ended, b, cc])
     received = along_cuts(even_end, {})
+    (base,) = run(
+        late_body,
+        "late",
+        [state],
+        [base, after_hop],
+        [
+            halver_scratch(12, rows // 4, cols),
+            pltpu.VMEM(outer_shape, F32),
+            pltpu.SemaphoreType.DMA((2,)),
+        ],
+        specs=[ANY, VMEM],
+        out_specs=[ANY],
+        aliases={0: 0},
+    )
     (new_start,) = run(
         correct_body,
         "correct",

time: 45.5 us -> 43 us (0.945)
  the two profiles are of different devices: /device:TPU:27 before, /device:TPU:9 now
where the time goes in v4:
time: 43 us; the launch traced here: 42.8 us
  Pallas kernels  15.4 us (36%)
  waiting for transfers between devices  14.6 us (34%)
  starting transfers between devices  12.1 us (28%)
  between operations  0.79 us (2%)
    pallas_call x16, Pallas kernels, run(): pl.pallas_call(body, name=name, out_shape=[jax.ShapeDtypeStruct(shape, F3...  15.4 us
    ppermute x7, waiting for transfers between devices, along_cuts(): return lax.ppermute(value, 'cuts', pairs)  11.3 us
    ppermute x7, starting transfers between devices, along_cuts(): return lax.ppermute(value, 'cuts', pairs)  6.35 us
    ppermute x3, waiting for transfers between devices, to_chip_1(): return lax.ppermute(value, ('strip', 'cuts'), pairs)  3.26 us
    ppermute x3, starting transfers between devices, to_chip_1(): return lax.ppermute(value, ('strip', 'cuts'), pairs)  2.65 us
    ppermute x2, starting transfers between devices, around_loop(): return lax.ppermute(value, 'strip', pairs)  2.36 us
  transfers between devices with their start and end apart: 13, of which 7 were waited for; matrix products, arithmetic and copies ran while one was open for 0% of the time, Pallas kernels for 27%

profile of v4, /device:TPU:9, one launch (start us, length us, event | category | flops | bytes accessed | tf_op | source)
XLA Modules:
  0.0 42.8 jit_solution(4942319275653266320)
XLA Ops:
  0.6 2.4 %pack.1 = (f32[40,512]{1,0:T(8,128)S(1)}, f32[40,512]{1,0:T(8,128)S(1)}, f32[10,16,512]{2,1,0:T(8,128)S(1)}, f32[10,8,256]{2,1,0:T(8,128)S(1)}, f32[6,128,512]{2...) custom-call(f32[6,128,512]{2,1,0:T(8,128)} %bitcast.4, ...), custom_call_target="tpu_custom_call" | custom-call | tf_op jit(solution)/shard_map/pack/pallas_call | solution.py:35
  3.1 1.9 %collective-permute-start = (f32[6,80,512]{2,1,0:T(8,128)S(1)}, f32[6,80,512]{2,1,0:T(8,128)S(1)}, u32[]{:S(2)}, u32[]{:S(2)}) collective-permute-start(f32[6,80,512]{2,1,0:T(8,128)S(1)} %get-tuple-element.24), channel_id=1, source_target_pairs={{0,1},{1,2},{2,3},{3,4},{4,5},{5,6},{6,7},{7,0},{8,9},{9,10},{10,1... | collective-permute-start | bytes 2949128 | tf_op jit(solution)/shard_map/ppermute | solution.py:692
  5.0 1.2 %collective-permute-start.1 = (f32[40,512]{1,0:T(8,128)S(1)}, f32[40,512]{1,0:T(8,128)S(1)}, u32[]{:S(2)}, u32[]{:S(2)}) collective-permute-start(f32[40,512]{1,0:T(8,128)S(1)} %get-tuple-element.36), channel_id=1, source_target_pairs={{0,8},{8,16},{16,24},{24,0},{1,9},{9,17},{17,25},{25,1},{2,10},{10... | collective-permute-start | bytes 245768 | tf_op jit(solution)/shard_map/ppermute | solution.py:685
  6.2 1.2 %collective-permute-start.2 = (f32[40,512]{1,0:T(8,128)S(1)}, f32[40,512]{1,0:T(8,128)S(1)}, u32[]{:S(2)}, u32[]{:S(2)}) collective-permute-start(f32[40,512]{1,0:T(8,128)S(1)} %get-tuple-element.37), channel_id=1, source_target_pairs={{0,24},{8,0},{16,8},{24,16},{1,25},{9,1},{17,9},{25,17},{2,26},{10... | collective-permute-start | bytes 245768 | tf_op jit(solution)/shard_map/ppermute | solution.py:685
  7.3 4.2 %interior.1 = (f32[6,128,512]{2,1,0:T(8,128)S(1)}, f32[6,64,256]{2,1,0:T(8,128)S(1)}, f32[7,80,256]{2,1,0:T(8,128)S(1)}, f32[7,128,512]{2,1,0:T(8,128)S(1)}) custom-call(f32[6,128,512]{2,1,0:T(8,128)S(1)} %get-tuple-element.25.u, f32[6,128,512]{2,1,0:T(8,128)} %init.5, f32[128,512]{1,0:T(8,128)S(1)} %get-tuple-element.26.kc, ...), custom_call_target="tpu_custom_call" | custom-call | tf_op jit(solution)/shard_map/interior/pallas_call | solution.py:35
  11.6 0.0 collective-permute-done.1.from_below
  11.6 0.0 collective-permute-done.2.from_above
  11.6 0.8 %edges.1 = (f32[6,16,512]{2,1,0:T(8,128)S(1)}, f32[6,64,256]{2,1,0:T(8,128)S(1)}, f32[7,80,256]{2,1,0:T(8,128)S(1)}) custom-call(f32[6,128,512]{2,1,0:T(8,128)S(1)} %get-tuple-element.31.f, f32[10,16,512]{2,1,0:T(8,128)S(1)} %get-tuple-element.32.own, f32[10,8,256]{2,1,0:T(8,128)S(1)} %get-tuple-element.33.own_coarse, ...), custom_call_target="tpu_custom_call" | custom-call | tf_op jit(solution)/shard_map/edges/pallas_call | solution.py:35
  12.5 0.1 collective-permute-start.4
  12.5 1.7 %collective-permute-done.4.b_odd = f32[6,64,256]{2,1,0:T(8,128)S(1)} collective-permute-done((f32[6,64,256]{2,1,0:T(8,128)S(1)}, f32[6,64,256]{2,1,0:T(8,128)S(1)}, u32[]{:S(2)}, u32[]{:S(2)}) %collective-permute-start.4) | collective-permute-done | bytes 393248 | tf_op jit(solution)/shard_map/ppermute | solution.py:692
  14.3 0.5 %pair.1 = (f32[408,256]{1,0:T(8,128)S(1)}, f32[48,256]{1,0:T(8,128)S(1)}, f32[48,256]{1,0:T(8,128)S(1)}) custom-call(f32[6,64,256]{2,1,0:T(8,128)S(1)} %get-tuple-element.39.b_even, f32[6,64,256]{2,1,0:T(8,128)S(1)} %collective-permute-done.4.b_odd, f32[7,80,256]{2,1,0:T(8,128)S(1)} %get-tuple-element.40.cc), custom_call_target="tpu_custom_call" | custom-call | tf_op jit(solution)/shard_map/pair/pallas_call | solution.py:35
  14.8 1.2 %collective-permute-start.6 = (f32[48,256]{1,0:T(8,128)S(1)}, f32[48,256]{1,0:T(8,128)S(1)}, u32[]{:S(2)}, u32[]{:S(2)}) collective-permute-start(f32[48,256]{1,0:T(8,128)S(1)} %get-tuple-element.42), channel_id=1, source_target_pairs={{0,10},{10,19},{19,1},{1,0},{4,13},{5,4},{6,15},{7,6},{8,18},{18,2... | collective-permute-start | bytes 147464 | tf_op jit(solution)/shard_map/ppermute | solution.py:728
  16.0 0.1 collective-permute-start.7
  16.1 1.3 %collective-permute-start.5 = (f32[408,256]{1,0:T(8,128)S(1)}, f32[408,256]{1,0:T(8,128)S(1)}, u32[]{:S(2)}, u32[]{:S(2)}) collective-permute-start(f32[408,256]{1,0:T(8,128)S(1)} %get-tuple-element.41.source), channel_id=1, source_target_pairs={{0,2},{2,3},{3,1},{1,0},{4,5},{5,4},{6,7},{7,6},{8,10},{10,11},{11... | collective-permute-start | bytes 1253384 | tf_op jit(solution)/shard_map/ppermute | solution.py:728
  17.4 0.1 outer.1.value
  17.5 0.4 %collective-permute-start.3 = (f32[6,64,512]{2,1,0:T(8,128)S(1)}, f32[6,64,512]{2,1,0:T(8,128)S(1)}, u32[]{:S(2)}, u32[]{:S(2)}) collective-permute-start(f32[6,64,512]{2,1,0:T(8,128)S(1)} %outer.1.value), channel_id=1, source_target_pairs={{2,3},{3,4},{4,5},{5,6},{6,7},{7,2},{0,1},{1,0},{10,11},{11,12},{1... | collective-permute-start | bytes 2359304 | tf_op jit(solution)/shard_map/ppermute | solution.py:692
  17.9 1.3 %collective-permute-done.6.below = f32[48,256]{1,0:T(8,128)S(1)} collective-permute-done((f32[48,256]{1,0:T(8,128)S(1)}, f32[48,256]{1,0:T(8,128)S(1)}, u32[]{:S(2)}, u32[]{:S(2)}) %collective-permute-start.6) | collective-permute-done | bytes 49184 | tf_op jit(solution)/shard_map/ppermute | solution.py:728
  19.3 1.9 %collective-permute-done.7.above = f32[48,256]{1,0:T(8,128)S(1)} collective-permute-done((f32[48,256]{1,0:T(8,128)S(1)}, f32[48,256]{1,0:T(8,128)S(1)}, u32[]{:S(2)}, u32[]{:S(2)}) %collective-permute-start.7) | collective-permute-done | bytes 49184 | tf_op jit(solution)/shard_map/ppermute | solution.py:728
  21.2 0.4 %collective-permute-start.8 = (f32[2,48,256]{2,1,0:T(8,128)S(1)}, f32[2,48,256]{2,1,0:T(8,128)S(1)}, u32[]{:S(2)}, u32[]{:S(2)}) collective-permute-start(f32[2,48,256]{2,1,0:T(8,128)S(1)} %halo.1), channel_id=1, source_target_pairs={{0,1},{1,0},{2,3},{3,2},{4,5},{5,4},{6,7},{7,6},{8,9},{9,8},{10,11... | collective-permute-start | bytes 294920 | tf_op jit(solution)/shard_map/ppermute | solution.py:692
  21.6 0.9 %collective-permute-done.8.halo_source = f32[2,48,256]{2,1,0:T(8,128)S(1)} collective-permute-done((f32[2,48,256]{2,1,0:T(8,128)S(1)}, f32[2,48,256]{2,1,0:T(8,128)S(1)}, u32[]{:S(2)}, u32[]{:S(2)}) %collective-permute-start.8) | collective-permute-done | bytes 98336 | tf_op jit(solution)/shard_map/ppermute | solution.py:692
  22.6 0.0 collective-permute-done.5.message
  22.6 0.0 collective-permute-done.u.refs_0_
  22.6 0.9 %leap.1.after = f32[6,72,256]{2,1,0:T(8,128)S(1)} custom-call(f32[408,256]{1,0:T(8,128)S(1)} %collective-permute-done.5.message, f32[2,48,256]{2,1,0:T(8,128)S(1)} %halo.1, f32[408,256]{1,0:T(8,128)S(1)} %get-tuple-element.41.source, f32[2,48,256]{2,1,0:T(8,128)S(1)} %collective-permute-done.8.halo_source, f32[7,80,256]{2,1,0:T(8,128)S(1)} %get-tuple-element.40.cc, ...), custom_call_target="tpu_custom_call" | custom-call | tf_op jit(solution)/shard_map/leap/pallas_call | solution.py:35
  23.5 3.4 %collective-permute-start.10 = (f32[6,72,256]{2,1,0:T(8,128)S(1)}, f32[6,72,256]{2,1,0:T(8,128)S(1)}, u32[]{:S(2)}, u32[]{:S(2)}) collective-permute-start(f32[6,72,256]{2,1,0:T(8,128)S(1)} %leap.1.after), channel_id=1, source_target_pairs={{2,6},{6,7},{7,3},{3,2},{0,1},{1,0},{4,5},{5,4},{10,14},{14,15},{1... | collective-permute-start | bytes 1327112 | tf_op jit(solution)/shard_map/ppermute | solution.py:692
  26.9 0.1 collective-permute-start.11
  26.9 0.1 later.1
  27.0 0.7 %collective-permute-start.9 = (f32[6,64,512]{2,1,0:T(8,128)S(1)}, f32[6,64,512]{2,1,0:T(8,128)S(1)}, u32[]{:S(2)}, u32[]{:S(2)}) collective-permute-start(f32[6,64,512]{2,1,0:T(8,128)S(1)} %later.1), channel_id=1, source_target_pairs={{1,2},{9,10},{17,18},{25,26}} | collective-permute-start | bytes 2359304 | tf_op jit(solution)/shard_map/ppermute | solution.py:827
  27.7 1.2 %join.1.refs_1_ = f32[6,128,512]{2,1,0:T(8,128)} custom-call(f32[6,128,512]{2,1,0:T(8,128)S(1)} %get-tuple-element.31.f, f32[6,16,512]{2,1,0:T(8,128)S(1)} %get-tuple-element.38.ends), custom_call_target="tpu_custom_call" | custom-call | bytes 3145728 | tf_op jit(solution)/shard_map/join/pallas_call | solution.py:35
  28.9 1.2 %again.1.inner = f32[6,64,512]{2,1,0:T(8,128)S(1)} custom-call(f32[6,80,512]{2,1,0:T(8,128)S(1)} %collective-permute-done.u.refs_0_, f32[7,128,512]{2,1,0:T(8,128)S(1)} %get-tuple-element.30.cf), custom_call_target="tpu_custom_call" | custom-call | bytes 3145728 | tf_op jit(solution)/shard_map/again/pallas_call | solution.py:35
  30.1 0.0 collective-permute-done.3.outer
  30.1 1.8 %remainder.1.base_in.refs_0_ = f32[6,128,512]{2,1,0:T(8,128)S(1)} custom-call(f32[6,64,512]{2,1,0:T(8,128)S(1)} %again.1.inner, f32[6,64,512]{2,1,0:T(8,128)S(1)} %collective-permute-done.3.outer, f32[6,128,512]{2,1,0:T(8,128)} %init.5), custom_call_target="tpu_custom_call" | custom-call | bytes 3145728 | tf_op jit(solution)/shard_map/remainder/pallas_call | solution.py:35
  31.9 2.1 %collective-permute-done.10.leaped = f32[6,72,256]{2,1,0:T(8,128)S(1)} collective-permute-done((f32[6,72,256]{2,1,0:T(8,128)S(1)}, f32[6,72,256]{2,1,0:T(8,128)S(1)}, u32[]{:S(2)}, u32[]{:S(2)}) %collective-permute-start.10) | collective-permute-done | bytes 442400 | tf_op jit(solution)/shard_map/ppermute | solution.py:692
  34.0 4.9 %collective-permute-done.11.step = f32[6,72,256]{2,1,0:T(8,128)S(1)} collective-permute-done((f32[6,72,256]{2,1,0:T(8,128)S(1)}, f32[6,72,256]{2,1,0:T(8,128)S(1)}, u32[]{:S(2)}, u32[]{:S(2)}) %collective-permute-start.11) | collective-permute-done | bytes 442400 | tf_op jit(solution)/shard_map/ppermute | solution.py:692
  38.9 0.1 collect.1
  39.0 0.5 %even.1 = f32[6,64,256]{2,1,0:T(8,128)S(1)} custom-call(f32[6,80,256]{2,1,0:T(8,128)S(1)} %get-tuple-element.45.ext, f32[6,64,256]{2,1,0:T(8,128)S(1)} %get-tuple-element.39.b_even, f32[7,80,256]{2,1,0:T(8,128)S(1)} %get-tuple-element.40.cc), custom_call_target="tpu_custom_call" | custom-call | tf_op jit(solution)/shard_map/even/pallas_call | solution.py:35
  39.5 0.1 collective-permute-start.12
  39.6 0.0 collective-permute-done.9.after_hop
  39.7 1.7 %collective-permute-done.12.received = f32[6,64,256]{2,1,0:T(8,128)S(1)} collective-permute-done((f32[6,64,256]{2,1,0:T(8,128)S(1)}, f32[6,64,256]{2,1,0:T(8,128)S(1)}, u32[]{:S(2)}, u32[]{:S(2)}) %collective-permute-start.12) | collective-permute-done | bytes 393248 | tf_op jit(solution)/shard_map/ppermute | solution.py:692
  41.3 1.5 %correct.1 = f32[6,128,512]{2,1,0:T(8,128)} custom-call(f32[6,128,512]{2,1,0:T(8,128)S(1)} %late.1.base, f32[6,64,256]{2,1,0:T(8,128)S(1)} %get-tuple-element.44.own, f32[6,64,256]{2,1,0:T(8,128)S(1)} %collective-permute-done.12.received), custom_call_target="tpu_custom_call" | custom-call | tf_op jit(solution)/shard_map/correct/pallas_call | solution.py:35
  (3 shorter events, 0.0 us)
Async XLA Ops:
  3.1 19.5 %collective-permute-start = (f32[6,80,512]{2,1,0:T(8,128)S(1)}, f32[6,80,512]{2,1,0:T(8,128)S(1)}, u32[]{:S(2)}, u32[]{:S(2)}) collective-permute-start(f32[6,80,512]{2,1,0:T(8,128)S(1)} %get-tuple-element.24), channel_id=1, source_target_pairs={{0,1},{1,2},{2,3},{3,4},{4,5},{5,6},{6,7},{7,0},{8,9},{9,10},{10,1... | collective-permute-start | bytes 2949128 | tf_op jit(solution)/shard_map/ppermute | solution.py:692
  5.0 6.6 %collective-permute-start.1 = (f32[40,512]{1,0:T(8,128)S(1)}, f32[40,512]{1,0:T(8,128)S(1)}, u32[]{:S(2)}, u32[]{:S(2)}) collective-permute-start(f32[40,512]{1,0:T(8,128)S(1)} %get-tuple-element.36), channel_id=1, source_target_pairs={{0,8},{8,16},{16,24},{24,0},{1,9},{9,17},{17,25},{25,1},{2,10},{10... | collective-permute-start | bytes 245768 | tf_op jit(solution)/shard_map/ppermute | solution.py:685
  6.2 5.4 %collective-permute-start.2 = (f32[40,512]{1,0:T(8,128)S(1)}, f32[40,512]{1,0:T(8,128)S(1)}, u32[]{:S(2)}, u32[]{:S(2)}) collective-permute-start(f32[40,512]{1,0:T(8,128)S(1)} %get-tuple-element.37), channel_id=1, source_target_pairs={{0,24},{8,0},{16,8},{24,16},{1,25},{9,1},{17,9},{25,17},{2,26},{10... | collective-permute-start | bytes 245768 | tf_op jit(solution)/shard_map/ppermute | solution.py:685
  12.5 1.8 %collective-permute-start.4 = (f32[6,64,256]{2,1,0:T(8,128)S(1)}, f32[6,64,256]{2,1,0:T(8,128)S(1)}, u32[]{:S(2)}, u32[]{:S(2)}) collective-permute-start(f32[6,64,256]{2,1,0:T(8,128)S(1)} %get-tuple-element.39.b_even), channel_id=1, source_target_pairs={{0,1},{1,0},{2,3},{3,2},{4,5},{5,4},{6,7},{7,6},{8,9},{9,8},{10,11... | collective-permute-start | bytes 1179656 | tf_op jit(solution)/shard_map/ppermute | solution.py:692
  14.8 4.5 %collective-permute-start.6 = (f32[48,256]{1,0:T(8,128)S(1)}, f32[48,256]{1,0:T(8,128)S(1)}, u32[]{:S(2)}, u32[]{:S(2)}) collective-permute-start(f32[48,256]{1,0:T(8,128)S(1)} %get-tuple-element.42), channel_id=1, source_target_pairs={{0,10},{10,19},{19,1},{1,0},{4,13},{5,4},{6,15},{7,6},{8,18},{18,2... | collective-permute-start | bytes 147464 | tf_op jit(solution)/shard_map/ppermute | solution.py:728
  16.0 5.2 %collective-permute-start.7 = (f32[48,256]{1,0:T(8,128)S(1)}, f32[48,256]{1,0:T(8,128)S(1)}, u32[]{:S(2)}, u32[]{:S(2)}) collective-permute-start(f32[48,256]{1,0:T(8,128)S(1)} %get-tuple-element.43), channel_id=1, source_target_pairs={{0,26},{26,19},{19,1},{1,0},{4,29},{5,4},{6,31},{7,6},{8,2},{2,27}... | collective-permute-start | bytes 147464 | tf_op jit(solution)/shard_map/ppermute | solution.py:728
  16.1 6.5 %collective-permute-start.5 = (f32[408,256]{1,0:T(8,128)S(1)}, f32[408,256]{1,0:T(8,128)S(1)}, u32[]{:S(2)}, u32[]{:S(2)}) collective-permute-start(f32[408,256]{1,0:T(8,128)S(1)} %get-tuple-element.41.source), channel_id=1, source_target_pairs={{0,2},{2,3},{3,1},{1,0},{4,5},{5,4},{6,7},{7,6},{8,10},{10,11},{11... | collective-permute-start | bytes 1253384 | tf_op jit(solution)/shard_map/ppermute | solution.py:728
  17.5 12.6 %collective-permute-start.3 = (f32[6,64,512]{2,1,0:T(8,128)S(1)}, f32[6,64,512]{2,1,0:T(8,128)S(1)}, u32[]{:S(2)}, u32[]{:S(2)}) collective-permute-start(f32[6,64,512]{2,1,0:T(8,128)S(1)} %outer.1.value), channel_id=1, source_target_pairs={{2,3},{3,4},{4,5},{5,6},{6,7},{7,2},{0,1},{1,0},{10,11},{11,12},{1... | collective-permute-start | bytes 2359304 | tf_op jit(solution)/shard_map/ppermute | solution.py:692
  21.2 1.4 %collective-permute-start.8 = (f32[2,48,256]{2,1,0:T(8,128)S(1)}, f32[2,48,256]{2,1,0:T(8,128)S(1)}, u32[]{:S(2)}, u32[]{:S(2)}) collective-permute-start(f32[2,48,256]{2,1,0:T(8,128)S(1)} %halo.1), channel_id=1, source_target_pairs={{0,1},{1,0},{2,3},{3,2},{4,5},{5,4},{6,7},{7,6},{8,9},{9,8},{10,11... | collective-permute-start | bytes 294920 | tf_op jit(solution)/shard_map/ppermute | solution.py:692
  23.5 10.5 %collective-permute-start.10 = (f32[6,72,256]{2,1,0:T(8,128)S(1)}, f32[6,72,256]{2,1,0:T(8,128)S(1)}, u32[]{:S(2)}, u32[]{:S(2)}) collective-permute-start(f32[6,72,256]{2,1,0:T(8,128)S(1)} %leap.1.after), channel_id=1, source_target_pairs={{2,6},{6,7},{7,3},{3,2},{0,1},{1,0},{4,5},{5,4},{10,14},{14,15},{1... | collective-permute-start | bytes 1327112 | tf_op jit(solution)/shard_map/ppermute | solution.py:692
  26.9 12.1 %collective-permute-start.11 = (f32[6,72,256]{2,1,0:T(8,128)S(1)}, f32[6,72,256]{2,1,0:T(8,128)S(1)}, u32[]{:S(2)}, u32[]{:S(2)}) collective-permute-start(f32[6,72,256]{2,1,0:T(8,128)S(1)} %leap.1.after), channel_id=1, source_target_pairs={{2,4},{4,6},{6,7},{7,5},{5,3},{3,2},{0,1},{1,0},{10,12},{12,14},{1... | collective-permute-start | bytes 1327112 | tf_op jit(solution)/shard_map/ppermute | solution.py:692
  27.0 12.6 %collective-permute-start.9 = (f32[6,64,512]{2,1,0:T(8,128)S(1)}, f32[6,64,512]{2,1,0:T(8,128)S(1)}, u32[]{:S(2)}, u32[]{:S(2)}) collective-permute-start(f32[6,64,512]{2,1,0:T(8,128)S(1)} %later.1), channel_id=1, source_target_pairs={{1,2},{9,10},{17,18},{25,26}} | collective-permute-start | bytes 2359304 | tf_op jit(solution)/shard_map/ppermute | solution.py:827
  39.5 1.8 %collective-permute-start.12 = (f32[6,64,256]{2,1,0:T(8,128)S(1)}, f32[6,64,256]{2,1,0:T(8,128)S(1)}, u32[]{:S(2)}, u32[]{:S(2)}) collective-permute-start(f32[6,64,256]{2,1,0:T(8,128)S(1)} %even.1), channel_id=1, source_target_pairs={{0,1},{1,0},{2,3},{3,2},{4,5},{5,4},{6,7},{7,6},{8,9},{9,8},{10,11... | collective-permute-start | bytes 1179656 | tf_op jit(solution)/shard_map/ppermute | solution.py:692

commit v5 on v4

--- a/solution.py
+++ b/solution.py
@@ -16,7 +16,7 @@
 FINE_TOTAL = sum(FINE_ROWS)
 PACK_ROWS = -(-(FINE_TOTAL + -(-sum(COARSE_ROWS) // 2)) // 8) * 8
 CHUNK = 16
-HALO_COST = int(3.4e9)
+HALO_COST = int(2e9)
 LAST_COST = int(1e9)
 MARGIN = 8
 
@@ -164,11 +164,12 @@
     rows, cols = kc.shape
     pair_sum = Halver(slots)
     first = is_first()
-    copies = [
+    copies = [(kc_far, kc), (ka_far, ka), (mass_far, mass), (hoop_far, hoop)]
+    copies += [
         (init.at[:, start : start + 16], early.at[:, pl.ds(16 * end, 16)])
         for end, start in enumerate((0, rows - 16))
     ]
-    copies += [(u_far, u), (kc_far, kc), (ka_far, ka), (mass_far, mass), (hoop_far, hoop)]
+    copies.append((u_far, u))
     copies = [
         pltpu.make_async_copy(source, target, sems.at[n])
         for n, (source, target) in enumerate(copies)
@@ -420,16 +421,26 @@
     return ref.at[0], ref.at[1]
 
 
-def pair_body(b_even, b_odd, cc, message, to_above, to_below, ext):
+def pair_body(b, b_other, cc, message, to_above, to_below, ext, late):
     few = ext.shape[1] - 16
     top = 8 + few
-    for i in range(6):
-        ext[i, 0:8, :] = jnp.zeros_like(ext[i, 0:8, :])
-        ext[i, 8:top, :] = b_even[i]
-        ext[i, top : top + 8, :] = jnp.zeros_like(ext[i, 0:8, :])
+    odd = lax.axis_index("cuts") % 2
+    ext[:, 0:8, :] = jnp.zeros_like(ext[:, 0:8, :])
+    ext[:, top : top + 8, :] = jnp.zeros_like(ext[:, 0:8, :])
+
+    @pl.when(odd == 0)
+    def _():
+        ext[:, 8:top, :] = b[...]
+        late[...] = b_other[...]
+
+    @pl.when(odd == 1)
+    def _():
+        ext[:, 8:top, :] = b_other[...]
+        late[...] = b[...]
+
     for i, value in enumerate(advance(ext, cc, 1)):
         own, beyond = i * few, 6 * few + 4 * i
-        message[own : own + few, :] = value[8:top] + b_odd[i]
+        message[own : own + few, :] = value[8:top] + late[i]
         if i < 3:
             message[beyond : beyond + 1, :] = value[7:8]
             message[beyond + 1 : beyond + 2, :] = value[top : top + 1]
@@ -721,6 +732,8 @@
         for s in range(strips):
             here, there, beyond = (slices * ((s + k * by) % strips) for k in range(3))
             path = [here, there + 2, beyond + 3, here + 1]
+            if by:
+                path = [here + 1, there + 2, beyond + 3, here]
             pairs += list(zip(path, path[1:] + path[:1]))
             for j in range(4, slices, 2):
                 pairs += [(here + j, there + j + 1), (here + j + 1, here + j)]
@@ -782,7 +795,13 @@
     )
     ext = [pltpu.VMEM(ext_state, F32)]
     b_other = along_cuts(b, {})
-    source = run(pair_body, "pair", [message, edge, edge], [b, b_other, cc], ext)
+    source = run(
+        pair_body,
+        "pair",
+        [message, edge, edge],
+        [b, b_other, cc],
+        ext + [pltpu.VMEM(coarse_state, F32)],
+    )
     (outer,) = run(outer_body, "outer", [outer_shape], [f, ends])
 
     previous = along_cuts(outer, {j: j + 1 for j in range(2, slices - 1)} | {slices - 1: 2})

time: 43 us -> 42.8 us (level)
  the two profiles are of different devices: /device:TPU:9 before, /device:TPU:11 now
where the time goes in v5:
time: 42.8 us; the launch traced here: 42.6 us
  waiting for transfers between devices  16.5 us (39%)
  Pallas kernels  15.4 us (36%)
  starting transfers between devices  9.96 us (23%)
  between operations  0.77 us (2%)
    pallas_call x16, Pallas kernels, run(): pl.pallas_call(body, name=name, out_shape=[jax.ShapeDtypeStruct(shape, F3...  15.4 us
    ppermute x7, waiting for transfers between devices, along_cuts(): return lax.ppermute(value, 'cuts', pairs)  11.1 us
    ppermute x7, starting transfers between devices, along_cuts(): return lax.ppermute(value, 'cuts', pairs)  6.13 us
    ppermute x3, waiting for transfers between devices, to_chip_1(): return lax.ppermute(value, ('strip', 'cuts'), pairs)  4.85 us
    ppermute x3, starting transfers between devices, to_chip_1(): return lax.ppermute(value, ('strip', 'cuts'), pairs)  1.65 us
    ppermute x2, starting transfers between devices, around_loop(): return lax.ppermute(value, 'strip', pairs)  1.47 us
  transfers between devices with their start and end apart: 13, of which 8 were waited for; matrix products, arithmetic and copies ran while one was open for 0% of the time, Pallas kernels for 27%

profile of v5, /device:TPU:11, one launch (start us, length us, event | category | flops | bytes accessed | tf_op | source)
XLA Modules:
  0.0 42.6 jit_solution(10625050899077296422)
XLA Ops:
  0.6 2.4 %pack.1 = (f32[40,512]{1,0:T(8,128)S(1)}, f32[40,512]{1,0:T(8,128)S(1)}, f32[10,16,512]{2,1,0:T(8,128)S(1)}, f32[10,8,256]{2,1,0:T(8,128)S(1)}, f32[6,128,512]{2...) custom-call(f32[6,128,512]{2,1,0:T(8,128)} %bitcast.4, ...), custom_call_target="tpu_custom_call" | custom-call | tf_op jit(solution)/shard_map/pack/pallas_call | solution.py:35
  3.1 1.9 %collective-permute-start = (f32[6,80,512]{2,1,0:T(8,128)S(1)}, f32[6,80,512]{2,1,0:T(8,128)S(1)}, u32[]{:S(2)}, u32[]{:S(2)}) collective-permute-start(f32[6,80,512]{2,1,0:T(8,128)S(1)} %get-tuple-element.24), channel_id=1, source_target_pairs={{0,1},{1,2},{2,3},{3,4},{4,5},{5,6},{6,7},{7,0},{8,9},{9,10},{10,1... | collective-permute-start | bytes 2949128 | tf_op jit(solution)/shard_map/ppermute | solution.py:703
  5.0 1.2 %collective-permute-start.1 = (f32[40,512]{1,0:T(8,128)S(1)}, f32[40,512]{1,0:T(8,128)S(1)}, u32[]{:S(2)}, u32[]{:S(2)}) collective-permute-start(f32[40,512]{1,0:T(8,128)S(1)} %get-tuple-element.36), channel_id=1, source_target_pairs={{0,8},{8,16},{16,24},{24,0},{1,9},{9,17},{17,25},{25,1},{2,10},{10... | collective-permute-start | bytes 245768 | tf_op jit(solution)/shard_map/ppermute | solution.py:696
  6.2 0.3 collective-permute-start.2
  6.5 4.2 %interior.1 = (f32[6,128,512]{2,1,0:T(8,128)S(1)}, f32[6,64,256]{2,1,0:T(8,128)S(1)}, f32[7,80,256]{2,1,0:T(8,128)S(1)}, f32[7,128,512]{2,1,0:T(8,128)S(1)}) custom-call(f32[6,128,512]{2,1,0:T(8,128)S(1)} %get-tuple-element.25.u, f32[6,128,512]{2,1,0:T(8,128)} %init.5, f32[128,512]{1,0:T(8,128)S(1)} %get-tuple-element.26.kc, ...), custom_call_target="tpu_custom_call" | custom-call | tf_op jit(solution)/shard_map/interior/pallas_call | solution.py:35
  10.7 0.0 collective-permute-done.1.from_below
  10.7 0.5 %collective-permute-done.2.from_above = f32[40,512]{1,0:T(8,128)S(1)} collective-permute-done((f32[40,512]{1,0:T(8,128)S(1)}, f32[40,512]{1,0:T(8,128)S(1)}, u32[]{:S(2)}, u32[]{:S(2)}) %collective-permute-start.2) | collective-permute-done | bytes 81952 | tf_op jit(solution)/shard_map/ppermute | solution.py:696
  11.2 0.8 %edges.1 = (f32[6,16,512]{2,1,0:T(8,128)S(1)}, f32[6,64,256]{2,1,0:T(8,128)S(1)}, f32[7,80,256]{2,1,0:T(8,128)S(1)}) custom-call(f32[6,128,512]{2,1,0:T(8,128)S(1)} %get-tuple-element.31.f, f32[10,16,512]{2,1,0:T(8,128)S(1)} %get-tuple-element.32.own, f32[10,8,256]{2,1,0:T(8,128)S(1)} %get-tuple-element.33.own_coarse, ...), custom_call_target="tpu_custom_call" | custom-call | tf_op jit(solution)/shard_map/edges/pallas_call | solution.py:35
  12.0 0.4 collective-permute-start.4
  12.4 1.4 %collective-permute-done.4.b_other = f32[6,64,256]{2,1,0:T(8,128)S(1)} collective-permute-done((f32[6,64,256]{2,1,0:T(8,128)S(1)}, f32[6,64,256]{2,1,0:T(8,128)S(1)}, u32[]{:S(2)}, u32[]{:S(2)}) %collective-permute-start.4) | collective-permute-done | bytes 393248 | tf_op jit(solution)/shard_map/ppermute | solution.py:703
  13.8 0.6 %pair.1 = (f32[408,256]{1,0:T(8,128)S(1)}, f32[48,256]{1,0:T(8,128)S(1)}, f32[48,256]{1,0:T(8,128)S(1)}) custom-call(f32[6,64,256]{2,1,0:T(8,128)S(1)} %get-tuple-element.39.b.b_even, f32[6,64,256]{2,1,0:T(8,128)S(1)} %collective-permute-done.4.b_other, f32[7,80,256]{2,1,0:T(8,128)S(1)} %get-tuple-element.40.cc), custom_call_target="tpu_custom_call" | custom-call | tf_op jit(solution)/shard_map/pair/pallas_call | solution.py:35
  14.4 0.6 %collective-permute-start.5 = (f32[408,256]{1,0:T(8,128)S(1)}, f32[408,256]{1,0:T(8,128)S(1)}, u32[]{:S(2)}, u32[]{:S(2)}) collective-permute-start(f32[408,256]{1,0:T(8,128)S(1)} %get-tuple-element.41.source), channel_id=1, source_target_pairs={{0,2},{2,3},{3,1},{1,0},{4,5},{5,4},{6,7},{7,6},{8,10},{10,11},{11... | collective-permute-start | bytes 1253384 | tf_op jit(solution)/shard_map/ppermute | solution.py:741
  15.0 0.1 outer.1.value
  15.0 1.2 %collective-permute-start.3 = (f32[6,64,512]{2,1,0:T(8,128)S(1)}, f32[6,64,512]{2,1,0:T(8,128)S(1)}, u32[]{:S(2)}, u32[]{:S(2)}) collective-permute-start(f32[6,64,512]{2,1,0:T(8,128)S(1)} %outer.1.value), channel_id=1, source_target_pairs={{2,3},{3,4},{4,5},{5,6},{6,7},{7,2},{0,1},{1,0},{10,11},{11,12},{1... | collective-permute-start | bytes 2359304 | tf_op jit(solution)/shard_map/ppermute | solution.py:703
  16.3 0.7 %collective-permute-start.6 = (f32[48,256]{1,0:T(8,128)S(1)}, f32[48,256]{1,0:T(8,128)S(1)}, u32[]{:S(2)}, u32[]{:S(2)}) collective-permute-start(f32[48,256]{1,0:T(8,128)S(1)} %get-tuple-element.42), channel_id=1, source_target_pairs={{1,10},{10,19},{19,0},{0,1},{4,13},{5,4},{6,15},{7,6},{9,18},{18,2... | collective-permute-start | bytes 147464 | tf_op jit(solution)/shard_map/ppermute | solution.py:741
  16.9 0.4 %collective-permute-start.7 = (f32[48,256]{1,0:T(8,128)S(1)}, f32[48,256]{1,0:T(8,128)S(1)}, u32[]{:S(2)}, u32[]{:S(2)}) collective-permute-start(f32[48,256]{1,0:T(8,128)S(1)} %get-tuple-element.43), channel_id=1, source_target_pairs={{1,26},{26,19},{19,0},{0,1},{4,29},{5,4},{6,31},{7,6},{9,2},{2,27}... | collective-permute-start | bytes 147464 | tf_op jit(solution)/shard_map/ppermute | solution.py:741
  17.4 4.3 %collective-permute-done.6.below = f32[48,256]{1,0:T(8,128)S(1)} collective-permute-done((f32[48,256]{1,0:T(8,128)S(1)}, f32[48,256]{1,0:T(8,128)S(1)}, u32[]{:S(2)}, u32[]{:S(2)}) %collective-permute-start.6) | collective-permute-done | bytes 49184 | tf_op jit(solution)/shard_map/ppermute | solution.py:741
  21.7 0.5 %collective-permute-done.7.above = f32[48,256]{1,0:T(8,128)S(1)} collective-permute-done((f32[48,256]{1,0:T(8,128)S(1)}, f32[48,256]{1,0:T(8,128)S(1)}, u32[]{:S(2)}, u32[]{:S(2)}) %collective-permute-start.7) | collective-permute-done | bytes 49184 | tf_op jit(solution)/shard_map/ppermute | solution.py:741
  22.2 2.0 %collective-permute-start.8 = (f32[2,48,256]{2,1,0:T(8,128)S(1)}, f32[2,48,256]{2,1,0:T(8,128)S(1)}, u32[]{:S(2)}, u32[]{:S(2)}) collective-permute-start(f32[2,48,256]{2,1,0:T(8,128)S(1)} %halo.1), channel_id=1, source_target_pairs={{0,1},{1,0},{2,3},{3,2},{4,5},{5,4},{6,7},{7,6},{8,9},{9,8},{10,11... | collective-permute-start | bytes 294920 | tf_op jit(solution)/shard_map/ppermute | solution.py:703
  24.3 0.9 %collective-permute-done.8.halo_source = f32[2,48,256]{2,1,0:T(8,128)S(1)} collective-permute-done((f32[2,48,256]{2,1,0:T(8,128)S(1)}, f32[2,48,256]{2,1,0:T(8,128)S(1)}, u32[]{:S(2)}, u32[]{:S(2)}) %collective-permute-start.8) | collective-permute-done | bytes 98336 | tf_op jit(solution)/shard_map/ppermute | solution.py:703
  25.2 0.0 collective-permute-done.5.message
  25.2 0.0 collective-permute-done.u.refs_0_
  25.2 0.9 %leap.1.after = f32[6,72,256]{2,1,0:T(8,128)S(1)} custom-call(f32[408,256]{1,0:T(8,128)S(1)} %collective-permute-done.5.message, f32[2,48,256]{2,1,0:T(8,128)S(1)} %halo.1, f32[408,256]{1,0:T(8,128)S(1)} %get-tuple-element.41.source, f32[2,48,256]{2,1,0:T(8,128)S(1)} %collective-permute-done.8.halo_source, f32[7,80,256]{2,1,0:T(8,128)S(1)} %get-tuple-element.40.cc, ...), custom_call_target="tpu_custom_call" | custom-call | tf_op jit(solution)/shard_map/leap/pallas_call | solution.py:35
  26.1 0.4 collective-permute-start.10
  26.5 0.1 collective-permute-start.11
  26.6 0.1 later.1
  26.7 0.7 %collective-permute-start.9 = (f32[6,64,512]{2,1,0:T(8,128)S(1)}, f32[6,64,512]{2,1,0:T(8,128)S(1)}, u32[]{:S(2)}, u32[]{:S(2)}) collective-permute-start(f32[6,64,512]{2,1,0:T(8,128)S(1)} %later.1), channel_id=1, source_target_pairs={{1,2},{9,10},{17,18},{25,26}} | collective-permute-start | bytes 2359304 | tf_op jit(solution)/shard_map/ppermute | solution.py:846
  27.4 1.2 %join.1.refs_1_ = f32[6,128,512]{2,1,0:T(8,128)} custom-call(f32[6,128,512]{2,1,0:T(8,128)S(1)} %get-tuple-element.31.f, f32[6,16,512]{2,1,0:T(8,128)S(1)} %get-tuple-element.38.ends), custom_call_target="tpu_custom_call" | custom-call | bytes 3145728 | tf_op jit(solution)/shard_map/join/pallas_call | solution.py:35
  28.5 1.2 %again.1.inner = f32[6,64,512]{2,1,0:T(8,128)S(1)} custom-call(f32[6,80,512]{2,1,0:T(8,128)S(1)} %collective-permute-done.u.refs_0_, f32[7,128,512]{2,1,0:T(8,128)S(1)} %get-tuple-element.30.cf), custom_call_target="tpu_custom_call" | custom-call | bytes 3145728 | tf_op jit(solution)/shard_map/again/pallas_call | solution.py:35
  29.8 0.0 collective-permute-done.3.outer
  29.8 1.8 %remainder.1.base_in.refs_0_ = f32[6,128,512]{2,1,0:T(8,128)S(1)} custom-call(f32[6,64,512]{2,1,0:T(8,128)S(1)} %again.1.inner, f32[6,64,512]{2,1,0:T(8,128)S(1)} %collective-permute-done.3.outer, f32[6,128,512]{2,1,0:T(8,128)} %init.5), custom_call_target="tpu_custom_call" | custom-call | bytes 3145728 | tf_op jit(solution)/shard_map/remainder/pallas_call | solution.py:35
  31.6 2.7 %collective-permute-done.10.leaped = f32[6,72,256]{2,1,0:T(8,128)S(1)} collective-permute-done((f32[6,72,256]{2,1,0:T(8,128)S(1)}, f32[6,72,256]{2,1,0:T(8,128)S(1)}, u32[]{:S(2)}, u32[]{:S(2)}) %collective-permute-start.10) | collective-permute-done | bytes 442400 | tf_op jit(solution)/shard_map/ppermute | solution.py:703
  34.3 4.4 %collective-permute-done.11.step = f32[6,72,256]{2,1,0:T(8,128)S(1)} collective-permute-done((f32[6,72,256]{2,1,0:T(8,128)S(1)}, f32[6,72,256]{2,1,0:T(8,128)S(1)}, u32[]{:S(2)}, u32[]{:S(2)}) %collective-permute-start.11) | collective-permute-done | bytes 442400 | tf_op jit(solution)/shard_map/ppermute | solution.py:703
  38.7 0.1 collect.1
  38.9 0.5 %even.1 = f32[6,64,256]{2,1,0:T(8,128)S(1)} custom-call(f32[6,80,256]{2,1,0:T(8,128)S(1)} %get-tuple-element.45.ext, f32[6,64,256]{2,1,0:T(8,128)S(1)} %get-tuple-element.39.b.b_even, f32[7,80,256]{2,1,0:T(8,128)S(1)} %get-tuple-element.40.cc), custom_call_target="tpu_custom_call" | custom-call | tf_op jit(solution)/shard_map/even/pallas_call | solution.py:35
  39.4 0.1 collective-permute-start.12
  39.4 0.0 collective-permute-done.9.after_hop
  39.5 1.7 %collective-permute-done.12.received = f32[6,64,256]{2,1,0:T(8,128)S(1)} collective-permute-done((f32[6,64,256]{2,1,0:T(8,128)S(1)}, f32[6,64,256]{2,1,0:T(8,128)S(1)}, u32[]{:S(2)}, u32[]{:S(2)}) %collective-permute-start.12) | collective-permute-done | bytes 393248 | tf_op jit(solution)/shard_map/ppermute | solution.py:703
  41.1 1.5 %correct.1 = f32[6,128,512]{2,1,0:T(8,128)} custom-call(f32[6,128,512]{2,1,0:T(8,128)S(1)} %late.1.base, f32[6,64,256]{2,1,0:T(8,128)S(1)} %get-tuple-element.44.own, f32[6,64,256]{2,1,0:T(8,128)S(1)} %collective-permute-done.12.received), custom_call_target="tpu_custom_call" | custom-call | tf_op jit(solution)/shard_map/correct/pallas_call | solution.py:35
  (3 shorter events, 0.0 us)
Async XLA Ops:
  3.1 22.2 %collective-permute-start = (f32[6,80,512]{2,1,0:T(8,128)S(1)}, f32[6,80,512]{2,1,0:T(8,128)S(1)}, u32[]{:S(2)}, u32[]{:S(2)}) collective-permute-start(f32[6,80,512]{2,1,0:T(8,128)S(1)} %get-tuple-element.24), channel_id=1, source_target_pairs={{0,1},{1,2},{2,3},{3,4},{4,5},{5,6},{6,7},{7,0},{8,9},{9,10},{10,1... | collective-permute-start | bytes 2949128 | tf_op jit(solution)/shard_map/ppermute | solution.py:703
  5.0 5.7 %collective-permute-start.1 = (f32[40,512]{1,0:T(8,128)S(1)}, f32[40,512]{1,0:T(8,128)S(1)}, u32[]{:S(2)}, u32[]{:S(2)}) collective-permute-start(f32[40,512]{1,0:T(8,128)S(1)} %get-tuple-element.36), channel_id=1, source_target_pairs={{0,8},{8,16},{16,24},{24,0},{1,9},{9,17},{17,25},{25,1},{2,10},{10... | collective-permute-start | bytes 245768 | tf_op jit(solution)/shard_map/ppermute | solution.py:696
  6.2 5.0 %collective-permute-start.2 = (f32[40,512]{1,0:T(8,128)S(1)}, f32[40,512]{1,0:T(8,128)S(1)}, u32[]{:S(2)}, u32[]{:S(2)}) collective-permute-start(f32[40,512]{1,0:T(8,128)S(1)} %get-tuple-element.37), channel_id=1, source_target_pairs={{0,24},{8,0},{16,8},{24,16},{1,25},{9,1},{17,9},{25,17},{2,26},{10... | collective-permute-start | bytes 245768 | tf_op jit(solution)/shard_map/ppermute | solution.py:696
  12.0 1.8 %collective-permute-start.4 = (f32[6,64,256]{2,1,0:T(8,128)S(1)}, f32[6,64,256]{2,1,0:T(8,128)S(1)}, u32[]{:S(2)}, u32[]{:S(2)}) collective-permute-start(f32[6,64,256]{2,1,0:T(8,128)S(1)} %get-tuple-element.39.b.b_even), channel_id=1, source_target_pairs={{0,1},{1,0},{2,3},{3,2},{4,5},{5,4},{6,7},{7,6},{8,9},{9,8},{10,11... | collective-permute-start | bytes 1179656 | tf_op jit(solution)/shard_map/ppermute | solution.py:703
  14.4 10.8 %collective-permute-start.5 = (f32[408,256]{1,0:T(8,128)S(1)}, f32[408,256]{1,0:T(8,128)S(1)}, u32[]{:S(2)}, u32[]{:S(2)}) collective-permute-start(f32[408,256]{1,0:T(8,128)S(1)} %get-tuple-element.41.source), channel_id=1, source_target_pairs={{0,2},{2,3},{3,1},{1,0},{4,5},{5,4},{6,7},{7,6},{8,10},{10,11},{11... | collective-permute-start | bytes 1253384 | tf_op jit(solution)/shard_map/ppermute | solution.py:741
  15.0 14.8 %collective-permute-start.3 = (f32[6,64,512]{2,1,0:T(8,128)S(1)}, f32[6,64,512]{2,1,0:T(8,128)S(1)}, u32[]{:S(2)}, u32[]{:S(2)}) collective-permute-start(f32[6,64,512]{2,1,0:T(8,128)S(1)} %outer.1.value), channel_id=1, source_target_pairs={{2,3},{3,4},{4,5},{5,6},{6,7},{7,2},{0,1},{1,0},{10,11},{11,12},{1... | collective-permute-start | bytes 2359304 | tf_op jit(solution)/shard_map/ppermute | solution.py:703
  16.3 5.4 %collective-permute-start.6 = (f32[48,256]{1,0:T(8,128)S(1)}, f32[48,256]{1,0:T(8,128)S(1)}, u32[]{:S(2)}, u32[]{:S(2)}) collective-permute-start(f32[48,256]{1,0:T(8,128)S(1)} %get-tuple-element.42), channel_id=1, source_target_pairs={{1,10},{10,19},{19,0},{0,1},{4,13},{5,4},{6,15},{7,6},{9,18},{18,2... | collective-permute-start | bytes 147464 | tf_op jit(solution)/shard_map/ppermute | solution.py:741
  16.9 5.3 %collective-permute-start.7 = (f32[48,256]{1,0:T(8,128)S(1)}, f32[48,256]{1,0:T(8,128)S(1)}, u32[]{:S(2)}, u32[]{:S(2)}) collective-permute-start(f32[48,256]{1,0:T(8,128)S(1)} %get-tuple-element.43), channel_id=1, source_target_pairs={{1,26},{26,19},{19,0},{0,1},{4,29},{5,4},{6,31},{7,6},{9,2},{2,27}... | collective-permute-start | bytes 147464 | tf_op jit(solution)/shard_map/ppermute | solution.py:741
  22.2 3.0 %collective-permute-start.8 = (f32[2,48,256]{2,1,0:T(8,128)S(1)}, f32[2,48,256]{2,1,0:T(8,128)S(1)}, u32[]{:S(2)}, u32[]{:S(2)}) collective-permute-start(f32[2,48,256]{2,1,0:T(8,128)S(1)} %halo.1), channel_id=1, source_target_pairs={{0,1},{1,0},{2,3},{3,2},{4,5},{5,4},{6,7},{7,6},{8,9},{9,8},{10,11... | collective-permute-start | bytes 294920 | tf_op jit(solution)/shard_map/ppermute | solution.py:703
  26.1 8.2 %collective-permute-start.10 = (f32[6,72,256]{2,1,0:T(8,128)S(1)}, f32[6,72,256]{2,1,0:T(8,128)S(1)}, u32[]{:S(2)}, u32[]{:S(2)}) collective-permute-start(f32[6,72,256]{2,1,0:T(8,128)S(1)} %leap.1.after), channel_id=1, source_target_pairs={{2,6},{6,7},{7,3},{3,2},{0,1},{1,0},{4,5},{5,4},{10,14},{14,15},{1... | collective-permute-start | bytes 1327112 | tf_op jit(solution)/shard_map/ppermute | solution.py:703
  26.5 12.2 %collective-permute-start.11 = (f32[6,72,256]{2,1,0:T(8,128)S(1)}, f32[6,72,256]{2,1,0:T(8,128)S(1)}, u32[]{:S(2)}, u32[]{:S(2)}) collective-permute-start(f32[6,72,256]{2,1,0:T(8,128)S(1)} %leap.1.after), channel_id=1, source_target_pairs={{2,4},{4,6},{6,7},{7,5},{5,3},{3,2},{0,1},{1,0},{10,12},{12,14},{1... | collective-permute-start | bytes 1327112 | tf_op jit(solution)/shard_map/ppermute | solution.py:703
  26.7 12.8 %collective-permute-start.9 = (f32[6,64,512]{2,1,0:T(8,128)S(1)}, f32[6,64,512]{2,1,0:T(8,128)S(1)}, u32[]{:S(2)}, u32[]{:S(2)}) collective-permute-start(f32[6,64,512]{2,1,0:T(8,128)S(1)} %later.1), channel_id=1, source_target_pairs={{1,2},{9,10},{17,18},{25,26}} | collective-permute-start | bytes 2359304 | tf_op jit(solution)/shard_map/ppermute | solution.py:846
  39.4 1.8 %collective-permute-start.12 = (f32[6,64,256]{2,1,0:T(8,128)S(1)}, f32[6,64,256]{2,1,0:T(8,128)S(1)}, u32[]{:S(2)}, u32[]{:S(2)}) collective-permute-start(f32[6,64,256]{2,1,0:T(8,128)S(1)} %even.1), channel_id=1, source_target_pairs={{0,1},{1,0},{2,3},{3,2},{4,5},{5,4},{6,7},{7,6},{8,9},{9,8},{10,11... | collective-permute-start | bytes 1179656 | tf_op jit(solution)/shard_map/ppermute | solution.py:703

commit v6 on v5

--- a/solution.py
+++ b/solution.py
@@ -100,18 +100,12 @@
     return w, q
 
 
-def three_parts(value):
-    high = value.astype(jnp.bfloat16)
-    rest = value - high.astype(F32)
-    middle = rest.astype(jnp.bfloat16)
-    low = (rest - middle.astype(F32)).astype(jnp.bfloat16)
-    return high, middle, low
-
-
 def exact_dot(value, matrix):
-    return sum(
-        jnp.dot(part, matrix, preferred_element_type=F32) for part in three_parts(value)[::-1]
-    )
+    split = []
+    for _ in range(3):
+        split.append(value.astype(jnp.bfloat16))
+        value = value - split[-1].astype(F32)
+    return sum(jnp.dot(part, matrix, preferred_element_type=F32) for part in split[::-1])
 
 
 def averaging(cols):
@@ -166,8 +160,8 @@
     first = is_first()
     copies = [(kc_far, kc), (ka_far, ka), (mass_far, mass), (hoop_far, hoop)]
     copies += [
-        (init.at[:, start : start + 16], early.at[:, pl.ds(16 * end, 16)])
-        for end, start in enumerate((0, rows - 16))
+        (init.at[:, start : start + 8], early.at[:, pl.ds(8 * end, 8)])
+        for end, start in enumerate((0, rows - 8))
     ]
     copies.append((u_far, u))
     copies = [
@@ -177,39 +171,43 @@
     for copy in copies:
         copy.start()
     matrix = averaging(cols)
-    for copy in copies:
+    half = cols // 2
+    fine_at = [sum(FINE_ROWS[:number]) for number in range(10)]
+    coarse_at = [sum(COARSE_ROWS[:number]) for number in range(10)]
+
+    def pack(numbers, sources, sums, ends):
+        for number, (ref, place) in zip(numbers, sources):
+            own[number, 0:8, :] = ref[place + (slice(0, 8), slice(None))]
+            own[number, 8:16, :] = ref[place + (slice(rows - 8, rows), slice(None))]
+            at, count = fine_at[number], FINE_ROWS[number]
+            to_above[at : at + count, :] = own[number, 16 - count : 16, :]
+            to_below[at : at + count, :] = own[number, 0:count, :]
+        means = exact_dot(jnp.concatenate(sums, axis=0), matrix)
+        for n, number in enumerate(numbers):
+            low = means[2 * n * ends : (2 * n + 1) * ends]
+            high = means[(2 * n + 1) * ends : (2 * n + 2) * ends]
+            own_coarse[number, 0:4, :] = low[0:4]
+            own_coarse[number, 4:8, :] = high[ends - 4 : ends]
+            count = COARSE_ROWS[number]
+            for k in range(count):
+                at = coarse_at[number] + k
+                line = FINE_TOTAL + at // 2
+                where = (slice(line, line + 1), pl.ds((at % 2) * half, half))
+                to_above[where] = high[ends - count + k : ends - count + k + 1]
+                to_below[where] = low[k : k + 1]
+
+    for copy in copies[:4]:
         copy.wait()
-    for end, start in enumerate((0, rows - 8)):
-        at = pl.ds(8 * end, 8)
-        for i in range(6):
-            own[i, at, :] = u[i, start : start + 8, :]
-        for number, ref in enumerate((kc, ka, mass, hoop)):
-            own[6 + number, at, :] = ref[start : start + 8, :]
-    at = 0
-    for number, count in enumerate(FINE_ROWS):
-        to_above[at : at + count, :] = own[number, 16 - count : 16, :]
-        to_below[at : at + count, :] = own[number, 0:count, :]
-        at += count
+    sources = [(ref, ()) for ref in (kc, ka, mass, hoop)]
+    sums = [pair_sum(ref, (), start, 8) for ref, _ in sources for start in (0, rows - 16)]
+    pack(range(6, 10), sources, sums, 8)
+    for copy in copies[4:]:
+        copy.wait()
     sums = []
-    for start in (rows - 16, 0):
-        for number, ref in enumerate([u] * 6 + [kc, ka, mass, hoop]):
-            value = pair_sum(ref, (number,) if number < 6 else (), start, 8)
-            if number < 6:
-                value = value - first * pair_sum(early, (number,), 16 * (start > 0), 8)
-            sums.append(value)
-    means = exact_dot(jnp.concatenate(sums, axis=0), matrix)
-    half = cols // 2
-    at = 0
-    for number, count in enumerate(COARSE_ROWS):
-        high, low = means[8 * number : 8 * number + 8], means[80 + 8 * number : 88 + 8 * number]
-        own_coarse[number, 0:4, :] = low[0:4]
-        own_coarse[number, 4:8, :] = high[4:8]
-        for k in range(count):
-            line = FINE_TOTAL + at // 2
-            place = (slice(line, line + 1), pl.ds((at % 2) * half, half))
-            to_above[place] = high[8 - count + k : 9 - count + k]
-            to_below[place] = low[k : k + 1]
-            at += 1
+    for i in range(6):
+        for end, start in enumerate((0, rows - 8)):
+            sums.append(pair_sum(u, (i,), start, 4) - first * pair_sum(early, (i,), 8 * end, 4))
+    pack(range(6), [(u, (i,)) for i in range(6)], sums, 4)
     lead = rows // 4 - MARGIN
     middle[...] = u[:, lead : rows - lead, :]
 
@@ -485,9 +483,17 @@
 
 
 def leap_body(message, halo, source, halo_source, cc, *refs):
-    out, ext, add = refs[-3:]
+    far, near, ext, add = refs[-4:]
     chip = lax.axis_index("cuts") // 2
-    rows = ext.shape[1]
+    few = ext.shape[1] - 16
+    top = 8 + few
+
+    def put(i, value):
+        own, beyond = i * few, 6 * few + 4 * i
+        far[i] = value[4 : top + 4]
+        near[own : own + few, :] = value[8:top]
+        near[beyond : beyond + 2, :] = value[6:8]
+        near[beyond + 2 : beyond + 4, :] = value[top : top + 2]
 
     @pl.when((chip == 1) | (chip == 2))
     def _():
@@ -499,11 +505,12 @@
         ext[...] = jnp.zeros_like(ext)
         read_message(ext, message, *halves(halo))
         for i, value in enumerate(advance(ext, cc, 2)):
-            out[i] = (value + add[i])[4 : rows - 4]
+            put(i, value + add[i])
 
     @pl.when(chip == 2)
     def _():
-        out[...] = add[:, 4 : rows - 4, :]
+        for i in range(6):
+            put(i, add[i])
 
 
 def last_body(leaped, cc, out, ext):
@@ -521,6 +528,7 @@
     total, ext = refs[-2:]
     chip = lax.axis_index("cuts") // 2
     rows = ext.shape[1]
+    few = rows - 16
     ext[...] = jnp.zeros_like(ext)
 
     @pl.when(chip == 1)
@@ -529,7 +537,11 @@
 
     @pl.when(chip >= 2)
     def _():
-        ext[:, 4 : rows - 4, :] = step[...]
+        for i in range(6):
+            own, beyond = i * few, 6 * few + 4 * i
+            ext[i, 8 : 8 + few, :] = step[own : own + few, :]
+            ext[i, 6:8, :] = step[beyond : beyond + 2, :]
+            ext[i, 8 + few : 10 + few, :] = step[beyond + 2 : beyond + 4, :]
 
     @pl.when(chip == 3)
     def _():
@@ -758,7 +770,7 @@
         + [middle_shape],
         [u, initial_state, *fields],
         [
-            pltpu.VMEM((6, 32, cols), F32),
+            pltpu.VMEM(ends_shape, F32),
             halver_scratch(32, 16, cols),
             pltpu.SemaphoreType.DMA((7,)),
         ],
@@ -808,17 +820,17 @@
     if leap:
         main, halo = hop_with_edges(*source, to_chip_1)
         halo_source = along_cuts(halo, {})
-        (leaped,) = run(
+        far, near = run(
             leap_body,
             "leap",
-            [(6, few + 8, half_cols)],
+            [(6, few + 8, half_cols), message],
             [main, halo, source[0], halo_source, cc, raw],
             ext * 2,
             specs=[VMEM] * 5 + [ANY],
         )
-        after_leap = leaped
-        to_chip_3 = around_cuts(leaped, 2, 6, 7, 3)
-        to_next = around_cuts(leaped, 2, 4, 6, 7, 5, 3)
+        after_leap = near
+        to_chip_3 = around_cuts(far, 2, 6, 7, 3)
+        to_next = around_cuts(near, 2, 4, 6, 7, 5, 3)
         (last,) = run(
             last_body, "last", [ext_state], [to_chip_3, cc], ext, cost=(LAST_COST, LAST_COST)
         )

time: 42.8 us -> 42.2 us (0.986)
  no operation moved by 1% of the time
where the time goes in v6:
time: 42.2 us; the launch traced here: 42 us
  waiting for transfers between devices  16.3 us (39%)
  Pallas kernels  15.1 us (36%)
  starting transfers between devices  9.92 us (24%)
  between operations  0.77 us (2%)
    pallas_call x16, Pallas kernels, run(): pl.pallas_call(body, name=name, out_shape=[jax.ShapeDtypeStruct(shape, F3...  15.1 us
    ppermute x7, waiting for transfers between devices, along_cuts(): return lax.ppermute(value, 'cuts', pairs)  10.9 us
    ppermute x7, starting transfers between devices, along_cuts(): return lax.ppermute(value, 'cuts', pairs)  6.09 us
    ppermute x3, waiting for transfers between devices, to_chip_1(): return lax.ppermute(value, ('strip', 'cuts'), pairs)  4.89 us
    ppermute x3, starting transfers between devices, to_chip_1(): return lax.ppermute(value, ('strip', 'cuts'), pairs)  1.65 us
    ppermute x2, starting transfers between devices, around_loop(): return lax.ppermute(value, 'strip', pairs)  1.47 us
  transfers between devices with their start and end apart: 13, of which 8 were waited for; matrix products, arithmetic and copies ran while one was open for 0% of the time, Pallas kernels for 27%

profile of v6, /device:TPU:11, one launch (start us, length us, event | category | flops | bytes accessed | tf_op | source)
XLA Modules:
  0.0 42.0 jit_solution(5763262464637428860)
XLA Ops:
  0.6 2.3 %pack.1 = (f32[40,512]{1,0:T(8,128)S(1)}, f32[40,512]{1,0:T(8,128)S(1)}, f32[10,16,512]{2,1,0:T(8,128)S(1)}, f32[10,8,256]{2,1,0:T(8,128)S(1)}, f32[6,128,512]{2...) custom-call(f32[6,128,512]{2,1,0:T(8,128)} %bitcast.4, ...), custom_call_target="tpu_custom_call" | custom-call | tf_op jit(solution)/shard_map/pack/pallas_call | solution.py:35
  2.9 1.9 %collective-permute-start = (f32[6,80,512]{2,1,0:T(8,128)S(1)}, f32[6,80,512]{2,1,0:T(8,128)S(1)}, u32[]{:S(2)}, u32[]{:S(2)}) collective-permute-start(f32[6,80,512]{2,1,0:T(8,128)S(1)} %get-tuple-element.26), channel_id=1, source_target_pairs={{0,1},{1,2},{2,3},{3,4},{4,5},{5,6},{6,7},{7,0},{8,9},{9,10},{10,1... | collective-permute-start | bytes 2949128 | tf_op jit(solution)/shard_map/ppermute | solution.py:715
  4.9 1.2 %collective-permute-start.1 = (f32[40,512]{1,0:T(8,128)S(1)}, f32[40,512]{1,0:T(8,128)S(1)}, u32[]{:S(2)}, u32[]{:S(2)}) collective-permute-start(f32[40,512]{1,0:T(8,128)S(1)} %get-tuple-element.38), channel_id=1, source_target_pairs={{0,8},{8,16},{16,24},{24,0},{1,9},{9,17},{17,25},{25,1},{2,10},{10... | collective-permute-start | bytes 245768 | tf_op jit(solution)/shard_map/ppermute | solution.py:708
  6.1 0.3 collective-permute-start.2
  6.3 4.2 %interior.1 = (f32[6,128,512]{2,1,0:T(8,128)S(1)}, f32[6,64,256]{2,1,0:T(8,128)S(1)}, f32[7,80,256]{2,1,0:T(8,128)S(1)}, f32[7,128,512]{2,1,0:T(8,128)S(1)}) custom-call(f32[6,128,512]{2,1,0:T(8,128)S(1)} %get-tuple-element.27.u, f32[6,128,512]{2,1,0:T(8,128)} %init.5, f32[128,512]{1,0:T(8,128)S(1)} %get-tuple-element.28.kc, ...), custom_call_target="tpu_custom_call" | custom-call | tf_op jit(solution)/shard_map/interior/pallas_call | solution.py:35
  10.6 0.0 collective-permute-done.1.from_below
  10.6 0.5 %collective-permute-done.2.from_above = f32[40,512]{1,0:T(8,128)S(1)} collective-permute-done((f32[40,512]{1,0:T(8,128)S(1)}, f32[40,512]{1,0:T(8,128)S(1)}, u32[]{:S(2)}, u32[]{:S(2)}) %collective-permute-start.2) | collective-permute-done | bytes 81952 | tf_op jit(solution)/shard_map/ppermute | solution.py:708
  11.1 0.8 %edges.1 = (f32[6,16,512]{2,1,0:T(8,128)S(1)}, f32[6,64,256]{2,1,0:T(8,128)S(1)}, f32[7,80,256]{2,1,0:T(8,128)S(1)}) custom-call(f32[6,128,512]{2,1,0:T(8,128)S(1)} %get-tuple-element.33.f, f32[10,16,512]{2,1,0:T(8,128)S(1)} %get-tuple-element.34.own, f32[10,8,256]{2,1,0:T(8,128)S(1)} %get-tuple-element.35.own_coarse, ...), custom_call_target="tpu_custom_call" | custom-call | tf_op jit(solution)/shard_map/edges/pallas_call | solution.py:35
  11.9 0.4 collective-permute-start.4
  12.3 1.4 %collective-permute-done.4.b_other = f32[6,64,256]{2,1,0:T(8,128)S(1)} collective-permute-done((f32[6,64,256]{2,1,0:T(8,128)S(1)}, f32[6,64,256]{2,1,0:T(8,128)S(1)}, u32[]{:S(2)}, u32[]{:S(2)}) %collective-permute-start.4) | collective-permute-done | bytes 393248 | tf_op jit(solution)/shard_map/ppermute | solution.py:715
  13.7 0.5 %pair.1 = (f32[408,256]{1,0:T(8,128)S(1)}, f32[48,256]{1,0:T(8,128)S(1)}, f32[48,256]{1,0:T(8,128)S(1)}) custom-call(f32[6,64,256]{2,1,0:T(8,128)S(1)} %get-tuple-element.41.b.b_even, f32[6,64,256]{2,1,0:T(8,128)S(1)} %collective-permute-done.4.b_other, f32[7,80,256]{2,1,0:T(8,128)S(1)} %get-tuple-element.42.cc), custom_call_target="tpu_custom_call" | custom-call | tf_op jit(solution)/shard_map/pair/pallas_call | solution.py:35
  14.3 0.6 %collective-permute-start.5 = (f32[408,256]{1,0:T(8,128)S(1)}, f32[408,256]{1,0:T(8,128)S(1)}, u32[]{:S(2)}, u32[]{:S(2)}) collective-permute-start(f32[408,256]{1,0:T(8,128)S(1)} %get-tuple-element.43.source), channel_id=1, source_target_pairs={{0,2},{2,3},{3,1},{1,0},{4,5},{5,4},{6,7},{7,6},{8,10},{10,11},{11... | collective-permute-start | bytes 1253384 | tf_op jit(solution)/shard_map/ppermute | solution.py:753
  14.8 0.1 outer.1.value
  14.9 1.2 %collective-permute-start.3 = (f32[6,64,512]{2,1,0:T(8,128)S(1)}, f32[6,64,512]{2,1,0:T(8,128)S(1)}, u32[]{:S(2)}, u32[]{:S(2)}) collective-permute-start(f32[6,64,512]{2,1,0:T(8,128)S(1)} %outer.1.value), channel_id=1, source_target_pairs={{2,3},{3,4},{4,5},{5,6},{6,7},{7,2},{0,1},{1,0},{10,11},{11,12},{1... | collective-permute-start | bytes 2359304 | tf_op jit(solution)/shard_map/ppermute | solution.py:715
  16.1 0.7 %collective-permute-start.6 = (f32[48,256]{1,0:T(8,128)S(1)}, f32[48,256]{1,0:T(8,128)S(1)}, u32[]{:S(2)}, u32[]{:S(2)}) collective-permute-start(f32[48,256]{1,0:T(8,128)S(1)} %get-tuple-element.44), channel_id=1, source_target_pairs={{1,10},{10,19},{19,0},{0,1},{4,13},{5,4},{6,15},{7,6},{9,18},{18,2... | collective-permute-start | bytes 147464 | tf_op jit(solution)/shard_map/ppermute | solution.py:753
  16.8 0.4 %collective-permute-start.7 = (f32[48,256]{1,0:T(8,128)S(1)}, f32[48,256]{1,0:T(8,128)S(1)}, u32[]{:S(2)}, u32[]{:S(2)}) collective-permute-start(f32[48,256]{1,0:T(8,128)S(1)} %get-tuple-element.45), channel_id=1, source_target_pairs={{1,26},{26,19},{19,0},{0,1},{4,29},{5,4},{6,31},{7,6},{9,2},{2,27}... | collective-permute-start | bytes 147464 | tf_op jit(solution)/shard_map/ppermute | solution.py:753
  17.2 4.4 %collective-permute-done.6.below = f32[48,256]{1,0:T(8,128)S(1)} collective-permute-done((f32[48,256]{1,0:T(8,128)S(1)}, f32[48,256]{1,0:T(8,128)S(1)}, u32[]{:S(2)}, u32[]{:S(2)}) %collective-permute-start.6) | collective-permute-done | bytes 49184 | tf_op jit(solution)/shard_map/ppermute | solution.py:753
  21.6 0.5 %collective-permute-done.7.above = f32[48,256]{1,0:T(8,128)S(1)} collective-permute-done((f32[48,256]{1,0:T(8,128)S(1)}, f32[48,256]{1,0:T(8,128)S(1)}, u32[]{:S(2)}, u32[]{:S(2)}) %collective-permute-start.7) | collective-permute-done | bytes 49184 | tf_op jit(solution)/shard_map/ppermute | solution.py:753
  22.1 2.0 %collective-permute-start.8 = (f32[2,48,256]{2,1,0:T(8,128)S(1)}, f32[2,48,256]{2,1,0:T(8,128)S(1)}, u32[]{:S(2)}, u32[]{:S(2)}) collective-permute-start(f32[2,48,256]{2,1,0:T(8,128)S(1)} %halo.1), channel_id=1, source_target_pairs={{0,1},{1,0},{2,3},{3,2},{4,5},{5,4},{6,7},{7,6},{8,9},{9,8},{10,11... | collective-permute-start | bytes 294920 | tf_op jit(solution)/shard_map/ppermute | solution.py:715
  24.1 0.9 %collective-permute-done.8.halo_source = f32[2,48,256]{2,1,0:T(8,128)S(1)} collective-permute-done((f32[2,48,256]{2,1,0:T(8,128)S(1)}, f32[2,48,256]{2,1,0:T(8,128)S(1)}, u32[]{:S(2)}, u32[]{:S(2)}) %collective-permute-start.8) | collective-permute-done | bytes 98336 | tf_op jit(solution)/shard_map/ppermute | solution.py:715
  25.0 0.0 collective-permute-done.5.message
  25.1 0.0 collective-permute-done.u.refs_0_
  25.1 0.8 %leap.1 = (f32[6,72,256]{2,1,0:T(8,128)S(1)}, f32[408,256]{1,0:T(8,128)S(1)}) custom-call(f32[408,256]{1,0:T(8,128)S(1)} %collective-permute-done.5.message, f32[2,48,256]{2,1,0:T(8,128)S(1)} %halo.1, f32[408,256]{1,0:T(8,128)S(1)} %get-tuple-element.43.source, f32[2,48,256]{2,1,0:T(8,128)S(1)} %collective-permute-done.8.halo_source, ...), custom_call_target="tpu_custom_call" | custom-call | tf_op jit(solution)/shard_map/leap/pallas_call | solution.py:35
  25.9 0.4 collective-permute-start.10
  26.3 0.1 collective-permute-start.11
  26.3 0.1 later.1
  26.4 0.7 %collective-permute-start.9 = (f32[6,64,512]{2,1,0:T(8,128)S(1)}, f32[6,64,512]{2,1,0:T(8,128)S(1)}, u32[]{:S(2)}, u32[]{:S(2)}) collective-permute-start(f32[6,64,512]{2,1,0:T(8,128)S(1)} %later.1), channel_id=1, source_target_pairs={{1,2},{9,10},{17,18},{25,26}} | collective-permute-start | bytes 2359304 | tf_op jit(solution)/shard_map/ppermute | solution.py:858
  27.1 1.2 %join.1.refs_1_ = f32[6,128,512]{2,1,0:T(8,128)} custom-call(f32[6,128,512]{2,1,0:T(8,128)S(1)} %get-tuple-element.33.f, f32[6,16,512]{2,1,0:T(8,128)S(1)} %get-tuple-element.40.ends), custom_call_target="tpu_custom_call" | custom-call | bytes 3145728 | tf_op jit(solution)/shard_map/join/pallas_call | solution.py:35
  28.3 1.2 %again.1.inner = f32[6,64,512]{2,1,0:T(8,128)S(1)} custom-call(f32[6,80,512]{2,1,0:T(8,128)S(1)} %collective-permute-done.u.refs_0_, f32[7,128,512]{2,1,0:T(8,128)S(1)} %get-tuple-element.32.cf), custom_call_target="tpu_custom_call" | custom-call | bytes 3145728 | tf_op jit(solution)/shard_map/again/pallas_call | solution.py:35
  29.5 0.0 collective-permute-done.3.outer
  29.5 1.8 %remainder.1.base_in.refs_0_ = f32[6,128,512]{2,1,0:T(8,128)S(1)} custom-call(f32[6,64,512]{2,1,0:T(8,128)S(1)} %again.1.inner, f32[6,64,512]{2,1,0:T(8,128)S(1)} %collective-permute-done.3.outer, f32[6,128,512]{2,1,0:T(8,128)} %init.5), custom_call_target="tpu_custom_call" | custom-call | bytes 3145728 | tf_op jit(solution)/shard_map/remainder/pallas_call | solution.py:35
  31.3 2.7 %collective-permute-done.10.leaped = f32[6,72,256]{2,1,0:T(8,128)S(1)} collective-permute-done((f32[6,72,256]{2,1,0:T(8,128)S(1)}, f32[6,72,256]{2,1,0:T(8,128)S(1)}, u32[]{:S(2)}, u32[]{:S(2)}) %collective-permute-start.10) | collective-permute-done | bytes 442400 | tf_op jit(solution)/shard_map/ppermute | solution.py:715
  34.1 4.1 %collective-permute-done.11.step = f32[408,256]{1,0:T(8,128)S(1)} collective-permute-done((f32[408,256]{1,0:T(8,128)S(1)}, f32[408,256]{1,0:T(8,128)S(1)}, u32[]{:S(2)}, u32[]{:S(2)}) %collective-permute-start.11) | collective-permute-done | bytes 417824 | tf_op jit(solution)/shard_map/ppermute | solution.py:715
  38.2 0.1 collect.1
  38.3 0.4 even.1
  38.8 0.1 collective-permute-start.12
  38.8 0.0 collective-permute-done.9.after_hop
  38.9 1.7 %collective-permute-done.12.received = f32[6,64,256]{2,1,0:T(8,128)S(1)} collective-permute-done((f32[6,64,256]{2,1,0:T(8,128)S(1)}, f32[6,64,256]{2,1,0:T(8,128)S(1)}, u32[]{:S(2)}, u32[]{:S(2)}) %collective-permute-start.12) | collective-permute-done | bytes 393248 | tf_op jit(solution)/shard_map/ppermute | solution.py:715
  40.5 1.5 %correct.1 = f32[6,128,512]{2,1,0:T(8,128)} custom-call(f32[6,128,512]{2,1,0:T(8,128)S(1)} %late.1.base, f32[6,64,256]{2,1,0:T(8,128)S(1)} %get-tuple-element.48.own, f32[6,64,256]{2,1,0:T(8,128)S(1)} %collective-permute-done.12.received), custom_call_target="tpu_custom_call" | custom-call | tf_op jit(solution)/shard_map/correct/pallas_call | solution.py:35
  (3 shorter events, 0.0 us)
Async XLA Ops:
  2.9 22.1 %collective-permute-start = (f32[6,80,512]{2,1,0:T(8,128)S(1)}, f32[6,80,512]{2,1,0:T(8,128)S(1)}, u32[]{:S(2)}, u32[]{:S(2)}) collective-permute-start(f32[6,80,512]{2,1,0:T(8,128)S(1)} %get-tuple-element.26), channel_id=1, source_target_pairs={{0,1},{1,2},{2,3},{3,4},{4,5},{5,6},{6,7},{7,0},{8,9},{9,10},{10,1... | collective-permute-start | bytes 2949128 | tf_op jit(solution)/shard_map/ppermute | solution.py:715
  4.9 5.7 %collective-permute-start.1 = (f32[40,512]{1,0:T(8,128)S(1)}, f32[40,512]{1,0:T(8,128)S(1)}, u32[]{:S(2)}, u32[]{:S(2)}) collective-permute-start(f32[40,512]{1,0:T(8,128)S(1)} %get-tuple-element.38), channel_id=1, source_target_pairs={{0,8},{8,16},{16,24},{24,0},{1,9},{9,17},{17,25},{25,1},{2,10},{10... | collective-permute-start | bytes 245768 | tf_op jit(solution)/shard_map/ppermute | solution.py:708
  6.1 5.0 %collective-permute-start.2 = (f32[40,512]{1,0:T(8,128)S(1)}, f32[40,512]{1,0:T(8,128)S(1)}, u32[]{:S(2)}, u32[]{:S(2)}) collective-permute-start(f32[40,512]{1,0:T(8,128)S(1)} %get-tuple-element.39), channel_id=1, source_target_pairs={{0,24},{8,0},{16,8},{24,16},{1,25},{9,1},{17,9},{25,17},{2,26},{10... | collective-permute-start | bytes 245768 | tf_op jit(solution)/shard_map/ppermute | solution.py:708
  11.9 1.8 %collective-permute-start.4 = (f32[6,64,256]{2,1,0:T(8,128)S(1)}, f32[6,64,256]{2,1,0:T(8,128)S(1)}, u32[]{:S(2)}, u32[]{:S(2)}) collective-permute-start(f32[6,64,256]{2,1,0:T(8,128)S(1)} %get-tuple-element.41.b.b_even), channel_id=1, source_target_pairs={{0,1},{1,0},{2,3},{3,2},{4,5},{5,4},{6,7},{7,6},{8,9},{9,8},{10,11... | collective-permute-start | bytes 1179656 | tf_op jit(solution)/shard_map/ppermute | solution.py:715
  14.3 10.8 %collective-permute-start.5 = (f32[408,256]{1,0:T(8,128)S(1)}, f32[408,256]{1,0:T(8,128)S(1)}, u32[]{:S(2)}, u32[]{:S(2)}) collective-permute-start(f32[408,256]{1,0:T(8,128)S(1)} %get-tuple-element.43.source), channel_id=1, source_target_pairs={{0,2},{2,3},{3,1},{1,0},{4,5},{5,4},{6,7},{7,6},{8,10},{10,11},{11... | collective-permute-start | bytes 1253384 | tf_op jit(solution)/shard_map/ppermute | solution.py:753
  14.9 14.7 %collective-permute-start.3 = (f32[6,64,512]{2,1,0:T(8,128)S(1)}, f32[6,64,512]{2,1,0:T(8,128)S(1)}, u32[]{:S(2)}, u32[]{:S(2)}) collective-permute-start(f32[6,64,512]{2,1,0:T(8,128)S(1)} %outer.1.value), channel_id=1, source_target_pairs={{2,3},{3,4},{4,5},{5,6},{6,7},{7,2},{0,1},{1,0},{10,11},{11,12},{1... | collective-permute-start | bytes 2359304 | tf_op jit(solution)/shard_map/ppermute | solution.py:715
  16.1 5.5 %collective-permute-start.6 = (f32[48,256]{1,0:T(8,128)S(1)}, f32[48,256]{1,0:T(8,128)S(1)}, u32[]{:S(2)}, u32[]{:S(2)}) collective-permute-start(f32[48,256]{1,0:T(8,128)S(1)} %get-tuple-element.44), channel_id=1, source_target_pairs={{1,10},{10,19},{19,0},{0,1},{4,13},{5,4},{6,15},{7,6},{9,18},{18,2... | collective-permute-start | bytes 147464 | tf_op jit(solution)/shard_map/ppermute | solution.py:753
  16.8 5.3 %collective-permute-start.7 = (f32[48,256]{1,0:T(8,128)S(1)}, f32[48,256]{1,0:T(8,128)S(1)}, u32[]{:S(2)}, u32[]{:S(2)}) collective-permute-start(f32[48,256]{1,0:T(8,128)S(1)} %get-tuple-element.45), channel_id=1, source_target_pairs={{1,26},{26,19},{19,0},{0,1},{4,29},{5,4},{6,31},{7,6},{9,2},{2,27}... | collective-permute-start | bytes 147464 | tf_op jit(solution)/shard_map/ppermute | solution.py:753
  22.1 2.9 %collective-permute-start.8 = (f32[2,48,256]{2,1,0:T(8,128)S(1)}, f32[2,48,256]{2,1,0:T(8,128)S(1)}, u32[]{:S(2)}, u32[]{:S(2)}) collective-permute-start(f32[2,48,256]{2,1,0:T(8,128)S(1)} %halo.1), channel_id=1, source_target_pairs={{0,1},{1,0},{2,3},{3,2},{4,5},{5,4},{6,7},{7,6},{8,9},{9,8},{10,11... | collective-permute-start | bytes 294920 | tf_op jit(solution)/shard_map/ppermute | solution.py:715
  25.9 8.2 %collective-permute-start.10 = (f32[6,72,256]{2,1,0:T(8,128)S(1)}, f32[6,72,256]{2,1,0:T(8,128)S(1)}, u32[]{:S(2)}, u32[]{:S(2)}) collective-permute-start(f32[6,72,256]{2,1,0:T(8,128)S(1)} %get-tuple-element.47), channel_id=1, source_target_pairs={{2,6},{6,7},{7,3},{3,2},{0,1},{1,0},{4,5},{5,4},{10,14},{14,15},{1... | collective-permute-start | bytes 1327112 | tf_op jit(solution)/shard_map/ppermute | solution.py:715
  26.3 11.9 %collective-permute-start.11 = (f32[408,256]{1,0:T(8,128)S(1)}, f32[408,256]{1,0:T(8,128)S(1)}, u32[]{:S(2)}, u32[]{:S(2)}) collective-permute-start(f32[408,256]{1,0:T(8,128)S(1)} %get-tuple-element.46.after), channel_id=1, source_target_pairs={{2,4},{4,6},{6,7},{7,5},{5,3},{3,2},{0,1},{1,0},{10,12},{12,14},{1... | collective-permute-start | bytes 1253384 | tf_op jit(solution)/shard_map/ppermute | solution.py:715
  26.4 12.4 %collective-permute-start.9 = (f32[6,64,512]{2,1,0:T(8,128)S(1)}, f32[6,64,512]{2,1,0:T(8,128)S(1)}, u32[]{:S(2)}, u32[]{:S(2)}) collective-permute-start(f32[6,64,512]{2,1,0:T(8,128)S(1)} %later.1), channel_id=1, source_target_pairs={{1,2},{9,10},{17,18},{25,26}} | collective-permute-start | bytes 2359304 | tf_op jit(solution)/shard_map/ppermute | solution.py:858
  38.8 1.8 %collective-permute-start.12 = (f32[6,64,256]{2,1,0:T(8,128)S(1)}, f32[6,64,256]{2,1,0:T(8,128)S(1)}, u32[]{:S(2)}, u32[]{:S(2)}) collective-permute-start(f32[6,64,256]{2,1,0:T(8,128)S(1)} %even.1), channel_id=1, source_target_pairs={{0,1},{1,0},{2,3},{3,2},{4,5},{5,4},{6,7},{7,6},{8,9},{9,8},{10,11... | collective-permute-start | bytes 1179656 | tf_op jit(solution)/shard_map/ppermute | solution.py:715

commit v7 on v6

--- a/solution.py
+++ b/solution.py
@@ -668,8 +668,8 @@
     odd = lax.axis_index("cuts") % 2
     cols = base.shape[2]
     copies = []
-    for lead in range(0, 6, 2):
-        part = range(lead, lead + 2)
+    for lead in range(6):
+        part = range(lead, lead + 1)
         values = []
         for i in part:
             value = jnp.where(odd == 1, received[i], own[i])
@@ -678,11 +678,11 @@
             jnp.concatenate(values, axis=0),
             [base.at[i] for i in part],
             [made.at[i] for i in part],
-            slots.at[pl.ds(cols // LANES * lead, cols // LANES * 2)],
+            slots.at[pl.ds(cols // LANES * lead, cols // LANES)],
         )
         copies.append(
             pltpu.make_async_copy(
-                made.at[pl.ds(lead, 2)], out.at[pl.ds(lead, 2)], sems.at[lead // 2]
+                made.at[pl.ds(lead, 1)], out.at[pl.ds(lead, 1)], sems.at[lead]
             )
         )
         copies[-1].start()
@@ -877,7 +877,7 @@
     rem_scratch = [
         halver_scratch(6, rows, cols),
         pltpu.VMEM(state, F32),
-        pltpu.SemaphoreType.DMA((3,)),
+        pltpu.SemaphoreType.DMA((6,)),
     ]
     (base,) = run(
         early_body,

time: 42.2 us -> 42.5 us (level)
  no operation moved by 1% of the time
where the time goes in v7:
time: 42.5 us; the launch traced here: 42.3 us
  waiting for transfers between devices  16.3 us (38%)
  Pallas kernels  15.4 us (36%)
  starting transfers between devices  9.92 us (23%)
  between operations  0.77 us (2%)
    pallas_call x16, Pallas kernels, run(): pl.pallas_call(body, name=name, out_shape=[jax.ShapeDtypeStruct(shape, F3...  15.4 us
    ppermute x7, waiting for transfers between devices, along_cuts(): return lax.ppermute(value, 'cuts', pairs)  10.9 us
    ppermute x7, starting transfers between devices, along_cuts(): return lax.ppermute(value, 'cuts', pairs)  6.09 us
    ppermute x3, waiting for transfers between devices, to_chip_1(): return lax.ppermute(value, ('strip', 'cuts'), pairs)  4.89 us
    ppermute x3, starting transfers between devices, to_chip_1(): return lax.ppermute(value, ('strip', 'cuts'), pairs)  1.65 us
    ppermute x2, starting transfers between devices, around_loop(): return lax.ppermute(value, 'strip', pairs)  1.47 us
  transfers between devices with their start and end apart: 13, of which 8 were waited for; matrix products, arithmetic and copies ran while one was open for 0% of the time, Pallas kernels for 27%

profile of v7, /device:TPU:11, one launch (start us, length us, event | category | flops | bytes accessed | tf_op | source)
XLA Modules:
  0.0 42.3 jit_solution(16963380408271573880)
XLA Ops:
  0.6 2.3 %pack.1 = (f32[40,512]{1,0:T(8,128)S(1)}, f32[40,512]{1,0:T(8,128)S(1)}, f32[10,16,512]{2,1,0:T(8,128)S(1)}, f32[10,8,256]{2,1,0:T(8,128)S(1)}, f32[6,128,512]{2...) custom-call(f32[6,128,512]{2,1,0:T(8,128)} %bitcast.4, ...), custom_call_target="tpu_custom_call" | custom-call | tf_op jit(solution)/shard_map/pack/pallas_call | solution.py:35
  2.9 1.9 %collective-permute-start = (f32[6,80,512]{2,1,0:T(8,128)S(1)}, f32[6,80,512]{2,1,0:T(8,128)S(1)}, u32[]{:S(2)}, u32[]{:S(2)}) collective-permute-start(f32[6,80,512]{2,1,0:T(8,128)S(1)} %get-tuple-element.26), channel_id=1, source_target_pairs={{0,1},{1,2},{2,3},{3,4},{4,5},{5,6},{6,7},{7,0},{8,9},{9,10},{10,1... | collective-permute-start | bytes 2949128 | tf_op jit(solution)/shard_map/ppermute | solution.py:715
  4.9 1.2 %collective-permute-start.1 = (f32[40,512]{1,0:T(8,128)S(1)}, f32[40,512]{1,0:T(8,128)S(1)}, u32[]{:S(2)}, u32[]{:S(2)}) collective-permute-start(f32[40,512]{1,0:T(8,128)S(1)} %get-tuple-element.38), channel_id=1, source_target_pairs={{0,8},{8,16},{16,24},{24,0},{1,9},{9,17},{17,25},{25,1},{2,10},{10... | collective-permute-start | bytes 245768 | tf_op jit(solution)/shard_map/ppermute | solution.py:708
  6.1 0.3 collective-permute-start.2
  6.3 4.2 %interior.1 = (f32[6,128,512]{2,1,0:T(8,128)S(1)}, f32[6,64,256]{2,1,0:T(8,128)S(1)}, f32[7,80,256]{2,1,0:T(8,128)S(1)}, f32[7,128,512]{2,1,0:T(8,128)S(1)}) custom-call(f32[6,128,512]{2,1,0:T(8,128)S(1)} %get-tuple-element.27.u, f32[6,128,512]{2,1,0:T(8,128)} %init.5, f32[128,512]{1,0:T(8,128)S(1)} %get-tuple-element.28.kc, ...), custom_call_target="tpu_custom_call" | custom-call | tf_op jit(solution)/shard_map/interior/pallas_call | solution.py:35
  10.6 0.0 collective-permute-done.1.from_below
  10.6 0.5 %collective-permute-done.2.from_above = f32[40,512]{1,0:T(8,128)S(1)} collective-permute-done((f32[40,512]{1,0:T(8,128)S(1)}, f32[40,512]{1,0:T(8,128)S(1)}, u32[]{:S(2)}, u32[]{:S(2)}) %collective-permute-start.2) | collective-permute-done | bytes 81952 | tf_op jit(solution)/shard_map/ppermute | solution.py:708
  11.1 0.8 %edges.1 = (f32[6,16,512]{2,1,0:T(8,128)S(1)}, f32[6,64,256]{2,1,0:T(8,128)S(1)}, f32[7,80,256]{2,1,0:T(8,128)S(1)}) custom-call(f32[6,128,512]{2,1,0:T(8,128)S(1)} %get-tuple-element.33.f, f32[10,16,512]{2,1,0:T(8,128)S(1)} %get-tuple-element.34.own, f32[10,8,256]{2,1,0:T(8,128)S(1)} %get-tuple-element.35.own_coarse, ...), custom_call_target="tpu_custom_call" | custom-call | tf_op jit(solution)/shard_map/edges/pallas_call | solution.py:35
  11.9 0.4 collective-permute-start.4
  12.3 1.4 %collective-permute-done.4.b_other = f32[6,64,256]{2,1,0:T(8,128)S(1)} collective-permute-done((f32[6,64,256]{2,1,0:T(8,128)S(1)}, f32[6,64,256]{2,1,0:T(8,128)S(1)}, u32[]{:S(2)}, u32[]{:S(2)}) %collective-permute-start.4) | collective-permute-done | bytes 393248 | tf_op jit(solution)/shard_map/ppermute | solution.py:715
  13.7 0.5 %pair.1 = (f32[408,256]{1,0:T(8,128)S(1)}, f32[48,256]{1,0:T(8,128)S(1)}, f32[48,256]{1,0:T(8,128)S(1)}) custom-call(f32[6,64,256]{2,1,0:T(8,128)S(1)} %get-tuple-element.41.b.b_even, f32[6,64,256]{2,1,0:T(8,128)S(1)} %collective-permute-done.4.b_other, f32[7,80,256]{2,1,0:T(8,128)S(1)} %get-tuple-element.42.cc), custom_call_target="tpu_custom_call" | custom-call | tf_op jit(solution)/shard_map/pair/pallas_call | solution.py:35
  14.3 0.6 %collective-permute-start.5 = (f32[408,256]{1,0:T(8,128)S(1)}, f32[408,256]{1,0:T(8,128)S(1)}, u32[]{:S(2)}, u32[]{:S(2)}) collective-permute-start(f32[408,256]{1,0:T(8,128)S(1)} %get-tuple-element.43.source), channel_id=1, source_target_pairs={{0,2},{2,3},{3,1},{1,0},{4,5},{5,4},{6,7},{7,6},{8,10},{10,11},{11... | collective-permute-start | bytes 1253384 | tf_op jit(solution)/shard_map/ppermute | solution.py:753
  14.8 0.1 outer.1.value
  14.9 1.2 %collective-permute-start.3 = (f32[6,64,512]{2,1,0:T(8,128)S(1)}, f32[6,64,512]{2,1,0:T(8,128)S(1)}, u32[]{:S(2)}, u32[]{:S(2)}) collective-permute-start(f32[6,64,512]{2,1,0:T(8,128)S(1)} %outer.1.value), channel_id=1, source_target_pairs={{2,3},{3,4},{4,5},{5,6},{6,7},{7,2},{0,1},{1,0},{10,11},{11,12},{1... | collective-permute-start | bytes 2359304 | tf_op jit(solution)/shard_map/ppermute | solution.py:715
  16.1 0.7 %collective-permute-start.6 = (f32[48,256]{1,0:T(8,128)S(1)}, f32[48,256]{1,0:T(8,128)S(1)}, u32[]{:S(2)}, u32[]{:S(2)}) collective-permute-start(f32[48,256]{1,0:T(8,128)S(1)} %get-tuple-element.44), channel_id=1, source_target_pairs={{1,10},{10,19},{19,0},{0,1},{4,13},{5,4},{6,15},{7,6},{9,18},{18,2... | collective-permute-start | bytes 147464 | tf_op jit(solution)/shard_map/ppermute | solution.py:753
  16.8 0.4 %collective-permute-start.7 = (f32[48,256]{1,0:T(8,128)S(1)}, f32[48,256]{1,0:T(8,128)S(1)}, u32[]{:S(2)}, u32[]{:S(2)}) collective-permute-start(f32[48,256]{1,0:T(8,128)S(1)} %get-tuple-element.45), channel_id=1, source_target_pairs={{1,26},{26,19},{19,0},{0,1},{4,29},{5,4},{6,31},{7,6},{9,2},{2,27}... | collective-permute-start | bytes 147464 | tf_op jit(solution)/shard_map/ppermute | solution.py:753
  17.2 4.4 %collective-permute-done.6.below = f32[48,256]{1,0:T(8,128)S(1)} collective-permute-done((f32[48,256]{1,0:T(8,128)S(1)}, f32[48,256]{1,0:T(8,128)S(1)}, u32[]{:S(2)}, u32[]{:S(2)}) %collective-permute-start.6) | collective-permute-done | bytes 49184 | tf_op jit(solution)/shard_map/ppermute | solution.py:753
  21.6 0.5 %collective-permute-done.7.above = f32[48,256]{1,0:T(8,128)S(1)} collective-permute-done((f32[48,256]{1,0:T(8,128)S(1)}, f32[48,256]{1,0:T(8,128)S(1)}, u32[]{:S(2)}, u32[]{:S(2)}) %collective-permute-start.7) | collective-permute-done | bytes 49184 | tf_op jit(solution)/shard_map/ppermute | solution.py:753
  22.1 2.0 %collective-permute-start.8 = (f32[2,48,256]{2,1,0:T(8,128)S(1)}, f32[2,48,256]{2,1,0:T(8,128)S(1)}, u32[]{:S(2)}, u32[]{:S(2)}) collective-permute-start(f32[2,48,256]{2,1,0:T(8,128)S(1)} %halo.1), channel_id=1, source_target_pairs={{0,1},{1,0},{2,3},{3,2},{4,5},{5,4},{6,7},{7,6},{8,9},{9,8},{10,11... | collective-permute-start | bytes 294920 | tf_op jit(solution)/shard_map/ppermute | solution.py:715
  24.1 0.9 %collective-permute-done.8.halo_source = f32[2,48,256]{2,1,0:T(8,128)S(1)} collective-permute-done((f32[2,48,256]{2,1,0:T(8,128)S(1)}, f32[2,48,256]{2,1,0:T(8,128)S(1)}, u32[]{:S(2)}, u32[]{:S(2)}) %collective-permute-start.8) | collective-permute-done | bytes 98336 | tf_op jit(solution)/shard_map/ppermute | solution.py:715
  25.0 0.0 collective-permute-done.5.message
  25.1 0.0 collective-permute-done.u.refs_0_
  25.1 0.8 %leap.1 = (f32[6,72,256]{2,1,0:T(8,128)S(1)}, f32[408,256]{1,0:T(8,128)S(1)}) custom-call(f32[408,256]{1,0:T(8,128)S(1)} %collective-permute-done.5.message, f32[2,48,256]{2,1,0:T(8,128)S(1)} %halo.1, f32[408,256]{1,0:T(8,128)S(1)} %get-tuple-element.43.source, f32[2,48,256]{2,1,0:T(8,128)S(1)} %collective-permute-done.8.halo_source, ...), custom_call_target="tpu_custom_call" | custom-call | tf_op jit(solution)/shard_map/leap/pallas_call | solution.py:35
  25.9 0.4 collective-permute-start.10
  26.3 0.1 collective-permute-start.11
  26.3 0.1 later.1
  26.4 0.7 %collective-permute-start.9 = (f32[6,64,512]{2,1,0:T(8,128)S(1)}, f32[6,64,512]{2,1,0:T(8,128)S(1)}, u32[]{:S(2)}, u32[]{:S(2)}) collective-permute-start(f32[6,64,512]{2,1,0:T(8,128)S(1)} %later.1), channel_id=1, source_target_pairs={{1,2},{9,10},{17,18},{25,26}} | collective-permute-start | bytes 2359304 | tf_op jit(solution)/shard_map/ppermute | solution.py:858
  27.1 1.2 %join.1.refs_1_ = f32[6,128,512]{2,1,0:T(8,128)} custom-call(f32[6,128,512]{2,1,0:T(8,128)S(1)} %get-tuple-element.33.f, f32[6,16,512]{2,1,0:T(8,128)S(1)} %get-tuple-element.40.ends), custom_call_target="tpu_custom_call" | custom-call | bytes 3145728 | tf_op jit(solution)/shard_map/join/pallas_call | solution.py:35
  28.3 1.2 %again.1.inner = f32[6,64,512]{2,1,0:T(8,128)S(1)} custom-call(f32[6,80,512]{2,1,0:T(8,128)S(1)} %collective-permute-done.u.refs_0_, f32[7,128,512]{2,1,0:T(8,128)S(1)} %get-tuple-element.32.cf), custom_call_target="tpu_custom_call" | custom-call | bytes 3145728 | tf_op jit(solution)/shard_map/again/pallas_call | solution.py:35
  29.5 0.0 collective-permute-done.3.outer
  29.5 1.8 %remainder.1.base_in.refs_0_ = f32[6,128,512]{2,1,0:T(8,128)S(1)} custom-call(f32[6,64,512]{2,1,0:T(8,128)S(1)} %again.1.inner, f32[6,64,512]{2,1,0:T(8,128)S(1)} %collective-permute-done.3.outer, f32[6,128,512]{2,1,0:T(8,128)} %init.5), custom_call_target="tpu_custom_call" | custom-call | bytes 3145728 | tf_op jit(solution)/shard_map/remainder/pallas_call | solution.py:35
  31.3 2.7 %collective-permute-done.10.leaped = f32[6,72,256]{2,1,0:T(8,128)S(1)} collective-permute-done((f32[6,72,256]{2,1,0:T(8,128)S(1)}, f32[6,72,256]{2,1,0:T(8,128)S(1)}, u32[]{:S(2)}, u32[]{:S(2)}) %collective-permute-start.10) | collective-permute-done | bytes 442400 | tf_op jit(solution)/shard_map/ppermute | solution.py:715
  34.1 4.1 %collective-permute-done.11.step = f32[408,256]{1,0:T(8,128)S(1)} collective-permute-done((f32[408,256]{1,0:T(8,128)S(1)}, f32[408,256]{1,0:T(8,128)S(1)}, u32[]{:S(2)}, u32[]{:S(2)}) %collective-permute-start.11) | collective-permute-done | bytes 417824 | tf_op jit(solution)/shard_map/ppermute | solution.py:715
  38.2 0.1 collect.1
  38.3 0.4 even.1
  38.8 0.1 collective-permute-start.12
  38.8 0.0 collective-permute-done.9.after_hop
  38.9 1.7 %collective-permute-done.12.received = f32[6,64,256]{2,1,0:T(8,128)S(1)} collective-permute-done((f32[6,64,256]{2,1,0:T(8,128)S(1)}, f32[6,64,256]{2,1,0:T(8,128)S(1)}, u32[]{:S(2)}, u32[]{:S(2)}) %collective-permute-start.12) | collective-permute-done | bytes 393248 | tf_op jit(solution)/shard_map/ppermute | solution.py:715
  40.5 1.8 %correct.1 = f32[6,128,512]{2,1,0:T(8,128)} custom-call(f32[6,128,512]{2,1,0:T(8,128)S(1)} %late.1.base, f32[6,64,256]{2,1,0:T(8,128)S(1)} %get-tuple-element.48.own, f32[6,64,256]{2,1,0:T(8,128)S(1)} %collective-permute-done.12.received), custom_call_target="tpu_custom_call" | custom-call | tf_op jit(solution)/shard_map/correct/pallas_call | solution.py:35
  (3 shorter events, 0.0 us)
Async XLA Ops:
  2.9 22.1 %collective-permute-start = (f32[6,80,512]{2,1,0:T(8,128)S(1)}, f32[6,80,512]{2,1,0:T(8,128)S(1)}, u32[]{:S(2)}, u32[]{:S(2)}) collective-permute-start(f32[6,80,512]{2,1,0:T(8,128)S(1)} %get-tuple-element.26), channel_id=1, source_target_pairs={{0,1},{1,2},{2,3},{3,4},{4,5},{5,6},{6,7},{7,0},{8,9},{9,10},{10,1... | collective-permute-start | bytes 2949128 | tf_op jit(solution)/shard_map/ppermute | solution.py:715
  4.9 5.7 %collective-permute-start.1 = (f32[40,512]{1,0:T(8,128)S(1)}, f32[40,512]{1,0:T(8,128)S(1)}, u32[]{:S(2)}, u32[]{:S(2)}) collective-permute-start(f32[40,512]{1,0:T(8,128)S(1)} %get-tuple-element.38), channel_id=1, source_target_pairs={{0,8},{8,16},{16,24},{24,0},{1,9},{9,17},{17,25},{25,1},{2,10},{10... | collective-permute-start | bytes 245768 | tf_op jit(solution)/shard_map/ppermute | solution.py:708
  6.1 5.0 %collective-permute-start.2 = (f32[40,512]{1,0:T(8,128)S(1)}, f32[40,512]{1,0:T(8,128)S(1)}, u32[]{:S(2)}, u32[]{:S(2)}) collective-permute-start(f32[40,512]{1,0:T(8,128)S(1)} %get-tuple-element.39), channel_id=1, source_target_pairs={{0,24},{8,0},{16,8},{24,16},{1,25},{9,1},{17,9},{25,17},{2,26},{10... | collective-permute-start | bytes 245768 | tf_op jit(solution)/shard_map/ppermute | solution.py:708
  11.9 1.8 %collective-permute-start.4 = (f32[6,64,256]{2,1,0:T(8,128)S(1)}, f32[6,64,256]{2,1,0:T(8,128)S(1)}, u32[]{:S(2)}, u32[]{:S(2)}) collective-permute-start(f32[6,64,256]{2,1,0:T(8,128)S(1)} %get-tuple-element.41.b.b_even), channel_id=1, source_target_pairs={{0,1},{1,0},{2,3},{3,2},{4,5},{5,4},{6,7},{7,6},{8,9},{9,8},{10,11... | collective-permute-start | bytes 1179656 | tf_op jit(solution)/shard_map/ppermute | solution.py:715
  14.3 10.8 %collective-permute-start.5 = (f32[408,256]{1,0:T(8,128)S(1)}, f32[408,256]{1,0:T(8,128)S(1)}, u32[]{:S(2)}, u32[]{:S(2)}) collective-permute-start(f32[408,256]{1,0:T(8,128)S(1)} %get-tuple-element.43.source), channel_id=1, source_target_pairs={{0,2},{2,3},{3,1},{1,0},{4,5},{5,4},{6,7},{7,6},{8,10},{10,11},{11... | collective-permute-start | bytes 1253384 | tf_op jit(solution)/shard_map/ppermute | solution.py:753
  14.9 14.7 %collective-permute-start.3 = (f32[6,64,512]{2,1,0:T(8,128)S(1)}, f32[6,64,512]{2,1,0:T(8,128)S(1)}, u32[]{:S(2)}, u32[]{:S(2)}) collective-permute-start(f32[6,64,512]{2,1,0:T(8,128)S(1)} %outer.1.value), channel_id=1, source_target_pairs={{2,3},{3,4},{4,5},{5,6},{6,7},{7,2},{0,1},{1,0},{10,11},{11,12},{1... | collective-permute-start | bytes 2359304 | tf_op jit(solution)/shard_map/ppermute | solution.py:715
  16.1 5.5 %collective-permute-start.6 = (f32[48,256]{1,0:T(8,128)S(1)}, f32[48,256]{1,0:T(8,128)S(1)}, u32[]{:S(2)}, u32[]{:S(2)}) collective-permute-start(f32[48,256]{1,0:T(8,128)S(1)} %get-tuple-element.44), channel_id=1, source_target_pairs={{1,10},{10,19},{19,0},{0,1},{4,13},{5,4},{6,15},{7,6},{9,18},{18,2... | collective-permute-start | bytes 147464 | tf_op jit(solution)/shard_map/ppermute | solution.py:753
  16.8 5.3 %collective-permute-start.7 = (f32[48,256]{1,0:T(8,128)S(1)}, f32[48,256]{1,0:T(8,128)S(1)}, u32[]{:S(2)}, u32[]{:S(2)}) collective-permute-start(f32[48,256]{1,0:T(8,128)S(1)} %get-tuple-element.45), channel_id=1, source_target_pairs={{1,26},{26,19},{19,0},{0,1},{4,29},{5,4},{6,31},{7,6},{9,2},{2,27}... | collective-permute-start | bytes 147464 | tf_op jit(solution)/shard_map/ppermute | solution.py:753
  22.1 2.9 %collective-permute-start.8 = (f32[2,48,256]{2,1,0:T(8,128)S(1)}, f32[2,48,256]{2,1,0:T(8,128)S(1)}, u32[]{:S(2)}, u32[]{:S(2)}) collective-permute-start(f32[2,48,256]{2,1,0:T(8,128)S(1)} %halo.1), channel_id=1, source_target_pairs={{0,1},{1,0},{2,3},{3,2},{4,5},{5,4},{6,7},{7,6},{8,9},{9,8},{10,11... | collective-permute-start | bytes 294920 | tf_op jit(solution)/shard_map/ppermute | solution.py:715
  25.9 8.2 %collective-permute-start.10 = (f32[6,72,256]{2,1,0:T(8,128)S(1)}, f32[6,72,256]{2,1,0:T(8,128)S(1)}, u32[]{:S(2)}, u32[]{:S(2)}) collective-permute-start(f32[6,72,256]{2,1,0:T(8,128)S(1)} %get-tuple-element.47), channel_id=1, source_target_pairs={{2,6},{6,7},{7,3},{3,2},{0,1},{1,0},{4,5},{5,4},{10,14},{14,15},{1... | collective-permute-start | bytes 1327112 | tf_op jit(solution)/shard_map/ppermute | solution.py:715
  26.3 11.9 %collective-permute-start.11 = (f32[408,256]{1,0:T(8,128)S(1)}, f32[408,256]{1,0:T(8,128)S(1)}, u32[]{:S(2)}, u32[]{:S(2)}) collective-permute-start(f32[408,256]{1,0:T(8,128)S(1)} %get-tuple-element.46.after), channel_id=1, source_target_pairs={{2,4},{4,6},{6,7},{7,5},{5,3},{3,2},{0,1},{1,0},{10,12},{12,14},{1... | collective-permute-start | bytes 1253384 | tf_op jit(solution)/shard_map/ppermute | solution.py:715
  26.4 12.4 %collective-permute-start.9 = (f32[6,64,512]{2,1,0:T(8,128)S(1)}, f32[6,64,512]{2,1,0:T(8,128)S(1)}, u32[]{:S(2)}, u32[]{:S(2)}) collective-permute-start(f32[6,64,512]{2,1,0:T(8,128)S(1)} %later.1), channel_id=1, source_target_pairs={{1,2},{9,10},{17,18},{25,26}} | collective-permute-start | bytes 2359304 | tf_op jit(solution)/shard_map/ppermute | solution.py:858
  38.8 1.8 %collective-permute-start.12 = (f32[6,64,256]{2,1,0:T(8,128)S(1)}, f32[6,64,256]{2,1,0:T(8,128)S(1)}, u32[]{:S(2)}, u32[]{:S(2)}) collective-permute-start(f32[6,64,256]{2,1,0:T(8,128)S(1)} %even.1), channel_id=1, source_target_pairs={{0,1},{1,0},{2,3},{3,2},{4,5},{5,4},{6,7},{7,6},{8,9},{9,8},{10,11... | collective-permute-start | bytes 1179656 | tf_op jit(solution)/shard_map/ppermute | solution.py:715
